TPU v7x, 256 devices: a whole 4x4x8 slice. The times are simulated.
256 devices in a mesh: gx: 16 (over z, core), gy: 16 (over y, x).
Axes of the slice: x: 4, y: 4, z: 8, core: 2. Of those that a mesh axis runs over, the one named last changes fastest.
Arguments:
- right_side: float32 [128, 128, 8, 512], P('gx', 'gy'), may hold values from -9 to 9
- kappa_sq: float32 [128, 128, 512], P('gx', 'gy'), may hold values from 0.01 to 2
- coarse_inverse: float32 [4096, 256], P('gx'), may hold values from -0.25 to 32, as said below
Outputs:
- iterate: float32 [128, 128, 8, 512], P('gx', 'gy')
- residual: float32 [128, 128, 8, 512], P('gx', 'gy')
Inputs may be any that keep to these rules, and one draw needn't show every extreme that they name: `coarse_inverse`: each slab's block of 256 rows is a symmetric 256 x 256 matrix; its off-diagonal entries lie within -0.25 to 0.25 and its diagonal entries within 8 to 32.
All inputs are finite; a program needn't handle non-finite values.
Results may differ from a plain program's by a relative error of at most 0.0003.
Values sent between devices are 32-bit elements; how exact they have to be, the bound alone decides.
No kernel may reach another device: no remote copies, remote signals or barrier semaphores. Data moves between devices by JAX's collectives and lax.ppermute only.
A program may use at most 64 MiB of HBM per device.

v0:
```python
import jax
import jax.numpy as jnp
from jax import lax
from jax.sharding import PartitionSpec as P

NCD = 16
ITERS = 2


relax_weight = 2.0 / 3.0


def with_halo(block, sides, width):
    for axis, dim in sides:
        count = lax.axis_size(axis)
        forward = [(i, i + 1) for i in range(count - 1)]
        backward = [(target, source) for source, target in forward]
        low = lax.ppermute(
            lax.slice_in_dim(block, block.shape[dim] - width, None, axis=dim), axis, forward
        )
        high = lax.ppermute(lax.slice_in_dim(block, 0, width, axis=dim), axis, backward)
        block = jnp.concatenate([low, block, high], axis=dim)
    return block


def stencil(padded, field, diag_shift):
    padded = jnp.pad(padded, ((0, 0), (0, 0), (0, 0), (1, 1)))
    beside = padded[2:, 1:-1, :, 1:-1] + padded[:-2, 1:-1, :, 1:-1]
    beside = beside + padded[1:-1, 2:, :, 1:-1] + padded[1:-1, :-2, :, 1:-1]
    beside = beside + padded[1:-1, 1:-1, :, 2:] + padded[1:-1, 1:-1, :, :-2]
    return diag_shift * field - beside


def apply_operator(field, diag_shift):
    padded = with_halo(field, (("gx", 0), ("gy", 1)), 1)
    return stencil(padded, field, diag_shift)


def jacobi_sweep(correction, source, diag_shift):
    return (
        correction + relax_weight * (source - apply_operator(correction, diag_shift)) / diag_shift
    )


def coarse_solve(defect, coarse_inverse):
    width_x, width_y, probes, depth = defect.shape
    zblock = depth // NCD
    blocks = defect.reshape(width_x, width_y, probes, NCD, zblock)
    local_means = jnp.mean(blocks, axis=(0, 1, 4))
    row_start = lax.axis_index("gy") * NCD
    own_rows = lax.dynamic_slice_in_dim(coarse_inverse, row_start, NCD, 0)
    return lax.dot_general(
        lax.all_gather(local_means, "gy", axis=1, tiled=True),
        own_rows,
        (((1,), (1,)), ((), ())),
        precision=lax.Precision.HIGHEST,
        preferred_element_type=jnp.float32,
    )


def prolong(coarse_values, shape):
    width_x, width_y, probes, depth = shape
    zblock = depth // NCD
    spread = jnp.broadcast_to(
        coarse_values[None, None, :, :, None], (width_x, width_y, probes, NCD, zblock)
    )
    return spread.reshape(shape)


def precondition(source, diag_shift, coarse_inverse):
    correction = relax_weight * source / diag_shift
    correction = jacobi_sweep(correction, source, diag_shift)
    defect = source - apply_operator(correction, diag_shift)
    coarse_values = coarse_solve(defect, coarse_inverse)
    coarse_field = prolong(coarse_values, source.shape)
    correction = correction + coarse_field
    correction = jacobi_sweep(correction, source, diag_shift)
    return jacobi_sweep(correction, source, diag_shift)


def probe_dot(first, second):
    return jnp.sum(first * second, axis=(0, 1, 3))


def per_probe(values):
    return values[None, None, :, None]


def energy_sum(residual, precond):
    return lax.psum(probe_dot(residual, precond), ("gx", "gy"))


def body(right_side, kappa_sq, coarse_inverse):
    diag_shift = (6.0 + kappa_sq)[:, :, None, :]
    iterate = jnp.zeros_like(right_side)
    residual = right_side
    precond = precondition(residual, diag_shift, coarse_inverse)
    search = precond
    energy = energy_sum(residual, precond)
    for iteration in range(ITERS):
        op_image = apply_operator(search, diag_shift)
        curvature = lax.psum(probe_dot(search, op_image), ("gx", "gy"))
        step_size = energy / curvature
        iterate = iterate + per_probe(step_size) * search
        residual = residual - per_probe(step_size) * op_image
        if iteration + 1 < ITERS:
            precond = precondition(residual, diag_shift, coarse_inverse)
            energy_next = energy_sum(residual, precond)
            search = precond + per_probe(energy_next / energy) * search
            energy = energy_next
    return (iterate, residual)


def solution(mesh):
    placed = (P("gx", "gy", None, None), P("gx", "gy", None), P("gx", None))
    return jax.shard_map(
        body,
        mesh=mesh,
        in_specs=placed,
        out_specs=(P("gx", "gy", None, None), P("gx", "gy", None, None)),
        check_vma=False,
    )
```

profile of v0, /device:TPU:1, one launch (start us, length us, event | category | flops | bytes accessed | tf_op | source)
XLA Modules:
  0.0 519.5 jit_solution(6656495104835346042)
XLA Ops:
  3.1 4.9 collective-permute-start.1
  8.0 1.9 collective-permute-start
  10.0 4.3 collective-permute-done
  14.3 3.3 collective-permute-start.3
  19.8 3.8 collective-permute-done.2
  25.0 4.1 collective-permute-start.5
  29.1 1.9 collective-permute-start.4
  31.0 4.3 collective-permute-done.4
  35.4 3.1 collective-permute-start.7
  40.8 3.8 collective-permute-done.6
  46.0 21.1 %all-gather = f32[16,16,8]{1,2,0:T(8,128)S(1)} all-gather(f32[1,16,8]{1,2,0:T(8,128)S(1)} %multiply_bitcast_fusion.1), channel_id=1, replica_groups=mesh['gx'=16,'gy'=16] {'gy'}, dimensions={0}, use_global_device_ids=true | all-gather | bytes 8704 | tf_op jit(solution)/shard_map/all_gather | solution.py:53
  67.7 9.0 %collective-permute-start.9 = (f32[1,8,8,512]{3,2,1,0:T(8,128)S(1)}, f32[1,8,8,512]{3,2,1,0:T(8,128)S(1)}, u32[]{:S(2)}, u32[]{:S(2)}) collective-permute-start(f32[1,8,8,512]{3,2,1,0:T(8,128)S(1)} %get-tuple-element.47), channel_id=1, source_target_pairs={{0,16},{16,32},{32,48},{48,64},{64,80},{80,96},{96,112},{112,128},... | collective-permute-start | bytes 393224 | tf_op jit(solution)/shard_map/ppermute | solution.py:18
  78.6 4.3 collective-permute-done.8
  87.0 3.8 collective-permute-done.10
  92.2 4.7 collective-permute-start.13
  96.8 1.9 collective-permute-start.12
  98.8 4.3 collective-permute-done.12
  103.1 2.8 collective-permute-start.15
  108.2 3.8 collective-permute-done.14
  113.4 4.0 collective-permute-start.17
  119.3 4.3 collective-permute-done.16
  123.7 4.9 collective-permute-start.19
  130.8 3.8 collective-permute-done.18
  137.0 84.1 %all-reduce.10 = (f32[8]{0:T(128)S(1)}, f32[8]{0:T(128)S(1)}) all-reduce(f32[8]{0:T(128)S(1)} %get-tuple-element.3, f32[8]{0:T(128)S(1)} %get-tuple-element.2), channel_id=1, replica_groups=mesh['gx'=16,'gy'=16] {'gx','gy'}, use_global_device_ids=true, to_apply=%region_3.4 | all-reduce | flops 16 | bytes 128 | tf_op jit(solution)/shard_map/psum | solution.py:90
  225.2 2.4 collective-permute-start.20
  227.6 3.9 collective-permute-done.20
  231.5 2.4 collective-permute-start.23
  236.2 3.8 collective-permute-done.22
  241.3 4.9 collective-permute-start.25
  246.2 1.9 collective-permute-start.24
  248.2 4.3 collective-permute-done.24
  252.5 2.2 collective-permute-start.27
  257.0 4.3 collective-permute-done.26
  264.1 21.4 %all-gather.1 = f32[16,16,8]{1,2,0:T(8,128)S(1)} all-gather(f32[1,16,8]{1,2,0:T(8,128)S(1)} %multiply_bitcast_fusion), channel_id=1, replica_groups=mesh['gx'=16,'gy'=16] {'gy'}, dimensions={0}, use_global_device_ids=true | all-gather | bytes 8704 | tf_op jit(solution)/shard_map/all_gather | solution.py:53
  289.0 9.9 %collective-permute-start.29 = (f32[1,8,8,512]{3,2,1,0:T(8,128)S(1)}, f32[1,8,8,512]{3,2,1,0:T(8,128)S(1)}, u32[]{:S(2)}, u32[]{:S(2)}) collective-permute-start(f32[1,8,8,512]{3,2,1,0:T(8,128)S(1)} %get-tuple-element.37), channel_id=1, source_target_pairs={{0,16},{16,32},{32,48},{48,64},{64,80},{80,96},{96,112},{112,128},... | collective-permute-start | bytes 393224 | tf_op jit(solution)/shard_map/ppermute | solution.py:18
  300.9 4.3 collective-permute-done.28
  308.8 3.8 collective-permute-done.30
  314.0 4.5 collective-permute-start.33
  320.4 4.3 collective-permute-done.32
  324.8 3.8 collective-permute-start.35
  330.8 3.8 collective-permute-done.34
  337.0 79.8 %psum.30 = f32[8]{0:T(128)S(1)} all-reduce(f32[8]{0:T(128)S(1)} %get-tuple-element.8), channel_id=1, replica_groups=mesh['gx'=16,'gy'=16] {'gx','gy'}, use_global_device_ids=true, to_apply=%region_9.10 | all-reduce | flops 8 | bytes 64 | tf_op jit(solution)/shard_map/psum | solution.py:90
  418.3 2.0 collective-permute-start.37
  420.3 2.3 collective-permute-start.36
  422.7 3.9 collective-permute-done.36
  430.5 3.8 collective-permute-done.38
  436.6 79.8 %psum.31 = f32[8]{0:T(128)S(1)} all-reduce(f32[8]{0:T(128)S(1)} %get-tuple-element.6), channel_id=1, replica_groups=mesh['gx'=16,'gy'=16] {'gx','gy'}, use_global_device_ids=true, to_apply=%region_11.12 | all-reduce | flops 8 | bytes 64 | tf_op jit(solution)/shard_map/psum | solution.py:102
  516.4 3.1 multiply_subtract_fusion
  (115 shorter events, 64.7 us)
Async XLA Ops:
  0.6 66.5 %copy-start = (f32[256,256]{1,0:T(8,128)S(1)}, f32[256,256]{1,0:T(8,128)}, u32[]{:S(2)}) copy-start(f32[256,256]{1,0:T(8,128)} %param.5) | copy-start | bytes 786436
  3.1 6.9 %collective-permute-start.1 = (f32[1,8,8,512]{3,2,1,0:T(8,128)S(1)}, f32[1,8,8,512]{3,2,1,0:T(8,128)S(1)}, u32[]{:S(2)}, u32[]{:S(2)}) collective-permute-start(f32[1,8,8,512]{3,2,1,0:T(8,128)S(1)} %get-tuple-element.51), channel_id=1, source_target_pairs={{0,16},{16,32},{32,48},{48,64},{64,80},{80,96},{96,112},{112,128},... | collective-permute-start | bytes 393224 | tf_op jit(solution)/shard_map/ppermute | solution.py:18
  8.0 6.3 %collective-permute-start = (f32[1,8,8,512]{3,2,1,0:T(8,128)S(1)}, f32[1,8,8,512]{3,2,1,0:T(8,128)S(1)}, u32[]{:S(2)}, u32[]{:S(2)}) collective-permute-start(f32[1,8,8,512]{3,2,1,0:T(8,128)S(1)} %get-tuple-element.52), channel_id=1, source_target_pairs={{16,0},{32,16},{48,32},{64,48},{80,64},{96,80},{112,96},{128,112},... | collective-permute-start | bytes 393224 | tf_op jit(solution)/shard_map/ppermute | solution.py:21
  14.3 9.9 %copy-start.1 = (f32[8,8,8,512]{3,2,1,0:T(8,128)S(1)}, f32[8,8,8,512]{3,2,1,0:T(8,128)}, u32[]{:S(2)}) copy-start(f32[8,8,8,512]{3,2,1,0:T(8,128)} %param.3) | copy-start | bytes 3145732
  14.3 5.5 %collective-permute-start.3 = (f32[10,1,8,512]{3,2,1,0:T(8,128)S(1)}, f32[10,1,8,512]{3,2,1,0:T(8,128)S(1)}, u32[]{:S(2)}, u32[]{:S(2)}) collective-permute-start(f32[10,1,8,512]{3,2,1,0:T(8,128)S(1)} %get-tuple-element.31), channel_id=1, source_target_pairs={{0,1},{1,2},{2,3},{3,4},{4,5},{5,6},{6,7},{7,8},{8,9},{9,10},{10,1... | collective-permute-start | bytes 491528 | tf_op jit(solution)/shard_map/ppermute | solution.py:18
  17.6 6.1 %collective-permute-start.2 = (f32[10,1,8,512]{3,2,1,0:T(8,128)S(1)}, f32[10,1,8,512]{3,2,1,0:T(8,128)S(1)}, u32[]{:S(2)}, u32[]{:S(2)}) collective-permute-start(f32[10,1,8,512]{3,2,1,0:T(8,128)S(1)} %get-tuple-element.32), channel_id=1, source_target_pairs={{1,0},{2,1},{3,2},{4,3},{5,4},{6,5},{7,6},{8,7},{9,8},{10,9},{11,1... | collective-permute-start | bytes 491528 | tf_op jit(solution)/shard_map/ppermute | solution.py:21
  25.0 6.0 %collective-permute-start.5 = (f32[1,8,8,512]{3,2,1,0:T(8,128)S(1)}, f32[1,8,8,512]{3,2,1,0:T(8,128)S(1)}, u32[]{:S(2)}, u32[]{:S(2)}) collective-permute-start(f32[1,8,8,512]{3,2,1,0:T(8,128)S(1)} %get-tuple-element.49), channel_id=1, source_target_pairs={{0,16},{16,32},{32,48},{48,64},{64,80},{80,96},{96,112},{112,128},... | collective-permute-start | bytes 393224 | tf_op jit(solution)/shard_map/ppermute | solution.py:18
  29.1 6.3 %collective-permute-start.4 = (f32[1,8,8,512]{3,2,1,0:T(8,128)S(1)}, f32[1,8,8,512]{3,2,1,0:T(8,128)S(1)}, u32[]{:S(2)}, u32[]{:S(2)}) collective-permute-start(f32[1,8,8,512]{3,2,1,0:T(8,128)S(1)} %get-tuple-element.50), channel_id=1, source_target_pairs={{16,0},{32,16},{48,32},{64,48},{80,64},{96,80},{112,96},{128,112},... | collective-permute-start | bytes 393224 | tf_op jit(solution)/shard_map/ppermute | solution.py:21
  35.4 5.4 %collective-permute-start.7 = (f32[10,1,8,512]{3,2,1,0:T(8,128)S(1)}, f32[10,1,8,512]{3,2,1,0:T(8,128)S(1)}, u32[]{:S(2)}, u32[]{:S(2)}) collective-permute-start(f32[10,1,8,512]{3,2,1,0:T(8,128)S(1)} %get-tuple-element.29), channel_id=1, source_target_pairs={{0,1},{1,2},{2,3},{3,4},{4,5},{5,6},{6,7},{7,8},{8,9},{9,10},{10,1... | collective-permute-start | bytes 491528 | tf_op jit(solution)/shard_map/ppermute | solution.py:18
  38.5 6.1 %collective-permute-start.6 = (f32[10,1,8,512]{3,2,1,0:T(8,128)S(1)}, f32[10,1,8,512]{3,2,1,0:T(8,128)S(1)}, u32[]{:S(2)}, u32[]{:S(2)}) collective-permute-start(f32[10,1,8,512]{3,2,1,0:T(8,128)S(1)} %get-tuple-element.30), channel_id=1, source_target_pairs={{1,0},{2,1},{3,2},{4,3},{5,4},{6,5},{7,6},{8,7},{9,8},{10,9},{11,1... | collective-permute-start | bytes 491528 | tf_op jit(solution)/shard_map/ppermute | solution.py:21
  67.7 10.9 %collective-permute-start.9 = (f32[1,8,8,512]{3,2,1,0:T(8,128)S(1)}, f32[1,8,8,512]{3,2,1,0:T(8,128)S(1)}, u32[]{:S(2)}, u32[]{:S(2)}) collective-permute-start(f32[1,8,8,512]{3,2,1,0:T(8,128)S(1)} %get-tuple-element.47), channel_id=1, source_target_pairs={{0,16},{16,32},{32,48},{48,64},{64,80},{80,96},{96,112},{112,128},... | collective-permute-start | bytes 393224 | tf_op jit(solution)/shard_map/ppermute | solution.py:18
  76.6 6.3 %collective-permute-start.8 = (f32[1,8,8,512]{3,2,1,0:T(8,128)S(1)}, f32[1,8,8,512]{3,2,1,0:T(8,128)S(1)}, u32[]{:S(2)}, u32[]{:S(2)}) collective-permute-start(f32[1,8,8,512]{3,2,1,0:T(8,128)S(1)} %get-tuple-element.48), channel_id=1, source_target_pairs={{16,0},{32,16},{48,32},{64,48},{80,64},{96,80},{112,96},{128,112},... | collective-permute-start | bytes 393224 | tf_op jit(solution)/shard_map/ppermute | solution.py:21
  82.9 4.1 collective-permute-start.11
  84.8 6.1 %collective-permute-start.10 = (f32[10,1,8,512]{3,2,1,0:T(8,128)S(1)}, f32[10,1,8,512]{3,2,1,0:T(8,128)S(1)}, u32[]{:S(2)}, u32[]{:S(2)}) collective-permute-start(f32[10,1,8,512]{3,2,1,0:T(8,128)S(1)} %get-tuple-element.28), channel_id=1, source_target_pairs={{1,0},{2,1},{3,2},{4,3},{5,4},{6,5},{7,6},{8,7},{9,8},{10,9},{11,1... | collective-permute-start | bytes 491528 | tf_op jit(solution)/shard_map/ppermute | solution.py:21
  92.2 6.6 %collective-permute-start.13 = (f32[1,8,8,512]{3,2,1,0:T(8,128)S(1)}, f32[1,8,8,512]{3,2,1,0:T(8,128)S(1)}, u32[]{:S(2)}, u32[]{:S(2)}) collective-permute-start(f32[1,8,8,512]{3,2,1,0:T(8,128)S(1)} %get-tuple-element.45), channel_id=1, source_target_pairs={{0,16},{16,32},{32,48},{48,64},{64,80},{80,96},{96,112},{112,128},... | collective-permute-start | bytes 393224 | tf_op jit(solution)/shard_map/ppermute | solution.py:18
  96.8 6.3 %collective-permute-start.12 = (f32[1,8,8,512]{3,2,1,0:T(8,128)S(1)}, f32[1,8,8,512]{3,2,1,0:T(8,128)S(1)}, u32[]{:S(2)}, u32[]{:S(2)}) collective-permute-start(f32[1,8,8,512]{3,2,1,0:T(8,128)S(1)} %get-tuple-element.46), channel_id=1, source_target_pairs={{16,0},{32,16},{48,32},{64,48},{80,64},{96,80},{112,96},{128,112},... | collective-permute-start | bytes 393224 | tf_op jit(solution)/shard_map/ppermute | solution.py:21
  103.1 5.1 collective-permute-start.15
  106.0 6.1 %collective-permute-start.14 = (f32[10,1,8,512]{3,2,1,0:T(8,128)S(1)}, f32[10,1,8,512]{3,2,1,0:T(8,128)S(1)}, u32[]{:S(2)}, u32[]{:S(2)}) collective-permute-start(f32[10,1,8,512]{3,2,1,0:T(8,128)S(1)} %get-tuple-element.26), channel_id=1, source_target_pairs={{1,0},{2,1},{3,2},{4,3},{5,4},{6,5},{7,6},{8,7},{9,8},{10,9},{11,1... | collective-permute-start | bytes 491528 | tf_op jit(solution)/shard_map/ppermute | solution.py:21
  113.4 5.9 %collective-permute-start.17 = (f32[1,8,8,512]{3,2,1,0:T(8,128)S(1)}, f32[1,8,8,512]{3,2,1,0:T(8,128)S(1)}, u32[]{:S(2)}, u32[]{:S(2)}) collective-permute-start(f32[1,8,8,512]{3,2,1,0:T(8,128)S(1)} %get-tuple-element.43), channel_id=1, source_target_pairs={{0,16},{16,32},{32,48},{48,64},{64,80},{80,96},{96,112},{112,128},... | collective-permute-start | bytes 393224 | tf_op jit(solution)/shard_map/ppermute | solution.py:18
  117.4 6.3 %collective-permute-start.16 = (f32[1,8,8,512]{3,2,1,0:T(8,128)S(1)}, f32[1,8,8,512]{3,2,1,0:T(8,128)S(1)}, u32[]{:S(2)}, u32[]{:S(2)}) collective-permute-start(f32[1,8,8,512]{3,2,1,0:T(8,128)S(1)} %get-tuple-element.44), channel_id=1, source_target_pairs={{16,0},{32,16},{48,32},{64,48},{80,64},{96,80},{112,96},{128,112},... | collective-permute-start | bytes 393224 | tf_op jit(solution)/shard_map/ppermute | solution.py:21
  123.7 7.1 %collective-permute-start.19 = (f32[10,1,8,512]{3,2,1,0:T(8,128)S(1)}, f32[10,1,8,512]{3,2,1,0:T(8,128)S(1)}, u32[]{:S(2)}, u32[]{:S(2)}) collective-permute-start(f32[10,1,8,512]{3,2,1,0:T(8,128)S(1)} %get-tuple-element.23), channel_id=1, source_target_pairs={{0,1},{1,2},{2,3},{3,4},{4,5},{5,6},{6,7},{7,8},{8,9},{9,10},{10,1... | collective-permute-start | bytes 491528 | tf_op jit(solution)/shard_map/ppermute | solution.py:18
  128.6 6.1 %collective-permute-start.18 = (f32[10,1,8,512]{3,2,1,0:T(8,128)S(1)}, f32[10,1,8,512]{3,2,1,0:T(8,128)S(1)}, u32[]{:S(2)}, u32[]{:S(2)}) collective-permute-start(f32[10,1,8,512]{3,2,1,0:T(8,128)S(1)} %get-tuple-element.24), channel_id=1, source_target_pairs={{1,0},{2,1},{3,2},{4,3},{5,4},{6,5},{7,6},{8,7},{9,8},{10,9},{11,1... | collective-permute-start | bytes 491528 | tf_op jit(solution)/shard_map/ppermute | solution.py:21
  221.1 0.5 copy-start.4
  221.7 1.6 copy-start.2
  223.3 4.3 collective-permute-start.21
  225.2 6.3 %collective-permute-start.20 = (f32[1,8,8,512]{3,2,1,0:T(8,128)S(1)}, f32[1,8,8,512]{3,2,1,0:T(8,128)S(1)}, u32[]{:S(2)}, u32[]{:S(2)}) collective-permute-start(f32[1,8,8,512]{3,2,1,0:T(8,128)S(1)} %get-tuple-element.42), channel_id=1, source_target_pairs={{16,0},{32,16},{48,32},{64,48},{80,64},{96,80},{112,96},{128,112},... | collective-permute-start | bytes 393224 | tf_op jit(solution)/shard_map/ppermute | solution.py:21
  231.5 4.7 collective-permute-start.23
  234.0 6.1 %collective-permute-start.22 = (f32[10,1,8,512]{3,2,1,0:T(8,128)S(1)}, f32[10,1,8,512]{3,2,1,0:T(8,128)S(1)}, u32[]{:S(2)}, u32[]{:S(2)}) collective-permute-start(f32[10,1,8,512]{3,2,1,0:T(8,128)S(1)} %get-tuple-element.22), channel_id=1, source_target_pairs={{1,0},{2,1},{3,2},{4,3},{5,4},{6,5},{7,6},{8,7},{9,8},{10,9},{11,1... | collective-permute-start | bytes 491528 | tf_op jit(solution)/shard_map/ppermute | solution.py:21
  241.3 6.8 %collective-permute-start.25 = (f32[1,8,8,512]{3,2,1,0:T(8,128)S(1)}, f32[1,8,8,512]{3,2,1,0:T(8,128)S(1)}, u32[]{:S(2)}, u32[]{:S(2)}) collective-permute-start(f32[1,8,8,512]{3,2,1,0:T(8,128)S(1)} %get-tuple-element.39), channel_id=1, source_target_pairs={{0,16},{16,32},{32,48},{48,64},{64,80},{80,96},{96,112},{112,128},... | collective-permute-start | bytes 393224 | tf_op jit(solution)/shard_map/ppermute | solution.py:18
  246.2 6.3 %collective-permute-start.24 = (f32[1,8,8,512]{3,2,1,0:T(8,128)S(1)}, f32[1,8,8,512]{3,2,1,0:T(8,128)S(1)}, u32[]{:S(2)}, u32[]{:S(2)}) collective-permute-start(f32[1,8,8,512]{3,2,1,0:T(8,128)S(1)} %get-tuple-element.40), channel_id=1, source_target_pairs={{16,0},{32,16},{48,32},{64,48},{80,64},{96,80},{112,96},{128,112},... | collective-permute-start | bytes 393224 | tf_op jit(solution)/shard_map/ppermute | solution.py:21
  252.5 4.4 collective-permute-start.27
  254.7 6.5 %collective-permute-start.26 = (f32[10,1,8,512]{3,2,1,0:T(8,128)S(1)}, f32[10,1,8,512]{3,2,1,0:T(8,128)S(1)}, u32[]{:S(2)}, u32[]{:S(2)}) collective-permute-start(f32[10,1,8,512]{3,2,1,0:T(8,128)S(1)} %get-tuple-element.20), channel_id=1, source_target_pairs={{1,0},{2,1},{3,2},{4,3},{5,4},{6,5},{7,6},{8,7},{9,8},{10,9},{11,1... | collective-permute-start | bytes 491528 | tf_op jit(solution)/shard_map/ppermute | solution.py:21
  289.0 11.8 %collective-permute-start.29 = (f32[1,8,8,512]{3,2,1,0:T(8,128)S(1)}, f32[1,8,8,512]{3,2,1,0:T(8,128)S(1)}, u32[]{:S(2)}, u32[]{:S(2)}) collective-permute-start(f32[1,8,8,512]{3,2,1,0:T(8,128)S(1)} %get-tuple-element.37), channel_id=1, source_target_pairs={{0,16},{16,32},{32,48},{48,64},{64,80},{80,96},{96,112},{112,128},... | collective-permute-start | bytes 393224 | tf_op jit(solution)/shard_map/ppermute | solution.py:18
  298.9 6.3 %collective-permute-start.28 = (f32[1,8,8,512]{3,2,1,0:T(8,128)S(1)}, f32[1,8,8,512]{3,2,1,0:T(8,128)S(1)}, u32[]{:S(2)}, u32[]{:S(2)}) collective-permute-start(f32[1,8,8,512]{3,2,1,0:T(8,128)S(1)} %get-tuple-element.38), channel_id=1, source_target_pairs={{16,0},{32,16},{48,32},{64,48},{80,64},{96,80},{112,96},{128,112},... | collective-permute-start | bytes 393224 | tf_op jit(solution)/shard_map/ppermute | solution.py:21
  305.2 3.5 collective-permute-start.31
  306.6 6.1 %collective-permute-start.30 = (f32[10,1,8,512]{3,2,1,0:T(8,128)S(1)}, f32[10,1,8,512]{3,2,1,0:T(8,128)S(1)}, u32[]{:S(2)}, u32[]{:S(2)}) collective-permute-start(f32[10,1,8,512]{3,2,1,0:T(8,128)S(1)} %get-tuple-element.18), channel_id=1, source_target_pairs={{1,0},{2,1},{3,2},{4,3},{5,4},{6,5},{7,6},{8,7},{9,8},{10,9},{11,1... | collective-permute-start | bytes 491528 | tf_op jit(solution)/shard_map/ppermute | solution.py:21
  314.0 6.4 %collective-permute-start.33 = (f32[1,8,8,512]{3,2,1,0:T(8,128)S(1)}, f32[1,8,8,512]{3,2,1,0:T(8,128)S(1)}, u32[]{:S(2)}, u32[]{:S(2)}) collective-permute-start(f32[1,8,8,512]{3,2,1,0:T(8,128)S(1)} %get-tuple-element.35), channel_id=1, source_target_pairs={{0,16},{16,32},{32,48},{48,64},{64,80},{80,96},{96,112},{112,128},... | collective-permute-start | bytes 393224 | tf_op jit(solution)/shard_map/ppermute | solution.py:18
  318.5 6.3 %collective-permute-start.32 = (f32[1,8,8,512]{3,2,1,0:T(8,128)S(1)}, f32[1,8,8,512]{3,2,1,0:T(8,128)S(1)}, u32[]{:S(2)}, u32[]{:S(2)}) collective-permute-start(f32[1,8,8,512]{3,2,1,0:T(8,128)S(1)} %get-tuple-element.36), channel_id=1, source_target_pairs={{16,0},{32,16},{48,32},{64,48},{80,64},{96,80},{112,96},{128,112},... | collective-permute-start | bytes 393224 | tf_op jit(solution)/shard_map/ppermute | solution.py:21
  324.8 6.0 %collective-permute-start.35 = (f32[10,1,8,512]{3,2,1,0:T(8,128)S(1)}, f32[10,1,8,512]{3,2,1,0:T(8,128)S(1)}, u32[]{:S(2)}, u32[]{:S(2)}) collective-permute-start(f32[10,1,8,512]{3,2,1,0:T(8,128)S(1)} %get-tuple-element.15), channel_id=1, source_target_pairs={{0,1},{1,2},{2,3},{3,4},{4,5},{5,6},{6,7},{7,8},{8,9},{9,10},{10,1... | collective-permute-start | bytes 491528 | tf_op jit(solution)/shard_map/ppermute | solution.py:18
  328.6 6.1 %collective-permute-start.34 = (f32[10,1,8,512]{3,2,1,0:T(8,128)S(1)}, f32[10,1,8,512]{3,2,1,0:T(8,128)S(1)}, u32[]{:S(2)}, u32[]{:S(2)}) collective-permute-start(f32[10,1,8,512]{3,2,1,0:T(8,128)S(1)} %get-tuple-element.16), channel_id=1, source_target_pairs={{1,0},{2,1},{3,2},{4,3},{5,4},{6,5},{7,6},{8,7},{9,8},{10,9},{11,1... | collective-permute-start | bytes 491528 | tf_op jit(solution)/shard_map/ppermute | solution.py:21
  335.2 81.6 %copy-start.5 = (f32[8]{0:T(128)S(1)}, f32[8]{0:T(128)}, u32[]{:S(2)}) copy-start(f32[8]{0:T(128)} %copy-done.4) | copy-start | bytes 100
  418.3 4.3 collective-permute-start.37
  420.3 6.3 %collective-permute-start.36 = (f32[1,8,8,512]{3,2,1,0:T(8,128)S(1)}, f32[1,8,8,512]{3,2,1,0:T(8,128)S(1)}, u32[]{:S(2)}, u32[]{:S(2)}) collective-permute-start(f32[1,8,8,512]{3,2,1,0:T(8,128)S(1)} %get-tuple-element.34), channel_id=1, source_target_pairs={{16,0},{32,16},{48,32},{64,48},{80,64},{96,80},{112,96},{128,112},... | collective-permute-start | bytes 393224 | tf_op jit(solution)/shard_map/ppermute | solution.py:21
  426.7 3.8 collective-permute-start.39
  428.2 6.1 %collective-permute-start.38 = (f32[10,1,8,512]{3,2,1,0:T(8,128)S(1)}, f32[10,1,8,512]{3,2,1,0:T(8,128)S(1)}, u32[]{:S(2)}, u32[]{:S(2)}) collective-permute-start(f32[10,1,8,512]{3,2,1,0:T(8,128)S(1)} %get-tuple-element.14), channel_id=1, source_target_pairs={{1,0},{2,1},{3,2},{4,3},{5,4},{6,5},{7,6},{8,7},{9,8},{10,9},{11,1... | collective-permute-start | bytes 491528 | tf_op jit(solution)/shard_map/ppermute | solution.py:21
  434.9 81.5 %copy-start.3 = (f32[8]{0:T(128)S(1)}, f32[8]{0:T(128)}, u32[]{:S(2)}) copy-start(f32[8]{0:T(128)} %copy-done.2) | copy-start | bytes 100
where the time goes:
time: 521 us; the launch traced here: 519 us
  blocking collectives  286 us (55%)
  starting transfers between devices  110 us (21%)
  waiting for transfers between devices  90.7 us (17%)
  other arithmetic  25.9 us (5%)
    psum x2, blocking collectives, energy_sum(): return lax.psum(probe_dot(residual, precond), ('gx', 'gy'))  164 us
    ppermute x20, waiting for transfers between devices, with_halo(): lax.ppermute(lax.slice_in_dim(block, 0, width, axis=dim), axis, backward)  81.3 us
    psum x1, blocking collectives, body(): curvature = lax.psum(probe_dot(search, op_image), ('gx', 'gy'))  79.8 us
    ppermute x20, starting transfers between devices, with_halo(): lax.ppermute(lax.slice_in_dim(block, block.shape[dim] - width, None, axis...  77 us
    all_gather x2, blocking collectives, coarse_solve(): lax.all_gather(local_means, 'gy', axis=1, tiled=True)  42.5 us
    ppermute x20, starting transfers between devices, with_halo(): lax.ppermute(lax.slice_in_dim(block, 0, width, axis=dim), axis, backward)  33 us
  transfers between devices with their start and end apart: 40, of which 30 were waited for; matrix products, arithmetic and copies ran while one was open for 0% of the time, Pallas kernels for 0%

commit v1 on v0

v1 whole, which is shorter than its diff:
```python
import functools

import jax
import jax.numpy as jnp
from jax import lax
from jax.experimental import pallas as pl
from jax.experimental.pallas import tpu as pltpu
from jax.sharding import Mesh
from jax.sharding import PartitionSpec as P

OMEGA = 2.0 / 3.0
THIRD = 1.0 / 3.0
L = 128
CH = 4
HALO = 4
GX = ("z", "core")
SLAB2 = ("core", "gy")
ALL = ("z", "core", "gy")
CORNERS = ((-1, -1), (-1, 1), (1, -1), (1, 1))
HIGHEST = lax.Precision.HIGHEST


def lanes():
    return lax.broadcasted_iota(jnp.int32, (8, L), 1)


def ld(ref, x, y):
    return [ref[x, y, :, k * L : (k + 1) * L] for k in range(CH)]


def row(ref, x, y):
    return [jnp.broadcast_to(ref[x, pl.ds(y, 1), k * L : (k + 1) * L], (8, L)) for k in range(CH)]


def put(ref, x, y, values):
    for k in range(CH):
        ref[x, y, :, k * L : (k + 1) * L] = values[k]


def zsum(v, lane):
    up = [pltpu.roll(c, 1, 1) for c in v]
    down = [pltpu.roll(c, L - 1, 1) for c in v]
    out = []
    for k in range(CH):
        before = up[k - 1] if k > 0 else jnp.zeros_like(up[0])
        after = down[k + 1] if k < CH - 1 else jnp.zeros_like(up[0])
        out.append(jnp.where(lane == 0, before, up[k]) + jnp.where(lane == L - 1, after, down[k]))
    return out


def add(*terms):
    return [functools.reduce(lambda a, b: a + b, t) for t in zip(*terms)]


def mul(a, b):
    return [p * q for p, q in zip(a, b)]


def scale(s, a):
    return [s * p for p in a]


def join(v):
    return jnp.concatenate(v, axis=1)


def beside_rows(ref, x, lo, hi, lane):
    prev, here = ld(ref, x, lo - 1), ld(ref, x, lo)
    for y in range(lo, hi):
        after = ld(ref, x, y + 1)
        near = add(prev, after, ld(ref, x - 1, y), ld(ref, x + 1, y), zsum(here, lane))
        yield y, here, near
        prev, here = here, after


def shares(h_ref, source, g_own, g_faces, rows_ref):
    lane = lanes()
    zero = [jnp.zeros((8, L), jnp.float32)] * CH

    def one_row(i, carry):
        a1, ylo, yhi = carry
        total = zero
        for y, here, near in beside_rows(h_ref, i + 1, 1, 9, lane):
            j = y - 1
            t1 = add(scale(THIRD, source(i, j)), near)
            s = mul(g_own(i, j), t1)
            a1 = add(a1, t1)
            total = add(total, s)
            if j == 0:
                ylo = add(ylo, s)
            if j == 7:
                yhi = add(yhi, s)
        for k in range(CH):
            rows_ref[i, :, k * L : (k + 1) * L] = total[k]
        return a1, ylo, yhi

    a1, ylo, yhi = lax.fori_loop(0, 8, one_row, (zero, zero, zero))
    rows = [[rows_ref[i, :, k * L : (k + 1) * L] for k in range(CH)] for i in range(8)]
    s_all = add(*rows)
    edges = (rows[0], rows[7], ylo, yhi)
    faces = []
    for f, (cells, edge) in enumerate(
        zip(
            (
                [(1, j + 1) for j in range(8)],
                [(8, j + 1) for j in range(8)],
                [(i + 1, 1) for i in range(8)],
                [(i + 1, 8) for i in range(8)],
            ),
            edges,
        )
    ):
        t_sum, s_sum = zero, zero
        for n, (x, y) in enumerate(cells):
            t = ld(h_ref, x, y)
            s = mul(g_faces(f, n), t)
            t_sum, s_sum = add(t_sum, t), add(s_sum, s)
            if n == 0:
                first = s
            if n == 7:
                last = s
        part = add(
            scale(THIRD, t_sum),
            edge,
            scale(3.0, s_sum),
            scale(-1.0, add(first, last)),
            zsum(s_sum, lane),
        )
        faces.append((part, s_sum, first, last))
    (xl, sxl, xl0, xl7), (xh, sxh, xh0, xh7), (yl, syl, yl0, yl7), (yh, syh, yh0, yh7) = faces
    own = add(
        scale(THIRD, a1),
        scale(4.0, s_all),
        scale(-1.0, add(*edges)),
        sxl,
        sxh,
        syl,
        syh,
        zsum(s_all, lane),
    )
    parts = [
        add(xl0, yl0),
        xl,
        add(xl7, yh0),
        yl,
        own,
        yh,
        add(xh0, yl7),
        xh,
        add(xh7, yh7),
    ]
    stacked = jnp.concatenate([join(p) for p in parts], axis=0)
    zi = lax.broadcasted_iota(jnp.int32, (CH * L, L), 0)
    li = lax.broadcasted_iota(jnp.int32, (CH * L, L), 1)
    fold = jnp.where((zi // 32) == (li % 16), 1.0 / 2048.0, 0.0)
    sums = jnp.dot(stacked, fold, precision=HIGHEST, preferred_element_type=jnp.float32)
    r = lax.broadcasted_iota(jnp.int32, (8, L), 0)
    keep = (lane // 16) == r
    out = [
        jnp.sum(jnp.where(keep, sums[8 * n : 8 * n + 8], 0.0), axis=0, keepdims=True)
        for n in range(9)
    ]
    return jnp.concatenate(out, axis=0)


def fill_border(ref):
    zero = jnp.zeros((8, CH * L), jnp.float32)

    def one(i, carry):
        ref[0, i] = zero
        ref[9, i] = zero
        ref[i, 0] = zero
        ref[i, 9] = zero
        return carry

    lax.fori_loop(0, 10, one, 0)


def first_shares_kernel(b_ref, kap_ref, kxl, kxh, kyl, kyh, has_ref, out_ref, h_ref, g_ref, gf_ref, rows_ref):
    fill_border(h_ref)

    def one_row(i, carry):
        g_ref[i] = OMEGA / (6.0 + kap_ref[i])
        gf_ref[2, pl.ds(i, 1)] = OMEGA / (6.0 + kyl[i, 7:8]) * has_ref[2]
        gf_ref[3, pl.ds(i, 1)] = OMEGA / (6.0 + kyh[i, 0:1]) * has_ref[3]
        for j in range(8):
            put(h_ref, i + 1, j + 1, mul(row(g_ref, i, j), ld(b_ref, i, j)))
        return carry

    lax.fori_loop(0, 8, one_row, 0)
    gf_ref[0] = OMEGA / (6.0 + kxl[3]) * has_ref[0]
    gf_ref[1] = OMEGA / (6.0 + kxh[0]) * has_ref[1]
    out_ref[...] = shares(
        h_ref,
        lambda i, j: ld(b_ref, i, j),
        lambda i, j: row(g_ref, i, j),
        lambda f, n: row(gf_ref, f, n),
        rows_ref,
    )


def coarse_values(recv_ref, inv_ref, c_ref, count):
    lane = lanes()
    parts = []
    for t in range(3):
        total = jnp.zeros((48, L), jnp.float32)
        for j in range(count):
            value = None
            for dy in (-1, 0, 1):
                if not 0 <= j - dy < count:
                    continue
                for c in range(2):
                    term = recv_ref[c * count + j - dy, pl.ds(t * 3 + dy + 1, 1), :]
                    value = term if value is None else value + term
            total = total + inv_ref[t, j] * jnp.broadcast_to(value, (48, L))
        parts.append(total)
    r = lax.broadcasted_iota(jnp.int32, (8, L), 0)
    pick = jnp.where((lane // 16) == r, 1.0, 0.0)
    for t in range(3):
        c = lax.dot_general(
            pick,
            parts[t],
            (((1,), (1,)), ((), ())),
            precision=HIGHEST,
            preferred_element_type=jnp.float32,
        )
        for jj in range(3):
            for k in range(CH):
                out = jnp.zeros((8, L), jnp.float32)
                for q in range(4):
                    m = jj * 16 + k * 4 + q
                    out = jnp.where((lane // 32) == q, jnp.broadcast_to(c[:, m : m + 1], (8, L)), out)
                c_ref[t * 3 + jj, :, k * L : (k + 1) * L] = out


def cycle_kernel(first, count, *refs):
    (f_own, f_xl, f_xh, f_yl, f_yh, f_c0, f_c1, f_c2, f_c3, b_c0, b_c1, b_c2, b_c3) = refs[:13]
    kap_ref, kxl, kxh, kyl, kyh, has_ref, recv_ref, inv_ref = refs[13:21]
    refs = refs[21:]
    if first:
        z_ref, q_ref, dots_ref, out_ref = refs[:4]
        refs = refs[4:]
    else:
        extra_ref, earlier_ref, z_ref, q_ref, dots_ref = refs[:5]
        refs = refs[5:]
    F, A, B, G, KC, c_ref, h_ref, gf_ref, rows_ref, sems = refs
    n_sem = iter(range(64))
    copies = []

    def start(src, dst):
        copy = pltpu.make_async_copy(src, dst, sems.at[next(n_sem)])
        copy.start()
        copies.append(copy)

    for n, ref in enumerate((b_c0, b_c1, b_c2, b_c3)):
        start(ref.at[6:9], KC.at[n])
    start(f_own, F.at[4:12, 4:12])
    start(f_xl, F.at[0:4, 4:12])
    start(f_xh, F.at[12:16, 4:12])
    start(f_yl, F.at[4:12, 0:4])
    start(f_yh, F.at[4:12, 12:16])
    for (sx, sy), ref in zip(CORNERS, (f_c0, f_c1, f_c2, f_c3)):
        at = 0
        for a in (1, 2, 3):
            wide = 4 - a
            x = 4 - a if sx < 0 else 11 + a
            y = 4 - wide if sy < 0 else 12
            start(ref.at[at : at + wide], F.at[x, y : y + wide])
            at += wide

    zero = jnp.zeros((8, CH * L), jnp.float32)
    for x, y in [(a, b) for a in range(4) for b in range(4) if (4 - a) + (4 - b) > 4]:
        for xx, yy in ((x, y), (x, 15 - y), (15 - x, y), (15 - x, 15 - y)):
            F[xx, yy] = zero

    def inv_diag(kappa):
        return OMEGA / (6.0 + kappa)

    coarse_values(recv_ref, inv_ref, c_ref, count)

    for copy in copies[:4]:
        copy.wait()
    for i in range(8):
        G[4 + i, 8:16] = inv_diag(kap_ref[i])
        G[4 + i, 0:8] = inv_diag(kyl[i]) * has_ref[2]
        G[4 + i, 16:24] = inv_diag(kyh[i]) * has_ref[3]
    for a in range(4):
        G[a, 8:16] = inv_diag(kxl[a]) * has_ref[0]
        G[12 + a, 8:16] = inv_diag(kxh[a]) * has_ref[1]
    for n, (sx, sy) in enumerate(CORNERS):
        mask = has_ref[0 if sx < 0 else 1] * has_ref[2 if sy < 0 else 3]
        y = 0 if sy < 0 else 16
        G[0 if sx < 0 else 15, y : y + 8] = zero
        for a in (1, 2, 3):
            x = 4 - a if sx < 0 else 11 + a
            G[x, y : y + 8] = inv_diag(KC[n, a - 1]) * mask
    for copy in copies[4:]:
        copy.wait()

    lane = lanes()

    def start_row(x, carry):
        for y in range(16):
            put(A, x, y, mul(row(G, x, y + 4), ld(F, x, y)))
        return carry

    lax.fori_loop(0, 16, start_row, 0)

    def sweep(src, dst, edge, coarse):
        def one_row(x, carry):
            t = jnp.where(x >= 4, 1, 0) + jnp.where(x >= 12, 1, 0)
            for y, here, near in beside_rows(src, x, edge, 16 - edge, lane):
                new = add(scale(THIRD, here), mul(add(ld(F, x, y), near), row(G, x, y + 4)))
                if coarse:
                    jj = (1 if y >= 4 else 0) + (1 if y >= 12 else 0)
                    new = add(new, [c_ref[t * 3 + jj, :, k * L : (k + 1) * L] for k in range(CH)])
                put(dst, x, y, new)
            return carry

        lax.fori_loop(edge, 16 - edge, one_row, 0)

    sweep(A, B, 1, True)
    sweep(B, A, 2, False)
    sweep(A, B, 3, False)
    if first:
        fill_border(h_ref)
    nil = jnp.zeros((8, L), jnp.float32)

    def image_row(i, carry):
        fz, zq, ez = carry
        x = i + 4
        for y, here, near in beside_rows(B, x, 4, 12, lane):
            j = y - 4
            kappa = row(kap_ref, i, j)
            image = [(6.0 + kappa[k]) * here[k] - near[k] for k in range(CH)]
            put(z_ref, i, j, here)
            put(q_ref, i, j, image)
            source = ld(F, x, y)
            fz = functools.reduce(lambda a, b: a + b, mul(source, here), fz)
            zq = functools.reduce(lambda a, b: a + b, mul(here, image), zq)
            if first:
                put(h_ref, i + 1, j + 1, mul(row(G, x, y + 4), image))
            else:
                ez = functools.reduce(lambda a, b: a + b, mul(ld(extra_ref, i, j), here), ez)
        return fz, zq, ez

    fz, zq, ez = lax.fori_loop(0, 8, image_row, (nil, nil, nil))
    if first:
        dots_ref[0] = fz
        dots_ref[1] = zq
        gf_ref[0] = G[3, 8:16]
        gf_ref[1] = G[12, 8:16]
        for i in range(8):
            gf_ref[2, pl.ds(i, 1)] = G[4 + i, 7:8]
            gf_ref[3, pl.ds(i, 1)] = G[4 + i, 16:17]
        out_ref[...] = shares(
            h_ref,
            lambda i, j: ld(q_ref, i, j),
            lambda i, j: row(G, i + 4, j + 8),
            lambda f, n: row(gf_ref, f, n),
            rows_ref,
        )
    else:
        total = [earlier_ref[0], earlier_ref[1], fz, zq, ez]
        packed = nil
        for k, part in enumerate(total):
            packed = jnp.where(lane == k, jnp.sum(part, axis=1, keepdims=True), packed)
        dots_ref[...] = packed


def combine_kernel(sums_ref, b_ref, z_ref, q_ref, w_ref, v_ref, x_ref, r_ref):
    sums = sums_ref[0]
    for n in range(1, sums_ref.shape[0]):
        sums = sums + sums_ref[n]
    bz, zq, qw, wv, bw = (sums[:, k : k + 1] for k in range(5))
    a0 = bz / zq
    e1 = bz - a0 * (bw + zq) + a0 * a0 * qw
    beta = e1 / bz
    z1q = zq - a0 * qw
    z1v = zq - 2.0 * a0 * qw + a0 * a0 * wv
    a1 = e1 / (z1v + 2.0 * beta * z1q + beta * beta * zq)
    cz = a0 + a1 * (1.0 + beta)
    cw = a1 * a0
    cz = jnp.broadcast_to(cz, (8, CH * L))
    cw = jnp.broadcast_to(cw, (8, CH * L))
    for i in range(x_ref.shape[0]):
        for j in range(x_ref.shape[1]):
            x_ref[i, j] = cz * z_ref[i, j] - cw * w_ref[i, j]
            r_ref[i, j] = b_ref[i, j] - cz * q_ref[i, j] + cw * v_ref[i, j]


def shift(value, axes, sizes, steps):
    pairs = []
    total = 1
    for n in sizes:
        total *= n
    for flat in range(total):
        rest, target = flat, 0
        weight = 1
        for n, step in zip(reversed(sizes), reversed(steps)):
            at = rest % n
            rest //= n
            target += ((at + step) % n) * weight
            weight *= n
        pairs.append((flat, target))
    return lax.ppermute(value, axes, pairs)


def corner_cells(field, sx, sy):
    pieces = []
    for a in (1, 2, 3):
        x = 8 - a if sx > 0 else a - 1
        wide = 4 - a
        y = 8 - wide if sy > 0 else 0
        pieces.append(field[x, y : y + wide])
    return pieces


def corner_rows(kappa, sx):
    return kappa[5:8][::-1] if sx > 0 else kappa[0:3]


VM = pl.BlockSpec(memory_space=pltpu.VMEM)
SM = pl.BlockSpec(memory_space=pltpu.SMEM)
HB = pl.BlockSpec(memory_space=pl.ANY)


def solution(mesh):
    n_gx, n_gy = mesh.shape["gx"], mesh.shape["gy"]
    n_z = n_gx // 2
    fine = Mesh(mesh.devices.reshape(n_z, 2, n_gy), ALL)

    def halo(field):
        xl = shift(field[4:8], GX, (n_gx,), (1,))
        xh = shift(field[0:4], GX, (n_gx,), (-1,))
        yl = shift(field[:, 4:8], ("gy",), (n_gy,), (1,))
        yh = shift(field[:, 0:4], ("gy",), (n_gy,), (-1,))
        return [xl, xh, yl, yh]

    def corners(field, kappa):
        out = []
        for sx, sy in CORNERS:
            pieces = corner_cells(field, -sx, -sy)
            if kappa is not None:
                pieces.append(corner_rows(kappa, -sx))
            packed = jnp.concatenate(pieces, axis=0)
            out.append(shift(packed, ALL, (n_gx, n_gy), (-sx, -sy)))
        return out

    def gather_shares(own, z, core):
        low = shift(own, ("z",), (n_z,), (1,)).reshape(3, 3, L)
        high = shift(own, ("z",), (n_z,), (-1,)).reshape(3, 3, L)
        low = jnp.where(z > 0, low, 0.0)
        high = jnp.where(z < n_z - 1, high, 0.0)
        own = own.reshape(3, 3, L)
        none = jnp.zeros((1, 3, L), jnp.float32)
        even = jnp.concatenate([own[0:1] + low[2:3], own[1:2], own[2:3] + high[0:1], high[1:2]])
        odd = jnp.concatenate([low[1:2], own[0:1] + low[2:3], own[1:2], own[2:3] + high[0:1]])
        total = jnp.where(core == 0, even, odd)
        to_even = jnp.broadcast_to(total[0:3].reshape(1, 9, L), (n_gy, 9, L))
        to_odd = jnp.broadcast_to(total[1:4].reshape(1, 9, L), (n_gy, 9, L))
        return lax.all_to_all(jnp.concatenate([to_even, to_odd]), SLAB2, 0, 0)

    def body(b, kappa, inverse):
        f32 = jnp.float32
        z, core, gy = lax.axis_index("z"), lax.axis_index("core"), lax.axis_index("gy")
        gx = z * 2 + core
        has = jnp.stack([gx > 0, gx < n_gx - 1, gy > 0, gy < n_gy - 1]).astype(f32)

        kxl, kxh, kyl, kyh = (
            shift(kappa[4:8], GX, (n_gx,), (1,)),
            shift(kappa[0:4], GX, (n_gx,), (-1,)),
            shift(kappa, ("gy",), (n_gy,), (1,)),
            shift(kappa, ("gy",), (n_gy,), (-1,)),
        )
        first_own = pl.pallas_call(
            first_shares_kernel,
            out_shape=jax.ShapeDtypeStruct((9, L), f32),
            in_specs=[VM] * 6 + [SM],
            out_specs=VM,
            scratch_shapes=[
                pltpu.VMEM((10, 10, 8, CH * L), f32),
                pltpu.VMEM((8, 8, CH * L), f32),
                pltpu.VMEM((4, 8, CH * L), f32),
                pltpu.VMEM((8, 8, CH * L), f32),
            ],
            compiler_params=pltpu.CompilerParams(vmem_limit_bytes=20 << 20),
            name="first_shares",
        )(b, kappa, kxl, kxh, kyl, kyh, has)

        near = jnp.pad(inverse, ((16, 16), (0, 0)))
        near = lax.dynamic_slice_in_dim(near, gy * 16, 48, 0)
        near_low = shift(near, GX, (n_gx,), (1,)) * has[0]
        near_high = shift(near, GX, (n_gx,), (-1,)) * has[1]
        inv = jnp.stack([near_low, near, near_high]).reshape(3, 48, n_gy, 16)
        inv = jnp.tile(jnp.transpose(inv, (0, 2, 1, 3)), (1, 1, 1, 8))

        b_halo = halo(b)
        b_corners = corners(b, kappa)

        def cycle(first, field, faces, diagonals, received, more):
            tile = jax.ShapeDtypeStruct((8, 8, 8, CH * L), f32)
            outs = [tile, tile]
            if first:
                outs += [jax.ShapeDtypeStruct((2, 8, L), f32), jax.ShapeDtypeStruct((9, L), f32)]
            else:
                outs += [jax.ShapeDtypeStruct((8, L), f32)]
            big = pltpu.VMEM((16, 16, 8, CH * L), f32)
            return pl.pallas_call(
                functools.partial(cycle_kernel, first, n_gy),
                out_shape=outs,
                in_specs=[HB] * 13 + [VM] * 5 + [SM] + [VM] * (2 + len(more)),
                out_specs=[VM] * len(outs),
                scratch_shapes=[
                    big,
                    big,
                    big,
                    pltpu.VMEM((16, 24, CH * L), f32),
                    pltpu.VMEM((4, 3, 8, CH * L), f32),
                    pltpu.VMEM((9, 8, CH * L), f32),
                    pltpu.VMEM((10, 10, 8, CH * L), f32),
                    pltpu.VMEM((4, 8, CH * L), f32),
                    pltpu.VMEM((8, 8, CH * L), f32),
                    pltpu.SemaphoreType.DMA((24,)),
                ],
                compiler_params=pltpu.CompilerParams(vmem_limit_bytes=40 << 20),
                name="first_cycle" if first else "second_cycle",
            )(field, *faces, *diagonals, *b_corners, kappa, kxl, kxh, kyl, kyh, has, received, inv, *more)

        received = gather_shares(first_own, z, core)
        z0, q0, dots, own = cycle(True, b, b_halo, b_corners, received, [])
        q_halo = halo(q0)
        q_corners = corners(q0, None)
        received = gather_shares(own, z, core)
        w0, v0, packed = cycle(False, q0, q_halo, q_corners, received, [b, dots])

        near_sum = jnp.sum(
            lax.all_to_all(jnp.broadcast_to(packed, (2 * n_gy, 8, L)), SLAB2, 0, 0), axis=0
        )
        sums = lax.all_to_all(jnp.broadcast_to(near_sum, (n_z, 8, L)), "z", 0, 0)
        tile = pl.BlockSpec((1, 8, 8, CH * L), lambda i: (i, 0, 0, 0))
        return pl.pallas_call(
            combine_kernel,
            grid=(8,),
            out_shape=[jax.ShapeDtypeStruct((8, 8, 8, CH * L), f32)] * 2,
            in_specs=[pl.BlockSpec((n_z, 8, L), lambda i: (0, 0, 0))] + [tile] * 5,
            out_specs=[tile, tile],
            name="combine",
        )(sums, b, z0, q0, w0, v0)

    field = P(GX, "gy", None, None)
    return jax.shard_map(
        body,
        mesh=fine,
        in_specs=(field, P(GX, "gy", None), P(GX, None)),
        out_specs=(field, field),
        check_vma=False,
    )
```

time: 521 us -> 194 us (0.37)
  blocking collectives: 286 us -> 28 us
  waiting for transfers between devices: 90.7 us -> 16.7 us
  starting transfers between devices: 110 us -> 60.5 us
  local copies, waits for them, and re-layouts: 5.02 us -> 46.4 us
  Pallas kernels: 0 us -> 33.7 us
  other arithmetic: 25.9 us -> 5.77 us
    psum x3 -> x0, blocking collectives: 244 us -> none  [the longest x2 164 us: energy_sum(): return lax.psum(probe_dot(residual, precond), ('gx', 'gy'))]
    ppermute x40 -> x26, waiting for transfers between devices: 90.7 us -> 16.4 us  [shift(): return lax.ppermute(value, axes, pairs)]
    ppermute x40 -> x26, starting transfers between devices: 110 us -> 50.7 us  [shift(): return lax.ppermute(value, axes, pairs)]
    all_gather x2 -> x0, blocking collectives: 42.5 us -> none  [coarse_solve(): lax.all_gather(local_means, 'gy', axis=1, tiled=True)]
    pallas_call x0 -> x4, Pallas kernels: none -> 33.7 us  [the longest x2 23.4 us: cycle(): pl.pallas_call(functools.partial(cycle_kernel, first, n_gy), out_shape=ou...]
    all_to_all x0 -> x2, blocking collectives: none -> 28 us  [the longest x1 15 us: body(): lax.all_to_all(jnp.broadcast_to(packed, (2 * n_gy, 8, L)), SLAB2, 0, 0)]
    unnamed x14 -> x77, local copies, waits for them, and re-layouts: 1.55 us -> 25.1 us
    all_to_all x0 -> x2, starting transfers between devices: none -> 9.81 us  [gather_shares(): return lax.all_to_all(jnp.concatenate([to_even, to_odd]), SLAB2, 0, 0)]
  transfers between devices with their start and end apart: 40 -> 28, of which waited for: 30 -> 6; matrix products, arithmetic and copies ran while one was open for 0% -> 15% of each run, Pallas kernels for 0% -> 1%
where the time goes in v1:
time: 194 us; the launch traced here: 192 us
  starting transfers between devices  60.5 us (31%)
  local copies, waits for them, and re-layouts  46.4 us (24%)
  Pallas kernels  33.7 us (17%)
  blocking collectives  28 us (14%)
  waiting for transfers between devices  16.7 us (9%)
  other arithmetic  5.77 us (3%)
    ppermute x26, starting transfers between devices, shift(): return lax.ppermute(value, axes, pairs)  50.7 us
    unnamed x77, local copies, waits for them, and re-layouts  25.1 us
    pallas_call x2, Pallas kernels, cycle(): pl.pallas_call(functools.partial(cycle_kernel, first, n_gy), out_shape=ou...  23.4 us
    ppermute x26, waiting for transfers between devices, shift(): return lax.ppermute(value, axes, pairs)  16.4 us
    all_to_all x1, blocking collectives, body(): lax.all_to_all(jnp.broadcast_to(packed, (2 * n_gy, 8, L)), SLAB2, 0, 0)  15 us
    all_to_all x1, blocking collectives, body(): sums = lax.all_to_all(jnp.broadcast_to(near_sum, (n_z, 8, L)), 'z', 0, 0)  13 us
    all_to_all x2, starting transfers between devices, gather_shares(): return lax.all_to_all(jnp.concatenate([to_even, to_odd]), SLAB2, 0, 0)  9.81 us
    pallas_call x1, Pallas kernels, body(): pl.pallas_call(combine_kernel, grid=(8,), out_shape=[jax.ShapeDtypeStruct...  7.97 us
  transfers between devices with their start and end apart: 28, of which 6 were waited for; matrix products, arithmetic and copies ran while one was open for 15% of the time, Pallas kernels for 1%

profile of v1, /device:TPU:1, one launch (start us, length us, event | category | flops | bytes accessed | tf_op | source)
XLA Modules:
  0.0 192.1 jit_solution(8220027962958692201)
XLA Ops:
  0.6 2.1 %collective-permute-start.10 = (f32[8,8,512]{2,1,0:T(8,128)}, f32[8,8,512]{2,1,0:T(8,128)S(1)}, u32[]{:S(2)}, u32[]{:S(2)}) collective-permute-start(f32[8,8,512]{2,1,0:T(8,128)} %refs_13_.3), channel_id=1, source_target_pairs={{0,1},{1,2},{2,3},{3,4},{4,5},{5,6},{6,7},{7,8},{8,9},{9,10},{10,1... | collective-permute-start | bytes 393224 | tf_op jit(solution)/shard_map/ppermute | solution.py:406
  2.8 3.8 %collective-permute-start.11 = (f32[8,8,512]{2,1,0:T(8,128)}, f32[8,8,512]{2,1,0:T(8,128)S(1)}, u32[]{:S(2)}, u32[]{:S(2)}) collective-permute-start(f32[8,8,512]{2,1,0:T(8,128)} %refs_13_.3), channel_id=1, source_target_pairs={{0,15},{1,0},{2,1},{3,2},{4,3},{5,4},{6,5},{7,6},{8,7},{9,8},{10,9... | collective-permute-start | bytes 393224 | tf_op jit(solution)/shard_map/ppermute | solution.py:406
  7.5 2.7 %collective-permute-start.9 = (f32[4,8,512]{2,1,0:T(8,128)S(1)}, f32[4,8,512]{2,1,0:T(8,128)S(1)}, u32[]{:S(2)}, u32[]{:S(2)}) collective-permute-start(f32[4,8,512]{2,1,0:T(8,128)S(1)} %get-tuple-element.48), channel_id=1, source_target_pairs={{0,240},{16,0},{32,16},{48,32},{64,48},{80,64},{96,80},{112,96},{1... | collective-permute-start | bytes 196616 | tf_op jit(solution)/shard_map/ppermute | solution.py:406
  10.2 1.1 copy.9
  11.4 3.2 %collective-permute-start.15 = (f32[48,256]{0,1:T(8,128)S(1)}, f32[48,256]{0,1:T(8,128)S(1)}, u32[]{:S(2)}, u32[]{:S(2)}) collective-permute-start(f32[48,256]{0,1:T(8,128)S(1)} %pad_dynamic-slice_fusion), channel_id=1, source_target_pairs={{0,240},{16,0},{32,16},{48,32},{64,48},{80,64},{96,80},{112,96},{1... | collective-permute-start | bytes 147464 | tf_op jit(solution)/shard_map/ppermute | solution.py:406
  18.0 2.3 %fusion.6 = (f32[8,4,8,512]{3,2,1,0:T(8,128)}, f32[8,4,8,512]{3,2,1,0:T(8,128)}) fusion(f32[8,8,8,512]{3,2,1,0:T(8,128)} %b_ref.3), kind=kLoop, calls=%fused_computation.61 | loop fusion | bytes 2097152 | tf_op jit(solution)/shard_map/slice | solution.py:437
  20.3 1.1 fusion.7
  22.3 1.3 collective-permute-start.4
  23.6 3.8 %collective-permute-start.7 = (f32[9,8,512]{2,1,0:T(8,128)S(1)}, f32[9,8,512]{2,1,0:T(8,128)S(1)}, u32[]{:S(2)}, u32[]{:S(2)}) collective-permute-start(f32[9,8,512]{2,1,0:T(8,128)S(1)} %get-tuple-element.52), channel_id=1, source_target_pairs={{0,255},{1,240},{2,241},{3,242},{4,243},{5,244},{6,245},{7,246},{8... | collective-permute-start | bytes 442376 | tf_op jit(solution)/shard_map/ppermute | solution.py:406
  27.5 2.4 %first_shares.1 = f32[9,128]{1,0:T(8,128)S(1)} custom-call(f32[8,8,8,512]{3,2,1,0:T(8,128)S(1)} %copy-done, f32[8,8,512]{2,1,0:T(8,128)S(1)} %copy-done.2, f32[4,8,512]{2,1,0:T(8,128)S(1)} %collective-permute-done.8.kxl.refs_14_, f32[4,8,512]{2,1,0:T(8,128)S(1)} %collective-permute-done.9.kxh.refs_15_, ...), custom_call_target="tpu_custom_call" | custom-call | tf_op jit(solution)/shard_map/first_shares/pallas_call | solution.py:476
  29.8 6.6 %collective-permute-start.13 = (f32[9,128]{1,0:T(8,128)S(1)}, f32[9,128]{1,0:T(8,128)S(1)}, u32[]{:S(2)}, u32[]{:S(2)}) collective-permute-start(f32[9,128]{1,0:T(8,128)S(1)} %first_shares.1), channel_id=1, source_target_pairs={{0,224},{32,0},{64,32},{96,64},{128,96},{160,128},{192,160},{224,1... | collective-permute-start | bytes 13832 | tf_op jit(solution)/shard_map/ppermute | solution.py:406
  37.2 4.0 %collective-permute-done.12 = f32[9,128]{1,0:T(8,128)S(1)} collective-permute-done((f32[9,128]{1,0:T(8,128)S(1)}, f32[9,128]{1,0:T(8,128)S(1)}, u32[]{:S(2)}, u32[]{:S(2)}) %collective-permute-start.12) | collective-permute-done | bytes 4640 | tf_op jit(solution)/shard_map/ppermute | solution.py:406
  41.2 1.5 collective-permute-start.2
  42.7 4.1 %collective-permute-start.1 = (f32[4,8,8,512]{3,2,1,0:T(8,128)}, f32[4,8,8,512]{3,2,1,0:T(8,128)}, u32[]{:S(2)}, u32[]{:S(2)}) collective-permute-start(f32[4,8,8,512]{3,2,1,0:T(8,128)} %get-tuple-element.46), channel_id=1, source_target_pairs={{0,240},{16,0},{32,16},{48,32},{64,48},{80,64},{96,80},{112,96},{1... | collective-permute-start | bytes 1572872 | tf_op jit(solution)/shard_map/ppermute | solution.py:406
  48.3 5.3 %all-to-all-start = ((f32[32,9,128]{2,1,0:T(8,128)}), f32[32,9,128]{2,1,0:T(8,128)S(1)}, u32[]{:S(2)}, u32[]{:S(2)}) async-start(f32[32,9,128]{2,1,0:T(8,128)} %pad_maximum_fusion), calls=%async_computation | async-start | bytes 524288 | tf_op jit(solution)/shard_map/all_to_all | solution.py:462
  53.6 1.9 collective-permute-start.6
  56.2 1.9 tile.4
  58.1 2.3 %copy.10.refs_20_ = f32[3,16,48,128]{3,2,1,0:T(8,128)S(1)} copy(f32[3,16,48,128]{2,3,1,0:T(8,128)} %bitcast.80) | data formatting | bytes 2359296 | tf_op jit(solution)/shard_map/tile | solution.py:496
  60.4 2.8 %collective-permute-done.6.refs_7_.refs_11_ = f32[9,8,512]{2,1,0:T(8,128)S(1)} collective-permute-done((f32[9,8,512]{2,1,0:T(8,128)S(1)}, f32[9,8,512]{2,1,0:T(8,128)S(1)}, u32[]{:S(2)}, u32[]{:S(2)}) %collective-permute-start.6) | collective-permute-done | bytes 147488 | tf_op jit(solution)/shard_map/ppermute | solution.py:406
  65.8 0.9 copy-done.7
  66.8 0.9 copy-done.10
  67.7 0.9 copy-done.13
  68.6 0.9 copy-done.16
  69.5 0.9 copy-done.22
  72.8 12.2 %first_cycle.1 = (f32[8,8,8,512]{3,2,1,0:T(8,128)S(1)}, f32[8,8,8,512]{3,2,1,0:T(8,128)S(1)}, f32[2,8,128]{2,1,0:T(8,128)S(1)}, f32[9,128]{1,0:T(8,128)S(1)}) custom-call(f32[8,8,8,512]{3,2,1,0:T(8,128)S(1)} %copy-done, f32[4,8,8,512]{3,2,1,0:T(8,128)} %collective-permute-done.refs_1_, f32[4,8,8,512]{3,2,1,0:T(8,128)} %collective-permute-done.1.refs_2_, ...), custom_call_target="tpu_custom_call" | custom-call | tf_op jit(solution)/shard_map/first_cycle/pallas_call | solution.py:509
  85.0 1.0 copy-done.18
  86.6 2.6 %collective-permute-start.25 = (f32[9,128]{1,0:T(8,128)S(1)}, f32[9,128]{1,0:T(8,128)S(1)}, u32[]{:S(2)}, u32[]{:S(2)}) collective-permute-start(f32[9,128]{1,0:T(8,128)S(1)} %get-tuple-element.10), channel_id=1, source_target_pairs={{0,224},{32,0},{64,32},{96,64},{128,96},{160,128},{192,160},{224,1... | collective-permute-start | bytes 13832 | tf_op jit(solution)/shard_map/ppermute | solution.py:406
  91.1 1.1 fusion.4
  92.2 1.1 fusion.5
  93.9 6.1 %collective-permute-start.19 = (f32[8,4,8,512]{3,2,1,0:T(8,128)}, f32[8,4,8,512]{3,2,1,0:T(8,128)}, u32[]{:S(2)}, u32[]{:S(2)}) collective-permute-start(f32[8,4,8,512]{3,2,1,0:T(8,128)} %get-tuple-element.28), channel_id=1, source_target_pairs={{0,15},{1,0},{2,1},{3,2},{4,3},{5,4},{6,5},{7,6},{8,7},{9,8},{10,9... | collective-permute-start | bytes 1572872 | tf_op jit(solution)/shard_map/ppermute | solution.py:406
  101.4 1.7 collective-permute-start.16
  103.7 1.3 broadcast_in_dim.46
  105.0 1.3 broadcast_in_dim.48
  106.3 4.9 %collective-permute-start.21 = (f32[6,8,512]{2,1,0:T(8,128)}, f32[6,8,512]{2,1,0:T(8,128)}, u32[]{:S(2)}, u32[]{:S(2)}) collective-permute-start(f32[6,8,512]{2,1,0:T(8,128)} %pad_maximum_fusion.7), channel_id=1, source_target_pairs={{0,31},{1,16},{2,17},{3,18},{4,19},{5,20},{6,21},{7,22},{8,23},{9,... | collective-permute-start | bytes 294920 | tf_op jit(solution)/shard_map/ppermute | solution.py:406
  113.4 4.5 %all-to-all-start.1 = ((f32[32,9,128]{2,1,0:T(8,128)}), f32[32,9,128]{2,1,0:T(8,128)}, u32[]{:S(2)}, u32[]{:S(2)}) async-start(f32[32,9,128]{2,1,0:T(8,128)} %pad_maximum_fusion.1), calls=%async_computation.1 | async-start | bytes 524288 | tf_op jit(solution)/shard_map/all_to_all | solution.py:462
  117.9 1.6 collective-permute-start.22
  120.4 6.9 %collective-permute-done.22.refs_7_ = f32[6,8,512]{2,1,0:T(8,128)S(1)} collective-permute-done((f32[6,8,512]{2,1,0:T(8,128)}, f32[6,8,512]{2,1,0:T(8,128)S(1)}, u32[]{:S(2)}, u32[]{:S(2)}) %collective-permute-start.22) | collective-permute-done | bytes 98336 | tf_op jit(solution)/shard_map/ppermute | solution.py:406
  127.9 2.5 %collective-permute-start.23 = (f32[6,8,512]{2,1,0:T(8,128)S(1)}, f32[6,8,512]{2,1,0:T(8,128)S(1)}, u32[]{:S(2)}, u32[]{:S(2)}) collective-permute-start(f32[6,8,512]{2,1,0:T(8,128)S(1)} %pad_maximum_fusion.9), channel_id=1, source_target_pairs={{0,255},{1,240},{2,241},{3,242},{4,243},{5,244},{6,245},{7,246},{8... | collective-permute-start | bytes 294920 | tf_op jit(solution)/shard_map/ppermute | solution.py:406
  130.4 2.6 %collective-permute-done.23.refs_8_ = f32[6,8,512]{2,1,0:T(8,128)S(1)} collective-permute-done((f32[6,8,512]{2,1,0:T(8,128)S(1)}, f32[6,8,512]{2,1,0:T(8,128)S(1)}, u32[]{:S(2)}, u32[]{:S(2)}) %collective-permute-start.23) | collective-permute-done | bytes 98336 | tf_op jit(solution)/shard_map/ppermute | solution.py:406
  134.5 0.9 copy-done.8
  135.4 0.9 copy-done.11
  136.3 0.9 copy-done.14
  143.0 11.1 %second_cycle.1 = (f32[8,8,8,512]{3,2,1,0:T(8,128)S(1)}, f32[8,8,8,512]{3,2,1,0:T(8,128)S(1)}, f32[8,128]{1,0:T(8,128)S(1)}) custom-call(f32[8,8,8,512]{3,2,1,0:T(8,128)S(1)} %get-tuple-element.9.refs_0_.q_ref, f32[4,8,8,512]{3,2,1,0:T(8,128)} %collective-permute-done.16.refs_1_, f32[4,8,8,512]{3,2,1,0:T(8,128)} %collective-permute-done.17.refs_2_, ...), custom_call_target="tpu_custom_call" | custom-call | tf_op jit(solution)/shard_map/second_cycle/pallas_call | solution.py:509
  154.1 1.0 copy-done.19
  155.1 1.0 copy-done.20
  156.1 15.0 %all_to_all.20 = f32[32,8,128]{2,1,0:T(8,128)S(1)} all-to-all(f32[32,8,128]{2,1,0:T(8,128)S(1)} %broadcast_in_dim.50), channel_id=1, replica_groups=mesh['z'=8,'core'=2,'gy'=16] {'core','gy'}, dimensions={0} | all-to-all | bytes 262144 | tf_op jit(solution)/shard_map/all_to_all | solution.py:538
  171.1 13.0 %all_to_all.21.sums_ref = f32[8,8,128]{2,1,0:T(8,128)} all-to-all(f32[8,8,128]{2,1,0:T(8,128)S(1)} %broadcast_in_dim.51), channel_id=1, replica_groups=mesh['z'=8,'core'=2,'gy'=16] {'z'}, dimensions={0} | all-to-all | bytes 65536 | tf_op jit(solution)/shard_map/all_to_all | solution.py:540
  184.1 8.0 %combine.1 = (f32[8,8,8,512]{3,2,1,0:T(8,128)}, f32[8,8,8,512]{3,2,1,0:T(8,128)}) custom-call(f32[8,8,128]{2,1,0:T(8,128)} %all_to_all.21.sums_ref, f32[8,8,8,512]{3,2,1,0:T(8,128)} %b_ref.3, f32[8,8,8,512]{3,2,1,0:T(8,128)} %copy-done.18, f32[8,8,8,512]{3,2,1,0:T(8,128)} %copy-done.1, f32[8,8,8,512]{3,2,1,0:T(8,128)} %copy-done.19, f32[8,8,8,512]{3,2,1,0:T(8,128)} %copy-done.20), custom_call_target="tpu_custom_call" | custom-call | tf_op jit(solution)/shard_map/combine/pallas_call | solution.py:542
  (141 shorter events, 29.1 us)
Async XLA Ops:
  0.6 19.7 %copy-start = (f32[8,8,8,512]{3,2,1,0:T(8,128)S(1)}, f32[8,8,8,512]{3,2,1,0:T(8,128)}, u32[]{:S(2)}) copy-start(f32[8,8,8,512]{3,2,1,0:T(8,128)} %b_ref.3) | copy-start | bytes 3145732
  0.6 21.6 %collective-permute-start.10 = (f32[8,8,512]{2,1,0:T(8,128)}, f32[8,8,512]{2,1,0:T(8,128)S(1)}, u32[]{:S(2)}, u32[]{:S(2)}) collective-permute-start(f32[8,8,512]{2,1,0:T(8,128)} %refs_13_.3), channel_id=1, source_target_pairs={{0,1},{1,2},{2,3},{3,4},{4,5},{5,6},{6,7},{7,8},{8,9},{9,10},{10,1... | collective-permute-start | bytes 393224 | tf_op jit(solution)/shard_map/ppermute | solution.py:406
  2.8 20.8 %collective-permute-start.11 = (f32[8,8,512]{2,1,0:T(8,128)}, f32[8,8,512]{2,1,0:T(8,128)S(1)}, u32[]{:S(2)}, u32[]{:S(2)}) collective-permute-start(f32[8,8,512]{2,1,0:T(8,128)} %refs_13_.3), channel_id=1, source_target_pairs={{0,15},{1,0},{2,1},{3,2},{4,3},{5,4},{6,5},{7,6},{8,7},{9,8},{10,9... | collective-permute-start | bytes 393224 | tf_op jit(solution)/shard_map/ppermute | solution.py:406
  7.5 14.7 %collective-permute-start.9 = (f32[4,8,512]{2,1,0:T(8,128)S(1)}, f32[4,8,512]{2,1,0:T(8,128)S(1)}, u32[]{:S(2)}, u32[]{:S(2)}) collective-permute-start(f32[4,8,512]{2,1,0:T(8,128)S(1)} %get-tuple-element.48), channel_id=1, source_target_pairs={{0,240},{16,0},{32,16},{48,32},{64,48},{80,64},{96,80},{112,96},{1... | collective-permute-start | bytes 196616 | tf_op jit(solution)/shard_map/ppermute | solution.py:406
  10.2 12.0 %collective-permute-start.8 = (f32[4,8,512]{2,1,0:T(8,128)S(1)}, f32[4,8,512]{2,1,0:T(8,128)S(1)}, u32[]{:S(2)}, u32[]{:S(2)}) collective-permute-start(f32[4,8,512]{2,1,0:T(8,128)S(1)} %get-tuple-element.49), channel_id=1, source_target_pairs={{0,16},{16,32},{32,48},{48,64},{64,80},{80,96},{96,112},{112,128},... | collective-permute-start | bytes 196616 | tf_op jit(solution)/shard_map/ppermute | solution.py:406
  11.4 18.4 %collective-permute-start.15 = (f32[48,256]{0,1:T(8,128)S(1)}, f32[48,256]{0,1:T(8,128)S(1)}, u32[]{:S(2)}, u32[]{:S(2)}) collective-permute-start(f32[48,256]{0,1:T(8,128)S(1)} %pad_dynamic-slice_fusion), channel_id=1, source_target_pairs={{0,240},{16,0},{32,16},{48,32},{64,48},{80,64},{96,80},{112,96},{1... | collective-permute-start | bytes 147464 | tf_op jit(solution)/shard_map/ppermute | solution.py:406
  15.5 12.0 %copy-start.2 = (f32[8,8,512]{2,1,0:T(8,128)S(1)}, f32[8,8,512]{2,1,0:T(8,128)}, u32[]{:S(2)}) copy-start(f32[8,8,512]{2,1,0:T(8,128)} %refs_13_.3) | copy-start | bytes 393220
  21.5 26.7 %copy-start.33 = (f32[4]{0:T(128)}, f32[4]{0:T(128)S(1)}, u32[]{:S(2)}) copy-start(f32[4]{0:T(128)S(1)} %add_convert_fusion.has_ref.refs_18_) | copy-start | bytes 52
  22.2 26.1 %copy-start.23 = (f32[4,8,512]{2,1,0:T(8,128)}, f32[4,8,512]{2,1,0:T(8,128)S(1)}, u32[]{:S(2)}) copy-start(f32[4,8,512]{2,1,0:T(8,128)S(1)} %collective-permute-done.9.kxh.refs_15_) | copy-start | bytes 196612
  22.2 19.0 %collective-permute-start.14 = (f32[48,256]{0,1:T(8,128)S(1)}, f32[48,256]{0,1:T(8,128)S(1)}, u32[]{:S(2)}, u32[]{:S(2)}) collective-permute-start(f32[48,256]{0,1:T(8,128)S(1)} %pad_dynamic-slice_fusion), channel_id=1, source_target_pairs={{0,16},{16,32},{32,48},{48,64},{64,80},{80,96},{96,112},{112,128},... | collective-permute-start | bytes 147464 | tf_op jit(solution)/shard_map/ppermute | solution.py:406
  22.2 26.1 %copy-start.26 = (f32[4,8,512]{2,1,0:T(8,128)}, f32[4,8,512]{2,1,0:T(8,128)S(1)}, u32[]{:S(2)}) copy-start(f32[4,8,512]{2,1,0:T(8,128)S(1)} %collective-permute-done.8.kxl.refs_14_) | copy-start | bytes 196612
  22.2 20.6 %collective-permute-start.5 = (f32[9,8,512]{2,1,0:T(8,128)S(1)}, f32[9,8,512]{2,1,0:T(8,128)S(1)}, u32[]{:S(2)}, u32[]{:S(2)}) collective-permute-start(f32[9,8,512]{2,1,0:T(8,128)S(1)} %get-tuple-element.54), channel_id=1, source_target_pairs={{0,31},{1,16},{2,17},{3,18},{4,19},{5,20},{6,21},{7,22},{8,23},{9,... | collective-permute-start | bytes 442376 | tf_op jit(solution)/shard_map/ppermute | solution.py:406
  22.3 31.3 %copy-start.12 = (f32[8,8,512]{2,1,0:T(8,128)}, f32[8,8,512]{2,1,0:T(8,128)S(1)}, u32[]{:S(2)}) copy-start(f32[8,8,512]{2,1,0:T(8,128)S(1)} %collective-permute-done.10.kyl.refs_16_) | copy-start | bytes 393220
  22.3 24.5 %collective-permute-start.4 = (f32[9,8,512]{2,1,0:T(8,128)S(1)}, f32[9,8,512]{2,1,0:T(8,128)S(1)}, u32[]{:S(2)}, u32[]{:S(2)}) collective-permute-start(f32[9,8,512]{2,1,0:T(8,128)S(1)} %get-tuple-element.55), channel_id=1, source_target_pairs={{0,17},{1,18},{2,19},{3,20},{4,21},{5,22},{6,23},{7,24},{8,25},{9,... | collective-permute-start | bytes 442376 | tf_op jit(solution)/shard_map/ppermute | solution.py:406
  23.6 30.0 %copy-start.15 = (f32[8,8,512]{2,1,0:T(8,128)}, f32[8,8,512]{2,1,0:T(8,128)S(1)}, u32[]{:S(2)}) copy-start(f32[8,8,512]{2,1,0:T(8,128)S(1)} %collective-permute-done.11.kyh.refs_17_) | copy-start | bytes 393220
  23.6 29.9 %collective-permute-start.7 = (f32[9,8,512]{2,1,0:T(8,128)S(1)}, f32[9,8,512]{2,1,0:T(8,128)S(1)}, u32[]{:S(2)}, u32[]{:S(2)}) collective-permute-start(f32[9,8,512]{2,1,0:T(8,128)S(1)} %get-tuple-element.52), channel_id=1, source_target_pairs={{0,255},{1,240},{2,241},{3,242},{4,243},{5,244},{6,245},{7,246},{8... | collective-permute-start | bytes 442376 | tf_op jit(solution)/shard_map/ppermute | solution.py:406
  29.8 7.4 %collective-permute-start.13 = (f32[9,128]{1,0:T(8,128)S(1)}, f32[9,128]{1,0:T(8,128)S(1)}, u32[]{:S(2)}, u32[]{:S(2)}) collective-permute-start(f32[9,128]{1,0:T(8,128)S(1)} %first_shares.1), channel_id=1, source_target_pairs={{0,224},{32,0},{64,32},{96,64},{128,96},{160,128},{192,160},{224,1... | collective-permute-start | bytes 13832 | tf_op jit(solution)/shard_map/ppermute | solution.py:406
  37.2 4.0 %collective-permute-start.12 = (f32[9,128]{1,0:T(8,128)S(1)}, f32[9,128]{1,0:T(8,128)S(1)}, u32[]{:S(2)}, u32[]{:S(2)}) collective-permute-start(f32[9,128]{1,0:T(8,128)S(1)} %first_shares.1), channel_id=1, source_target_pairs={{0,32},{32,64},{64,96},{96,128},{128,160},{160,192},{192,224},{224... | collective-permute-start | bytes 13832 | tf_op jit(solution)/shard_map/ppermute | solution.py:406
  41.2 23.7 %collective-permute-start.3 = (f32[8,4,8,512]{3,2,1,0:T(8,128)}, f32[8,4,8,512]{3,2,1,0:T(8,128)}, u32[]{:S(2)}, u32[]{:S(2)}) collective-permute-start(f32[8,4,8,512]{3,2,1,0:T(8,128)} %get-tuple-element.44), channel_id=1, source_target_pairs={{0,15},{1,0},{2,1},{3,2},{4,3},{5,4},{6,5},{7,6},{8,7},{9,8},{10,9... | collective-permute-start | bytes 1572872 | tf_op jit(solution)/shard_map/ppermute | solution.py:406
  41.2 23.7 %collective-permute-start.2 = (f32[8,4,8,512]{3,2,1,0:T(8,128)}, f32[8,4,8,512]{3,2,1,0:T(8,128)}, u32[]{:S(2)}, u32[]{:S(2)}) collective-permute-start(f32[8,4,8,512]{3,2,1,0:T(8,128)} %get-tuple-element.45), channel_id=1, source_target_pairs={{0,1},{1,2},{2,3},{3,4},{4,5},{5,6},{6,7},{7,8},{8,9},{9,10},{10,1... | collective-permute-start | bytes 1572872 | tf_op jit(solution)/shard_map/ppermute | solution.py:406
  42.7 22.2 %collective-permute-start.1 = (f32[4,8,8,512]{3,2,1,0:T(8,128)}, f32[4,8,8,512]{3,2,1,0:T(8,128)}, u32[]{:S(2)}, u32[]{:S(2)}) collective-permute-start(f32[4,8,8,512]{3,2,1,0:T(8,128)} %get-tuple-element.46), channel_id=1, source_target_pairs={{0,240},{16,0},{32,16},{48,32},{64,48},{80,64},{96,80},{112,96},{1... | collective-permute-start | bytes 1572872 | tf_op jit(solution)/shard_map/ppermute | solution.py:406
  47.5 17.4 %collective-permute-start = (f32[4,8,8,512]{3,2,1,0:T(8,128)}, f32[4,8,8,512]{3,2,1,0:T(8,128)}, u32[]{:S(2)}, u32[]{:S(2)}) collective-permute-start(f32[4,8,8,512]{3,2,1,0:T(8,128)} %get-tuple-element.47), channel_id=1, source_target_pairs={{0,16},{16,32},{32,48},{48,64},{64,80},{80,96},{96,112},{112,128},... | collective-permute-start | bytes 1572872 | tf_op jit(solution)/shard_map/ppermute | solution.py:406
  48.3 15.9 %all-to-all-start = ((f32[32,9,128]{2,1,0:T(8,128)}), f32[32,9,128]{2,1,0:T(8,128)S(1)}, u32[]{:S(2)}, u32[]{:S(2)}) async-start(f32[32,9,128]{2,1,0:T(8,128)} %pad_maximum_fusion), calls=%async_computation | async-start | bytes 524288 | tf_op jit(solution)/shard_map/all_to_all | solution.py:462
  53.6 6.9 %copy-start.6 = (f32[9,8,512]{2,1,0:T(8,128)}, f32[9,8,512]{2,1,0:T(8,128)S(1)}, u32[]{:S(2)}) copy-start(f32[9,8,512]{2,1,0:T(8,128)S(1)} %collective-permute-done.7.refs_8_.refs_12_) | copy-start | bytes 442372
  53.6 9.6 %collective-permute-start.6 = (f32[9,8,512]{2,1,0:T(8,128)S(1)}, f32[9,8,512]{2,1,0:T(8,128)S(1)}, u32[]{:S(2)}, u32[]{:S(2)}) collective-permute-start(f32[9,8,512]{2,1,0:T(8,128)S(1)} %get-tuple-element.53), channel_id=1, source_target_pairs={{0,241},{1,242},{2,243},{3,244},{4,245},{5,246},{6,247},{7,248},{8... | collective-permute-start | bytes 442376 | tf_op jit(solution)/shard_map/ppermute | solution.py:406
  64.9 0.9 copy-start.4
  65.8 0.9 copy-start.7
  66.8 0.9 copy-start.10
  69.5 0.9 copy-start.22
  85.0 1.0 copy-start.18
  86.6 47.0 %copy-start.1 = (f32[8,8,8,512]{3,2,1,0:T(8,128)}, f32[8,8,8,512]{3,2,1,0:T(8,128)S(1)}, u32[]{:S(2)}) copy-start(f32[8,8,8,512]{3,2,1,0:T(8,128)S(1)} %get-tuple-element.9.refs_0_.q_ref) | copy-start | bytes 3145732
  86.6 14.7 %collective-permute-start.25 = (f32[9,128]{1,0:T(8,128)S(1)}, f32[9,128]{1,0:T(8,128)S(1)}, u32[]{:S(2)}, u32[]{:S(2)}) collective-permute-start(f32[9,128]{1,0:T(8,128)S(1)} %get-tuple-element.10), channel_id=1, source_target_pairs={{0,224},{32,0},{64,32},{96,64},{128,96},{160,128},{192,160},{224,1... | collective-permute-start | bytes 13832 | tf_op jit(solution)/shard_map/ppermute | solution.py:406
  89.2 12.1 %collective-permute-start.24 = (f32[9,128]{1,0:T(8,128)S(1)}, f32[9,128]{1,0:T(8,128)S(1)}, u32[]{:S(2)}, u32[]{:S(2)}) collective-permute-start(f32[9,128]{1,0:T(8,128)S(1)} %get-tuple-element.10), channel_id=1, source_target_pairs={{0,32},{32,64},{64,96},{96,128},{128,160},{160,192},{192,224},{224... | collective-permute-start | bytes 13832 | tf_op jit(solution)/shard_map/ppermute | solution.py:406
  93.9 12.4 %collective-permute-start.20 = (f32[6,8,512]{2,1,0:T(8,128)}, f32[6,8,512]{2,1,0:T(8,128)}, u32[]{:S(2)}, u32[]{:S(2)}) collective-permute-start(f32[6,8,512]{2,1,0:T(8,128)} %pad_maximum_fusion.6), channel_id=1, source_target_pairs={{0,17},{1,18},{2,19},{3,20},{4,21},{5,22},{6,23},{7,24},{8,25},{9,... | collective-permute-start | bytes 294920 | tf_op jit(solution)/shard_map/ppermute | solution.py:406
  93.9 39.7 %collective-permute-start.19 = (f32[8,4,8,512]{3,2,1,0:T(8,128)}, f32[8,4,8,512]{3,2,1,0:T(8,128)}, u32[]{:S(2)}, u32[]{:S(2)}) collective-permute-start(f32[8,4,8,512]{3,2,1,0:T(8,128)} %get-tuple-element.28), channel_id=1, source_target_pairs={{0,15},{1,0},{2,1},{3,2},{4,3},{5,4},{6,5},{7,6},{8,7},{9,8},{10,9... | collective-permute-start | bytes 1572872 | tf_op jit(solution)/shard_map/ppermute | solution.py:406
  100.0 33.5 %collective-permute-start.18 = (f32[8,4,8,512]{3,2,1,0:T(8,128)}, f32[8,4,8,512]{3,2,1,0:T(8,128)}, u32[]{:S(2)}, u32[]{:S(2)}) collective-permute-start(f32[8,4,8,512]{3,2,1,0:T(8,128)} %get-tuple-element.29), channel_id=1, source_target_pairs={{0,1},{1,2},{2,3},{3,4},{4,5},{5,6},{6,7},{7,8},{8,9},{9,10},{10,1... | collective-permute-start | bytes 1572872 | tf_op jit(solution)/shard_map/ppermute | solution.py:406
  101.3 32.2 %collective-permute-start.17 = (f32[4,8,8,512]{3,2,1,0:T(8,128)}, f32[4,8,8,512]{3,2,1,0:T(8,128)}, u32[]{:S(2)}, u32[]{:S(2)}) collective-permute-start(f32[4,8,8,512]{3,2,1,0:T(8,128)} %get-tuple-element.30), channel_id=1, source_target_pairs={{0,240},{16,0},{32,16},{48,32},{64,48},{80,64},{96,80},{112,96},{1... | collective-permute-start | bytes 1572872 | tf_op jit(solution)/shard_map/ppermute | solution.py:406
  101.4 32.2 %collective-permute-start.16 = (f32[4,8,8,512]{3,2,1,0:T(8,128)}, f32[4,8,8,512]{3,2,1,0:T(8,128)}, u32[]{:S(2)}, u32[]{:S(2)}) collective-permute-start(f32[4,8,8,512]{3,2,1,0:T(8,128)} %get-tuple-element.31), channel_id=1, source_target_pairs={{0,16},{16,32},{32,48},{48,64},{64,80},{80,96},{96,112},{112,128},... | collective-permute-start | bytes 1572872 | tf_op jit(solution)/shard_map/ppermute | solution.py:406
  106.3 11.6 %collective-permute-start.21 = (f32[6,8,512]{2,1,0:T(8,128)}, f32[6,8,512]{2,1,0:T(8,128)}, u32[]{:S(2)}, u32[]{:S(2)}) collective-permute-start(f32[6,8,512]{2,1,0:T(8,128)} %pad_maximum_fusion.7), channel_id=1, source_target_pairs={{0,31},{1,16},{2,17},{3,18},{4,19},{5,20},{6,21},{7,22},{8,23},{9,... | collective-permute-start | bytes 294920 | tf_op jit(solution)/shard_map/ppermute | solution.py:406
  113.4 20.2 %all-to-all-start.1 = ((f32[32,9,128]{2,1,0:T(8,128)}), f32[32,9,128]{2,1,0:T(8,128)}, u32[]{:S(2)}, u32[]{:S(2)}) async-start(f32[32,9,128]{2,1,0:T(8,128)} %pad_maximum_fusion.1), calls=%async_computation.1 | async-start | bytes 524288 | tf_op jit(solution)/shard_map/all_to_all | solution.py:462
  117.9 9.4 %collective-permute-start.22 = (f32[6,8,512]{2,1,0:T(8,128)}, f32[6,8,512]{2,1,0:T(8,128)S(1)}, u32[]{:S(2)}, u32[]{:S(2)}) collective-permute-start(f32[6,8,512]{2,1,0:T(8,128)} %pad_maximum_fusion.8), channel_id=1, source_target_pairs={{0,241},{1,242},{2,243},{3,244},{4,245},{5,246},{6,247},{7,248},{8... | collective-permute-start | bytes 294920 | tf_op jit(solution)/shard_map/ppermute | solution.py:406
  127.9 5.0 %collective-permute-start.23 = (f32[6,8,512]{2,1,0:T(8,128)S(1)}, f32[6,8,512]{2,1,0:T(8,128)S(1)}, u32[]{:S(2)}, u32[]{:S(2)}) collective-permute-start(f32[6,8,512]{2,1,0:T(8,128)S(1)} %pad_maximum_fusion.9), channel_id=1, source_target_pairs={{0,255},{1,240},{2,241},{3,242},{4,243},{5,244},{6,245},{7,246},{8... | collective-permute-start | bytes 294920 | tf_op jit(solution)/shard_map/ppermute | solution.py:406
  133.6 0.9 copy-start.5
  134.5 0.9 copy-start.8
  135.4 0.9 copy-start.11
  136.3 0.9 copy-start.14
  154.1 1.0 copy-start.19
  155.1 1.0 copy-start.20
  (18 other events, 13.8 us)

commit v2 on v1

v2 whole, which is shorter than its diff:
```python
import functools

import jax
import jax.numpy as jnp
from jax import lax
from jax.experimental import pallas as pl
from jax.experimental.pallas import tpu as pltpu
from jax.sharding import Mesh
from jax.sharding import PartitionSpec as P

OMEGA = 2.0 / 3.0
THIRD = 1.0 / 3.0
L = 128
CH = 4
HALO = 4
GX = ("z", "core")
SLAB2 = ("core", "gy")
ALL = ("z", "core", "gy")
HIGHEST = lax.Precision.HIGHEST
WHOLE = pltpu.CompilerParams(vmem_limit_bytes=(64 << 20) - (64 << 10))
GRANT = pltpu.CompilerParams(vmem_limit_bytes=(63 << 20) + (256 << 10))


def lanes():
    return lax.broadcasted_iota(jnp.int32, (8, L), 1)


def ld(ref, x, y):
    return [ref[x, y, :, k * L : (k + 1) * L] for k in range(CH)]


def row(ref, x, y):
    return [jnp.broadcast_to(ref[x, pl.ds(y, 1), k * L : (k + 1) * L], (8, L)) for k in range(CH)]


def put(ref, x, y, values):
    for k in range(CH):
        ref[x, y, :, k * L : (k + 1) * L] = values[k]


def zsum(v, lane):
    up = [pltpu.roll(c, 1, 1) for c in v]
    down = [pltpu.roll(c, L - 1, 1) for c in v]
    out = []
    for k in range(CH):
        before = up[k - 1] if k > 0 else jnp.zeros_like(up[0])
        after = down[k + 1] if k < CH - 1 else jnp.zeros_like(up[0])
        out.append(jnp.where(lane == 0, before, up[k]) + jnp.where(lane == L - 1, after, down[k]))
    return out


def add(*terms):
    return [functools.reduce(lambda a, b: a + b, t) for t in zip(*terms)]


def mul(a, b):
    return [p * q for p, q in zip(a, b)]


def scale(s, a):
    return [s * p for p in a]


def join(v):
    return jnp.concatenate(v, axis=1)


def beside_rows(ref, x, lo, hi, lane):
    prev, here = ld(ref, x, lo - 1), ld(ref, x, lo)
    for y in range(lo, hi):
        after = ld(ref, x, y + 1)
        near = add(prev, after, ld(ref, x - 1, y), ld(ref, x + 1, y), zsum(here, lane))
        yield y, here, near
        prev, here = here, after


def shares(h_ref, source, g_own, g_faces, rows_ref):
    lane = lanes()
    zero = [jnp.zeros((8, L), jnp.float32)] * CH

    def one_row(i, carry):
        a1, ylo, yhi = carry
        total = zero
        for y, here, near in beside_rows(h_ref, i + 1, 1, 9, lane):
            j = y - 1
            t1 = add(scale(THIRD, source(i, j)), near)
            s = mul(g_own(i, j), t1)
            a1 = add(a1, t1)
            total = add(total, s)
            if j == 0:
                ylo = add(ylo, s)
            if j == 7:
                yhi = add(yhi, s)
        for k in range(CH):
            rows_ref[i, :, k * L : (k + 1) * L] = total[k]
        return a1, ylo, yhi

    a1, ylo, yhi = lax.fori_loop(0, 8, one_row, (zero, zero, zero))
    rows = [[rows_ref[i, :, k * L : (k + 1) * L] for k in range(CH)] for i in range(8)]
    s_all = add(*rows)
    edges = (rows[0], rows[7], ylo, yhi)
    faces = []
    for f, (cells, edge) in enumerate(
        zip(
            (
                [(1, j + 1) for j in range(8)],
                [(8, j + 1) for j in range(8)],
                [(i + 1, 1) for i in range(8)],
                [(i + 1, 8) for i in range(8)],
            ),
            edges,
        )
    ):
        t_sum, s_sum = zero, zero
        for n, (x, y) in enumerate(cells):
            t = ld(h_ref, x, y)
            s = mul(g_faces(f, n), t)
            t_sum, s_sum = add(t_sum, t), add(s_sum, s)
            if n == 0:
                first = s
            if n == 7:
                last = s
        part = add(
            scale(THIRD, t_sum),
            edge,
            scale(3.0, s_sum),
            scale(-1.0, add(first, last)),
            zsum(s_sum, lane),
        )
        faces.append((part, s_sum, first, last))
    (xl, sxl, xl0, xl7), (xh, sxh, xh0, xh7), (yl, syl, yl0, yl7), (yh, syh, yh0, yh7) = faces
    own = add(
        scale(THIRD, a1),
        scale(4.0, s_all),
        scale(-1.0, add(*edges)),
        sxl,
        sxh,
        syl,
        syh,
        zsum(s_all, lane),
    )
    parts = [
        add(xl0, yl0),
        xl,
        add(xl7, yh0),
        yl,
        own,
        yh,
        add(xh0, yl7),
        xh,
        add(xh7, yh7),
    ]
    stacked = jnp.concatenate([join(p) for p in parts], axis=0)
    zi = lax.broadcasted_iota(jnp.int32, (CH * L, L), 0)
    li = lax.broadcasted_iota(jnp.int32, (CH * L, L), 1)
    fold = jnp.where((zi // 32) == (li % 16), 1.0 / 2048.0, 0.0)
    sums = jnp.dot(stacked, fold, precision=HIGHEST, preferred_element_type=jnp.float32)
    r = lax.broadcasted_iota(jnp.int32, (8, L), 0)
    keep = (lane // 16) == r
    out = [
        jnp.sum(jnp.where(keep, sums[8 * n : 8 * n + 8], 0.0), axis=0, keepdims=True)
        for n in range(9)
    ]
    return jnp.concatenate(out, axis=0)


def fill_border(ref):
    zero = jnp.zeros((8, CH * L), jnp.float32)

    def one(i, carry):
        ref[0, i] = zero
        ref[9, i] = zero
        ref[i, 0] = zero
        ref[i, 9] = zero
        return carry

    lax.fori_loop(0, 10, one, 0)


def first_shares_kernel(n_gx, n_gy, b_hbm, kap_hbm, kxl_hbm, kxh_hbm, kyl_hbm, kyh_hbm, out_ref, *refs):
    h_ref, g_ref, gf_ref, rows_ref, b_ref, KX, KY, sems = refs
    copies = run_copies(
        [
            (kyl_hbm, KY.at[0]),
            (kap_hbm, KY.at[1]),
            (kyh_hbm, KY.at[2]),
            (kxl_hbm.at[7], KX.at[0]),
            (kxh_hbm.at[0], KX.at[1]),
            (b_hbm, b_ref),
        ],
        sems,
    )
    has_x, has_y = place(n_gx, n_gy)
    fill_border(h_ref)
    for copy in copies:
        copy.wait()

    def one_row(i, carry):
        g_ref[i] = OMEGA / (6.0 + KY[1, i])
        gf_ref[2, pl.ds(i, 1)] = OMEGA / (6.0 + KY[0, i, 7:8]) * has_y[0]
        gf_ref[3, pl.ds(i, 1)] = OMEGA / (6.0 + KY[2, i, 0:1]) * has_y[2]
        for j in range(8):
            put(h_ref, i + 1, j + 1, mul(row(g_ref, i, j), ld(b_ref, i, j)))
        return carry

    lax.fori_loop(0, 8, one_row, 0)
    gf_ref[0] = OMEGA / (6.0 + KX[0]) * has_x[0]
    gf_ref[1] = OMEGA / (6.0 + KX[1]) * has_x[2]
    out_ref[...] = shares(
        h_ref,
        lambda i, j: ld(b_ref, i, j),
        lambda i, j: row(g_ref, i, j),
        lambda f, n: row(gf_ref, f, n),
        rows_ref,
    )


def coarse_values(recv_ref, inv_ref, c_ref, count, valid):
    lane = lanes()
    r = lax.broadcasted_iota(jnp.int32, (8, L), 0)
    keep = (lane // 16) == r
    pieces = []
    for t in range(3):
        for j in range(count):
            value = None
            for dy in (-1, 0, 1):
                if not 0 <= j - dy < count:
                    continue
                for c in range(2):
                    term = recv_ref[c * count + j - dy, pl.ds(t * 3 + dy + 1, 1), :]
                    value = term if value is None else value + term
            pieces.append(jnp.where(keep, jnp.broadcast_to(value, (8, L)), 0.0))
    i0 = lax.broadcasted_iota(jnp.int32, (L, L), 0)
    i1 = lax.broadcasted_iota(jnp.int32, (L, L), 1)
    fold = jnp.where((i0 % 16) == (i1 % 16), 1.0, 0.0)
    spread = jnp.dot(
        jnp.concatenate(pieces, axis=0), fold, precision=HIGHEST, preferred_element_type=jnp.float32
    )
    for t in range(3):
        values = []
        for part in range(0, count, 8):
            out = jnp.zeros((8, L), jnp.float32)
            for j in range(part, min(part + 8, count)):
                at = (t * count + j) * 8
                out = jnp.where((lane // 16) == j - part, spread[at : at + 8], out)
            values.append(out)
        d = jnp.concatenate(values, axis=1)[:, : count * 16]
        c = lax.dot_general(
            d,
            inv_ref[t],
            (((1,), (1,)), ((), ())),
            precision=HIGHEST,
            preferred_element_type=jnp.float32,
        )
        for jj in range(3):
            for k in range(CH):
                out = jnp.zeros((8, L), jnp.float32)
                for q in range(4):
                    m = jj * 16 + k * 4 + q
                    out = jnp.where((lane // 32) == q, jnp.broadcast_to(c[:, m : m + 1], (8, L)), out)
                c_ref[t * 3 + jj, :, k * L : (k + 1) * L] = out * (valid[0][t] * valid[1][jj])


def place(n_gx, n_gy):
    gx = lax.axis_index("z") * 2 + lax.axis_index("core")
    gy = lax.axis_index("gy")

    def flag(condition):
        return jnp.where(condition, 1.0, 0.0).astype(jnp.float32)

    one = jnp.float32(1.0)
    return (flag(gx > 0), one, flag(gx < n_gx - 1)), (flag(gy > 0), one, flag(gy < n_gy - 1))


def run_copies(pairs, sems, base=0):
    copies = []
    for n, (src, dst) in enumerate(pairs):
        copy = pltpu.make_async_copy(src, dst, sems.at[base + n])
        copy.start()
        copies.append(copy)
    return copies


def pack_kernel(n_gy, cells, inverse, to_high, to_low, m_high, m_low, b_ref, inv_ref, in_sems, sems):
    gy = lax.axis_index("gy")
    inv = []
    for n in range(6):
        block = jnp.clip(gy - 1 + n // 2, 0, n_gy - 1) * 16 + (n % 2) * 8
        half = (n % 2) * 256
        inv.append(
            (inverse.at[pl.ds(pl.multiple_of(block, 8), 8)], inv_ref.at[n // 2, :, half : half + 256])
        )
    for copy in run_copies([(cells, b_ref)] + inv, in_sems):
        copy.wait()
    pairs = []
    for x in range(8):
        pairs.append((b_ref.at[8 * x + 4 : 8 * x + 8], to_high.at[x]))
        pairs.append((b_ref.at[8 * x : 8 * x + 4], to_low.at[x]))
    for start, m in ((32, m_high), (0, m_low)):
        pairs.append((b_ref.at[start : start + 32], m.at[0:CELLS]))
        pairs.append((inv_ref, m.at[INV_AT:LAST]))
    for copy in run_copies(pairs, sems):
        copy.wait()


def pass_kernel(*refs):
    pass


CELLS, LOW_AT, HIGH_AT, KAPPA_AT, INV_AT, LAST = 32, 32, 38, 44, 50, 53


def corner_segments():
    at = 0
    for a in (1, 2, 3):
        yield a, at, 4 - a
        at += 4 - a


def merge_kernel(first, n_z, n_gy, own_ref, low_ref, high_ref, y_low, y_high, m_high, m_low, *refs):
    if first:
        kyl, kyh = refs[:2]
        refs = refs[2:]
    out_ref, to_high, to_low, high_part, low_part, sems = refs
    pairs = []
    for up, m in ((True, high_part), (False, low_part)):
        for a, at, wide in corner_segments():
            x = 8 - a if up else a - 1
            pairs.append((y_low.at[x * 4 + 4 - wide : x * 4 + 4], m.at[at : at + wide]))
            pairs.append((y_high.at[x * 4 : x * 4 + wide], m.at[6 + at : 6 + at + wide]))
        if first:
            x = 5 if up else 0
            pairs.append((kyl.at[x : x + 3], m.at[12:15]))
            pairs.append((kyh.at[x : x + 3], m.at[15:18]))
    copies = run_copies(pairs, sems)
    z, core = lax.axis_index("z"), lax.axis_index("core")
    below = jnp.where(z > 0, 1.0, 0.0).astype(jnp.float32)
    above = jnp.where(z < n_z - 1, 1.0, 0.0).astype(jnp.float32)
    own = [own_ref[3 * t : 3 * t + 3] for t in range(3)]
    low = [low_ref[3 * t : 3 * t + 3] * below for t in range(3)]
    high = [high_ref[3 * t : 3 * t + 3] * above for t in range(3)]
    even = [own[0] + low[2], own[1], own[2] + high[0], high[1]]
    odd = [low[1], own[0] + low[2], own[1], own[2] + high[0]]
    slabs = [jnp.where(core == 0, e, o) for e, o in zip(even, odd)]
    for t in range(3):
        for n in range(n_gy):
            out_ref[n, 3 * t : 3 * t + 3] = slabs[t]
            out_ref[n_gy + n, 3 * t : 3 * t + 3] = slabs[t + 1]
    for copy in copies:
        copy.wait()
    end = INV_AT if first else KAPPA_AT
    for copy in run_copies([(high_part, to_high.at[CELLS:end]), (low_part, to_low.at[CELLS:end])], sems):
        copy.wait()


def cycle_kernel(first, n_gx, n_gy, *refs):
    f_own, f_yl, f_yh, f_xl, f_xh, b_xl, b_xh = refs[:7]
    kap_ref, kxl, kxh, kyl, kyh, recv_hbm, c_own = refs[7:14]
    refs = refs[14:]
    if first:
        z_out, q_out, dots_ref, out_ref = refs[:4]
        sends = refs[4:8]
        refs = refs[8:]
    else:
        extra_hbm, earlier_ref, z_out, q_out, dots_ref = refs[:5]
        refs = refs[5:]
    F, A, B, G, KC, KX, KY, inv_ref, c_ref, h_ref, gf_ref, rows_ref, z_ref, q_ref, recv_ref, extra_ref, sems = refs
    has_x, has_y = place(n_gx, n_gy)
    gy = lax.axis_index("gy")

    pairs = [(recv_hbm, recv_ref)]
    for jj in range(3):
        block = jnp.clip(gy - 1 + jj, 0, n_gy - 1)
        pairs.append(
            (c_own.at[pl.ds(pl.multiple_of(block * 16, 16), 16)], inv_ref.at[1, jj * 16 : jj * 16 + 16])
        )
    for t, ref in ((0, b_xl), (2, b_xh)):
        for n in range(6):
            half = (n % 2) * 256
            pairs.append((ref.at[INV_AT + n // 2, :, half : half + 256], inv_ref.at[t, n * 8 : n * 8 + 8]))
    n_inv = len(pairs)
    pairs += [
        (b_xl.at[KAPPA_AT : KAPPA_AT + 6], KC.at[0]),
        (b_xh.at[KAPPA_AT : KAPPA_AT + 6], KC.at[1]),
        (kap_ref, KY.at[1]),
        (kyl, KY.at[0]),
        (kyh, KY.at[2]),
        (kxl.at[4:8], KX.at[0]),
        (kxh.at[0:4], KX.at[1]),
    ]
    n_kappa = len(pairs)
    pairs += [
        (f_own, F.at[4:12, 4:12]),
        (f_yl, F.at[4:12, 0:4]),
        (f_yh, F.at[4:12, 12:16]),
    ]
    for low, ref in ((True, f_xl), (False, f_xh)):
        for i in range(4):
            pairs.append((ref.at[8 * i : 8 * i + 8], F.at[i if low else 12 + i, 4:12]))
        for a, at, wide in corner_segments():
            x = 4 - a if low else 11 + a
            pairs.append((ref.at[LOW_AT + at : LOW_AT + at + wide], F.at[x, 4 - wide : 4]))
            pairs.append((ref.at[HIGH_AT + at : HIGH_AT + at + wide], F.at[x, 12 : 12 + wide]))
    n_field = len(pairs)
    if not first:
        pairs.append((extra_hbm, extra_ref))
    copies = run_copies(pairs, sems)

    zero = jnp.zeros((8, CH * L), jnp.float32)
    for x, y in [(a, b) for a in range(4) for b in range(4) if (4 - a) + (4 - b) > 4]:
        for xx, yy in ((x, y), (x, 15 - y), (15 - x, y), (15 - x, 15 - y)):
            F[xx, yy] = zero

    def inv_diag(kappa):
        return OMEGA / (6.0 + kappa)

    for copy in copies[:n_inv]:
        copy.wait()
    coarse_values(recv_ref, inv_ref, c_ref, n_gy, (has_x, has_y))

    for copy in copies[n_inv:n_kappa]:
        copy.wait()
    for i in range(8):
        G[4 + i, 8:16] = inv_diag(KY[1, i])
        G[4 + i, 0:8] = inv_diag(KY[0, i]) * has_y[0]
        G[4 + i, 16:24] = inv_diag(KY[2, i]) * has_y[2]
    for a in range(4):
        G[a, 8:16] = inv_diag(KX[0, a]) * has_x[0]
        G[12 + a, 8:16] = inv_diag(KX[1, a]) * has_x[2]
    for side, sx in ((0, -1), (1, 1)):
        for half, sy in ((0, -1), (1, 1)):
            mask = has_x[1 + sx] * has_y[1 + sy]
            y = 0 if sy < 0 else 16
            G[0 if sx < 0 else 15, y : y + 8] = zero
            for i in range(3):
                G[1 + i if sx < 0 else 12 + i, y : y + 8] = inv_diag(KC[side, 3 * half + i]) * mask
    for copy in copies[n_kappa:n_field]:
        copy.wait()

    lane = lanes()

    def start_row(x, carry):
        for y in range(16):
            put(A, x, y, mul(row(G, x, y + 4), ld(F, x, y)))
        return carry

    lax.fori_loop(0, 16, start_row, 0)

    def sweep(src, dst, edge, coarse):
        def one_row(x, carry):
            t = jnp.where(x >= 4, 1, 0) + jnp.where(x >= 12, 1, 0)
            for y, here, near in beside_rows(src, x, edge, 16 - edge, lane):
                new = add(scale(THIRD, here), mul(add(ld(F, x, y), near), row(G, x, y + 4)))
                if coarse:
                    jj = (1 if y >= 4 else 0) + (1 if y >= 12 else 0)
                    new = add(new, [c_ref[t * 3 + jj, :, k * L : (k + 1) * L] for k in range(CH)])
                put(dst, x, y, new)
            return carry

        lax.fori_loop(edge, 16 - edge, one_row, 0, unroll=2)

    sweep(A, B, 1, True)
    sweep(B, A, 2, False)
    sweep(A, B, 3, False)
    for copy in copies[n_field:]:
        copy.wait()
    if first:
        fill_border(h_ref)
    nil = jnp.zeros((8, L), jnp.float32)

    def image_row(i, carry):
        fz, zq, ez = carry
        x = i + 4
        for y, here, near in beside_rows(B, x, 4, 12, lane):
            j = y - 4
            kappa = row(KY.at[1], i, j)
            image = [(6.0 + kappa[k]) * here[k] - near[k] for k in range(CH)]
            put(z_ref, i, j, here)
            put(q_ref, i, j, image)
            source = ld(F, x, y)
            fz = functools.reduce(lambda a, b: a + b, mul(source, here), fz)
            zq = functools.reduce(lambda a, b: a + b, mul(here, image), zq)
            if first:
                put(h_ref, i + 1, j + 1, mul(row(G, x, y + 4), image))
            else:
                ez = functools.reduce(lambda a, b: a + b, mul(ld(extra_ref, i, j), here), ez)
        return fz, zq, ez

    fz, zq, ez = lax.fori_loop(0, 8, image_row, (nil, nil, nil))
    if first:
        dots_ref[0] = fz
        dots_ref[1] = zq
        copies = run_copies(
            [
                (q_ref.at[0:8, 4:8], sends[0]),
                (q_ref.at[0:8, 0:4], sends[1]),
            ]
            + [(q_ref.at[4 + i], sends[2].at[8 * i : 8 * i + 8]) for i in range(4)]
            + [(q_ref.at[i], sends[3].at[8 * i : 8 * i + 8]) for i in range(4)]
            + [
                (q_ref, q_out),
                (z_ref, z_out),
            ],
            sems,
        )
        gf_ref[0] = G[3, 8:16]
        gf_ref[1] = G[12, 8:16]
        for i in range(8):
            gf_ref[2, pl.ds(i, 1)] = G[4 + i, 7:8]
            gf_ref[3, pl.ds(i, 1)] = G[4 + i, 16:17]
        out_ref[...] = shares(
            h_ref,
            lambda i, j: ld(q_ref, i, j),
            lambda i, j: row(G, i + 4, j + 8),
            lambda f, n: row(gf_ref, f, n),
            rows_ref,
        )
        for copy in copies:
            copy.wait()
    else:
        copies = run_copies([(z_ref, z_out), (q_ref, q_out)], sems)
        total = [earlier_ref[0], earlier_ref[1], fz, zq, ez]
        packed = nil
        for k, part in enumerate(total):
            packed = jnp.where(lane == k, jnp.sum(part, axis=1, keepdims=True), packed)
        for n in range(2 * n_gy):
            dots_ref[n] = packed
        for copy in copies:
            copy.wait()


def combine_kernel(sums_ref, *refs):
    sources, outs = refs[:5], refs[5:7]
    b_ref, z_ref, q_ref, w_ref, v_ref = refs[7:12]
    x_keep, r_keep, in_sems, sems = refs[12:]
    fetched = [
        run_copies(
            [(src.at[2 * i : 2 * i + 2], dst.at[2 * i : 2 * i + 2]) for src, dst in zip(sources, refs[7:12])],
            in_sems,
            5 * i,
        )
        for i in range(4)
    ]
    sums = sums_ref[0]
    for n in range(1, sums_ref.shape[0]):
        sums = sums + sums_ref[n]
    bz, zq, qw, wv, bw = (sums[:, k : k + 1] for k in range(5))
    a0 = bz / zq
    e1 = bz - a0 * (bw + zq) + a0 * a0 * qw
    beta = e1 / bz
    z1q = zq - a0 * qw
    z1v = zq - 2.0 * a0 * qw + a0 * a0 * wv
    a1 = e1 / (z1v + 2.0 * beta * z1q + beta * beta * zq)
    cz = jnp.broadcast_to(a0 + a1 * (1.0 + beta), (8, CH * L))
    cw = jnp.broadcast_to(a1 * a0, (8, CH * L))
    copies = []
    for n in range(4):
        for copy in fetched[n]:
            copy.wait()
        for i in (2 * n, 2 * n + 1):
            for j in range(8):
                x_keep[i, j] = cz * z_ref[i, j] - cw * w_ref[i, j]
                r_keep[i, j] = b_ref[i, j] - cz * q_ref[i, j] + cw * v_ref[i, j]
        part = slice(2 * n, 2 * n + 2)
        copies += run_copies([(x_keep.at[part], outs[0].at[part]), (r_keep.at[part], outs[1].at[part])], sems, 2 * n)
    for copy in copies:
        copy.wait()


def shift(value, axes, sizes, steps):
    pairs = []
    total = 1
    for n in sizes:
        total *= n
    for flat in range(total):
        rest, target = flat, 0
        weight = 1
        for n, step in zip(reversed(sizes), reversed(steps)):
            at = rest % n
            rest //= n
            target += ((at + step) % n) * weight
            weight *= n
        pairs.append((flat, target))
    return lax.ppermute(value, axes, pairs)


VM = pl.BlockSpec(memory_space=pltpu.VMEM)
HB = pl.BlockSpec(memory_space=pl.ANY)


def solution(mesh):
    n_gx, n_gy = mesh.shape["gx"], mesh.shape["gy"]
    n_z = n_gx // 2
    fine = Mesh(mesh.devices.reshape(n_z, 2, n_gy), ALL)

    f32 = jnp.float32

    def shape(*dims):
        return jax.ShapeDtypeStruct(dims, f32)

    tile = shape(8, 8, 8, CH * L)
    y_face = shape(8, 4, 8, CH * L)

    def along_gy(faces):
        return [shift(faces[0], ("gy",), (n_gy,), (1,)), shift(faces[1], ("gy",), (n_gy,), (-1,))]

    def exchange(own, faces, messages, more):
        low = shift(own, ("z",), (n_z,), (1,))
        high = shift(own, ("z",), (n_z,), (-1,))
        size = INV_AT if more else KAPPA_AT
        part = pltpu.VMEM((size - CELLS, 8, CH * L), f32)
        out, to_high, to_low = pl.pallas_call(
            functools.partial(merge_kernel, bool(more), n_z, n_gy),
            out_shape=[shape(2 * n_gy, 9, L)] + [shape(*m.shape) for m in messages],
            in_specs=[VM] * 3 + [HB] * (4 + len(more)),
            out_specs=[VM, HB, HB],
            input_output_aliases={5: 1, 6: 2},
            scratch_shapes=[part, part, pltpu.SemaphoreType.DMA((20,))],
            compiler_params=GRANT,
            name="merge_shares",
        )(own, low, high, *(f.reshape(32, 8, CH * L) for f in faces), *messages, *more)
        from_low = shift(to_high, GX, (n_gx,), (1,))
        from_high = shift(to_low, GX, (n_gx,), (-1,))
        return lax.all_to_all(out, SLAB2, 0, 0), [from_low, from_high]

    def body(b, kappa, inverse):
        around = [
            shift(kappa, GX, (n_gx,), (1,)),
            shift(kappa, GX, (n_gx,), (-1,)),
            shift(kappa, ("gy",), (n_gy,), (1,)),
            shift(kappa, ("gy",), (n_gy,), (-1,)),
        ]
        packed = pl.pallas_call(
            functools.partial(pack_kernel, n_gy),
            out_shape=[y_face, y_face] + [shape(LAST, 8, CH * L)] * 2,
            in_specs=[HB, HB],
            out_specs=[HB] * 4,
            scratch_shapes=[
                pltpu.VMEM((64, 8, CH * L), f32),
                pltpu.VMEM((3, 8, CH * L), f32),
                pltpu.SemaphoreType.DMA((7,)),
                pltpu.SemaphoreType.DMA((20,)),
            ],
            compiler_params=WHOLE,
            name="pack_faces",
        )(b.reshape(64, 8, CH * L), inverse)
        behind = pl.pallas_call(
            pass_kernel,
            out_shape=[y_face, y_face],
            in_specs=[HB] * 6,
            out_specs=[HB] * 2,
            input_output_aliases={4: 0, 5: 1},
            compiler_params=WHOLE,
            name="pass_faces",
        )(*around, packed[0], packed[1])
        b_faces = along_gy(behind)
        own = pl.pallas_call(
            functools.partial(first_shares_kernel, n_gx, n_gy),
            out_shape=shape(9, L),
            in_specs=[HB] * 6,
            out_specs=VM,
            scratch_shapes=[
                pltpu.VMEM((10, 10, 8, CH * L), f32),
                pltpu.VMEM((8, 8, CH * L), f32),
                pltpu.VMEM((4, 8, CH * L), f32),
                pltpu.VMEM((8, 8, CH * L), f32),
                pltpu.VMEM((8, 8, 8, CH * L), f32),
                pltpu.VMEM((2, 8, CH * L), f32),
                pltpu.VMEM((3, 8, 8, CH * L), f32),
                pltpu.SemaphoreType.DMA((6,)),
            ],
            compiler_params=GRANT,
            name="first_shares",
        )(b, kappa, *around)

        def cycle(first, field, faces, messages, b_messages, received, more):
            outs = [tile, tile]
            out_specs = [HB, HB, VM]
            if first:
                outs += [shape(2, 8, L), shape(9, L), y_face, y_face]
                outs += [shape(KAPPA_AT, 8, CH * L)] * 2
                out_specs += [VM, HB, HB, HB, HB]
            else:
                outs += [shape(2 * n_gy, 8, L)]
            big = pltpu.VMEM((16, 16, 8, CH * L), f32)
            own_tile = pltpu.VMEM((8, 8, 8, CH * L), f32)
            return pl.pallas_call(
                functools.partial(cycle_kernel, first, n_gx, n_gy),
                out_shape=outs,
                in_specs=[HB] * 14 + ([HB, VM] if more else []),
                out_specs=out_specs,
                scratch_shapes=[
                    big,
                    big,
                    big,
                    pltpu.VMEM((16, 24, CH * L), f32),
                    pltpu.VMEM((2, 6, 8, CH * L), f32),
                    pltpu.VMEM((2, 4, 8, CH * L), f32),
                    pltpu.VMEM((3, 8, 8, CH * L), f32),
                    pltpu.VMEM((3, 48, 16 * n_gy), f32),
                    pltpu.VMEM((9, 8, CH * L), f32),
                    pltpu.VMEM((10, 10, 8, CH * L), f32),
                    pltpu.VMEM((4, 8, CH * L), f32),
                    pltpu.VMEM((8, 8, CH * L), f32),
                    own_tile,
                    own_tile,
                    pltpu.VMEM((2 * n_gy, 9, L), f32),
                    own_tile,
                    pltpu.SemaphoreType.DMA((52,)),
                ],
                compiler_params=GRANT,
                name="first_cycle" if first else "second_cycle",
            )(field, *faces, *messages, *b_messages, kappa, *around, received, inverse, *more)

        received, b_messages = exchange(own, b_faces, packed[2:], around[2:])
        z0, q0, dots, own, *sends = cycle(True, b, b_faces, b_messages, b_messages, received, [])
        q_faces = along_gy(sends[:2])
        received, messages = exchange(own, q_faces, sends[2:], [])
        w0, v0, packed = cycle(False, q0, q_faces, messages, b_messages, received, [b, dots])

        near_sum = jnp.sum(lax.all_to_all(packed, SLAB2, 0, 0), axis=0)
        sums = lax.all_to_all(jnp.broadcast_to(near_sum, (n_z, 8, L)), "z", 0, 0)
        return pl.pallas_call(
            combine_kernel,
            out_shape=[tile, tile],
            in_specs=[VM] + [HB] * 5,
            out_specs=[HB, HB],
            scratch_shapes=[pltpu.VMEM((8, 8, 8, CH * L), f32)] * 7
            + [pltpu.SemaphoreType.DMA((20,)), pltpu.SemaphoreType.DMA((8,))],
            compiler_params=GRANT,
            name="combine",
        )(sums, b, z0, q0, w0, v0)

    field = P(GX, "gy", None, None)
    return jax.shard_map(
        body,
        mesh=fine,
        in_specs=(field, P(GX, "gy", None), P(GX, None)),
        out_specs=(field, field),
        check_vma=False,
    )
```

time: 194 us -> 150 us (0.77)
  local copies, waits for them, and re-layouts: 46.4 us -> 2.44 us
  starting transfers between devices: 60.5 us -> 31.4 us
  blocking collectives: 28 us -> 57 us
  Pallas kernels: 33.7 us -> 42.1 us
  other arithmetic: 5.77 us -> 0.04 us
    all_to_all x1 -> x3, blocking collectives: 15 us -> 44.9 us  [the longest x2 32.7 us: exchange(): return (lax.all_to_all(out, SLAB2, 0, 0), [from_low, from_high])]
    unnamed x77 -> x14, local copies, waits for them, and re-layouts: 25.1 us -> 2.44 us
    ppermute x26 -> x16, starting transfers between devices: 50.7 us -> 31.4 us  [shift(): return lax.ppermute(value, axes, pairs)]
    all_to_all x2 -> x0, starting transfers between devices: 9.81 us -> none  [gather_shares(): return lax.all_to_all(jnp.concatenate([to_even, to_odd]), SLAB2, 0, 0)]
    slice x9 -> x0, local copies, waits for them, and re-layouts: 8.5 us -> none  [the longest x2 3.38 us: halo(): yh = shift(field[:, 0:4], ('gy',), (n_gy,), (-1,))]
    pallas_call x4 -> x8, Pallas kernels: 33.7 us -> 42.1 us  [the longest x2 24.2 us: cycle(): pl.pallas_call(functools.partial(cycle_kernel, first, n_gx, n_gy), out_sh...]
    squeeze x6 -> x0, local copies, waits for them, and re-layouts: 4.35 us -> none  [corner_cells(): pieces.append(field[x, y:y + wide])]
    concatenate x8 -> x0, other arithmetic: 4.25 us -> none  [the longest x6 2.82 us: corners(): packed = jnp.concatenate(pieces, axis=0)]
  transfers between devices with their start and end apart: 28 -> 16, of which waited for: 6 -> 6; matrix products, arithmetic and copies ran while one was open for 15% -> 0% of each run, Pallas kernels for 1% -> 4%
where the time goes in v2:
time: 150 us
  blocking collectives  57 us (38%)
  Pallas kernels  42.1 us (28%)
  starting transfers between devices  31.4 us (21%)
  waiting for transfers between devices  15.6 us (10%)
  local copies, waits for them, and re-layouts  2.44 us (2%)
    all_to_all x2, blocking collectives, exchange(): return (lax.all_to_all(out, SLAB2, 0, 0), [from_low, from_high])  32.7 us
    ppermute x16, starting transfers between devices, shift(): return lax.ppermute(value, axes, pairs)  31.4 us
    pallas_call x2, Pallas kernels, cycle(): pl.pallas_call(functools.partial(cycle_kernel, first, n_gx, n_gy), out_sh...  24.2 us
    ppermute x16, waiting for transfers between devices, shift(): return lax.ppermute(value, axes, pairs)  15.6 us
    all_to_all x1, blocking collectives, body(): near_sum = jnp.sum(lax.all_to_all(packed, SLAB2, 0, 0), axis=0)  12.2 us
    all_to_all x1, blocking collectives, body(): sums = lax.all_to_all(jnp.broadcast_to(near_sum, (n_z, 8, L)), 'z', 0, 0)  12.1 us
    pallas_call x2, Pallas kernels, exchange(): pl.pallas_call(functools.partial(merge_kernel, bool(more), n_z, n_gy), ou...  6.77 us
    pallas_call x1, Pallas kernels, body(): pl.pallas_call(combine_kernel, out_shape=[tile, tile], in_specs=[VM] + [H...  4.53 us
  transfers between devices with their start and end apart: 16, of which 6 were waited for; matrix products, arithmetic and copies ran while one was open for 0% of the time, Pallas kernels for 4%

profile of v2, /device:TPU:1, one launch (start us, length us, event | category | flops | bytes accessed | tf_op | source)
XLA Modules:
  0.0 149.6 jit_solution(18286514331691157917)
XLA Ops:
  0.6 5.8 %collective-permute-start.3 = (f32[8,8,512]{2,1,0:T(8,128)}, f32[8,8,512]{2,1,0:T(8,128)}, u32[]{:S(2)}, u32[]{:S(2)}) collective-permute-start(f32[8,8,512]{2,1,0:T(8,128)} %refs_7_.3), channel_id=1, source_target_pairs={{0,15},{1,0},{2,1},{3,2},{4,3},{5,4},{6,5},{7,6},{8,7},{9,8},{10,9... | collective-permute-start | bytes 393224 | tf_op jit(solution)/shard_map/ppermute | solution.py:584
  6.5 0.0 collective-permute-start.2
  6.5 1.0 collective-permute-start.1
  7.4 1.5 %collective-permute-start = (f32[8,8,512]{2,1,0:T(8,128)}, f32[8,8,512]{2,1,0:T(8,128)}, u32[]{:S(2)}, u32[]{:S(2)}) collective-permute-start(f32[8,8,512]{2,1,0:T(8,128)} %refs_7_.3), channel_id=1, source_target_pairs={{0,16},{16,32},{32,48},{48,64},{64,80},{80,96},{96,112},{112,128},... | collective-permute-start | bytes 393224 | tf_op jit(solution)/shard_map/ppermute | solution.py:584
  8.9 2.8 %pack_faces.1 = (f32[8,4,8,512]{3,2,1,0:T(8,128)}, f32[8,4,8,512]{3,2,1,0:T(8,128)}, f32[53,8,512]{2,1,0:T(8,128)}, f32[53,8,512]{2,1,0:T(8,128)}) custom-call(f32[64,8,512]{2,1,0:T(8,128)} %bitcast.5, f32[256,256]{1,0:T(8,128)} %refs_13_.3), custom_call_target="tpu_custom_call" | custom-call | tf_op jit(solution)/shard_map/pack_faces/pallas_call | solution.py:633
  11.7 0.0 collective-permute-done.3.refs_3_.kyh_hbm.refs_1_.refs_11_
  11.8 2.2 %collective-permute-done.2.refs_2_.kyl_hbm.refs_0_.refs_10_ = f32[8,8,512]{2,1,0:T(8,128)} collective-permute-done((f32[8,8,512]{2,1,0:T(8,128)}, f32[8,8,512]{2,1,0:T(8,128)}, u32[]{:S(2)}, u32[]{:S(2)}) %collective-permute-start.2) | collective-permute-done | bytes 131104 | tf_op jit(solution)/shard_map/ppermute | solution.py:584
  13.9 0.0 collective-permute-done.1.refs_1_.kxh_hbm.refs_9_
  13.9 0.0 collective-permute-done.refs_0_.kxl_hbm.refs_8_
  13.9 0.1 collective-permute-start.4
  14.0 4.8 %collective-permute-start.5 = (f32[8,4,8,512]{3,2,1,0:T(8,128)}, f32[8,4,8,512]{3,2,1,0:T(8,128)}, u32[]{:S(2)}, u32[]{:S(2)}) collective-permute-start(f32[8,4,8,512]{3,2,1,0:T(8,128)} %get-tuple-element.28), channel_id=1, source_target_pairs={{0,15},{1,0},{2,1},{3,2},{4,3},{5,4},{6,5},{7,6},{8,7},{9,8},{10,9... | collective-permute-start | bytes 1572872 | tf_op jit(solution)/shard_map/ppermute | solution.py:584
  18.8 3.9 %first_shares.1.own_ref = f32[9,128]{1,0:T(8,128)} custom-call(f32[8,8,8,512]{3,2,1,0:T(8,128)} %refs_0_.3, f32[8,8,512]{2,1,0:T(8,128)} %refs_7_.3, f32[8,8,512]{2,1,0:T(8,128)} %collective-permute-done.refs_0_.kxl_hbm.refs_8_, f32[8,8,512]{2,1,0:T(8,128)} %collective-permute-done.1.refs_1_.kxh_hbm.refs_9_, ...), custom_call_target="tpu_custom_call" | custom-call | tf_op jit(solution)/shard_map/first_shares/pallas_call | solution.py:657
  22.7 5.7 %collective-permute-start.7 = (f32[9,128]{1,0:T(8,128)}, f32[9,128]{1,0:T(8,128)S(1)}, u32[]{:S(2)}, u32[]{:S(2)}) collective-permute-start(f32[9,128]{1,0:T(8,128)} %first_shares.1.own_ref), channel_id=1, source_target_pairs={{0,224},{32,0},{64,32},{96,64},{128,96},{160,128},{192,160},{224,1... | collective-permute-start | bytes 13832 | tf_op jit(solution)/shard_map/ppermute | solution.py:584
  28.3 0.0 collective-permute-start.6
  28.3 1.0 collective-permute-done.7.high_ref
  29.3 2.9 %collective-permute-done.6.low_ref = f32[9,128]{1,0:T(8,128)S(1)} collective-permute-done((f32[9,128]{1,0:T(8,128)}, f32[9,128]{1,0:T(8,128)S(1)}, u32[]{:S(2)}, u32[]{:S(2)}) %collective-permute-start.6) | collective-permute-done | bytes 4640 | tf_op jit(solution)/shard_map/ppermute | solution.py:584
  32.2 0.0 collective-permute-done.4.refs_1_
  32.2 0.0 collective-permute-done.5.refs_2_
  32.2 0.0 copy-done.3
  32.3 0.6 copy-done.5
  32.8 0.2 copy-done.1
  33.0 3.5 %merge_shares.2 = (f32[32,9,128]{2,1,0:T(8,128)}, f32[53,8,512]{2,1,0:T(8,128)}, f32[53,8,512]{2,1,0:T(8,128)}) custom-call(f32[9,128]{1,0:T(8,128)} %first_shares.1.own_ref, f32[9,128]{1,0:T(8,128)} %copy-done.5, f32[9,128]{1,0:T(8,128)} %copy-done.3, f32[32,8,512]{2,1,0:T(8,128)} %bitcast.7, ...), custom_call_target="tpu_custom_call", output_to_operand_aliasing={{1}: (5, {}), {2}: (6, {})} | custom-call | tf_op jit(solution)/shard_map/merge_shares/pallas_call | solution.py:612
  36.5 2.5 %collective-permute-start.8 = (f32[53,8,512]{2,1,0:T(8,128)}, f32[53,8,512]{2,1,0:T(8,128)}, u32[]{:S(2)}, u32[]{:S(2)}) collective-permute-start(f32[53,8,512]{2,1,0:T(8,128)} %get-tuple-element.31), channel_id=1, source_target_pairs={{0,16},{16,32},{32,48},{48,64},{64,80},{80,96},{96,112},{112,128},... | collective-permute-start | bytes 2605064 | tf_op jit(solution)/shard_map/ppermute | solution.py:584
  39.1 1.6 %collective-permute-start.9 = (f32[53,8,512]{2,1,0:T(8,128)}, f32[53,8,512]{2,1,0:T(8,128)}, u32[]{:S(2)}, u32[]{:S(2)}) collective-permute-start(f32[53,8,512]{2,1,0:T(8,128)} %get-tuple-element.32), channel_id=1, source_target_pairs={{0,240},{16,0},{32,16},{48,32},{64,48},{80,64},{96,80},{112,96},{1... | collective-permute-start | bytes 2605064 | tf_op jit(solution)/shard_map/ppermute | solution.py:584
  40.7 15.5 %all_to_all.20.refs_12_ = f32[32,9,128]{2,1,0:T(8,128)} all-to-all(f32[32,9,128]{2,1,0:T(8,128)} %get-tuple-element.33), channel_id=1, replica_groups=mesh['z'=8,'core'=2,'gy'=16] {'core','gy'}, dimensions={0} | all-to-all | bytes 294912 | tf_op jit(solution)/shard_map/all_to_all | solution.py:624
  56.2 0.0 collective-permute-done.8.refs_3_.refs_5_
  56.2 0.0 collective-permute-done.9.refs_4_.refs_6_
  56.2 12.2 %first_cycle.1 = (f32[8,8,8,512]{3,2,1,0:T(8,128)}, f32[8,8,8,512]{3,2,1,0:T(8,128)}, f32[2,8,128]{2,1,0:T(8,128)}, f32[9,128]{1,0:T(8,128)}, f32[8,4,8,512]{3,2...) custom-call(f32[8,8,8,512]{3,2,1,0:T(8,128)} %refs_0_.3, ...), custom_call_target="tpu_custom_call" | custom-call | tf_op jit(solution)/shard_map/first_cycle/pallas_call | solution.py:687
  68.4 0.2 collective-permute-start.10
  68.6 4.7 %collective-permute-start.11 = (f32[8,4,8,512]{3,2,1,0:T(8,128)}, f32[8,4,8,512]{3,2,1,0:T(8,128)}, u32[]{:S(2)}, u32[]{:S(2)}) collective-permute-start(f32[8,4,8,512]{3,2,1,0:T(8,128)} %get-tuple-element.36), channel_id=1, source_target_pairs={{0,15},{1,0},{2,1},{3,2},{4,3},{5,4},{6,5},{7,6},{8,7},{9,8},{10,9... | collective-permute-start | bytes 1572872 | tf_op jit(solution)/shard_map/ppermute | solution.py:584
  73.3 1.5 %collective-permute-start.13 = (f32[9,128]{1,0:T(8,128)}, f32[9,128]{1,0:T(8,128)S(1)}, u32[]{:S(2)}, u32[]{:S(2)}) collective-permute-start(f32[9,128]{1,0:T(8,128)} %get-tuple-element.37.own_ref), channel_id=1, source_target_pairs={{0,224},{32,0},{64,32},{96,64},{128,96},{160,128},{192,160},{224,1... | collective-permute-start | bytes 13832 | tf_op jit(solution)/shard_map/ppermute | solution.py:584
  74.8 0.0 collective-permute-start.12
  74.8 1.6 %collective-permute-done.13.high_ref = f32[9,128]{1,0:T(8,128)S(1)} collective-permute-done((f32[9,128]{1,0:T(8,128)}, f32[9,128]{1,0:T(8,128)S(1)}, u32[]{:S(2)}, u32[]{:S(2)}) %collective-permute-start.13) | collective-permute-done | bytes 4640 | tf_op jit(solution)/shard_map/ppermute | solution.py:584
  76.4 2.6 %collective-permute-done.12.low_ref = f32[9,128]{1,0:T(8,128)S(1)} collective-permute-done((f32[9,128]{1,0:T(8,128)}, f32[9,128]{1,0:T(8,128)S(1)}, u32[]{:S(2)}, u32[]{:S(2)}) %collective-permute-start.12) | collective-permute-done | bytes 4640 | tf_op jit(solution)/shard_map/ppermute | solution.py:584
  79.0 5.3 %collective-permute-done.10.refs_1_ = f32[8,4,8,512]{3,2,1,0:T(8,128)S(1)} collective-permute-done((f32[8,4,8,512]{3,2,1,0:T(8,128)}, f32[8,4,8,512]{3,2,1,0:T(8,128)S(1)}, u32[]{:S(2)}, u32[]{:S(2)}) %collective-permute-start.10) | collective-permute-done | bytes 524320 | tf_op jit(solution)/shard_map/ppermute | solution.py:584
  84.3 0.0 collective-permute-done.11.refs_2_
  84.3 0.8 copy-done
  85.1 3.3 %merge_shares.3 = (f32[32,9,128]{2,1,0:T(8,128)}, f32[44,8,512]{2,1,0:T(8,128)}, f32[44,8,512]{2,1,0:T(8,128)}) custom-call(f32[9,128]{1,0:T(8,128)} %get-tuple-element.37.own_ref, f32[9,128]{1,0:T(8,128)} %copy-done.6, f32[9,128]{1,0:T(8,128)} %copy-done.4, f32[32,8,512]{2,1,0:T(8,128)} %bitcast.6, ...), custom_call_target="tpu_custom_call", output_to_operand_aliasing={{1}: (5, {}), {2}: (6, {})} | custom-call | tf_op jit(solution)/shard_map/merge_shares/pallas_call | solution.py:612
  88.4 0.0 collective-permute-start.14
  88.4 2.1 %collective-permute-start.15 = (f32[44,8,512]{2,1,0:T(8,128)}, f32[44,8,512]{2,1,0:T(8,128)}, u32[]{:S(2)}, u32[]{:S(2)}) collective-permute-start(f32[44,8,512]{2,1,0:T(8,128)} %get-tuple-element.41), channel_id=1, source_target_pairs={{0,240},{16,0},{32,16},{48,32},{64,48},{80,64},{96,80},{112,96},{1... | collective-permute-start | bytes 2162696 | tf_op jit(solution)/shard_map/ppermute | solution.py:584
  90.5 17.1 %all_to_all.21.refs_12_ = f32[32,9,128]{2,1,0:T(8,128)} all-to-all(f32[32,9,128]{2,1,0:T(8,128)} %get-tuple-element.42), channel_id=1, replica_groups=mesh['z'=8,'core'=2,'gy'=16] {'core','gy'}, dimensions={0} | all-to-all | bytes 294912 | tf_op jit(solution)/shard_map/all_to_all | solution.py:624
  107.6 0.0 collective-permute-done.14.refs_3_
  107.6 0.0 collective-permute-done.15.refs_4_
  107.6 0.9 copy-done.2
  108.5 12.0 %second_cycle.1 = (f32[8,8,8,512]{3,2,1,0:T(8,128)}, f32[8,8,8,512]{3,2,1,0:T(8,128)}, f32[32,8,128]{2,1,0:T(8,128)}) custom-call(f32[8,8,8,512]{3,2,1,0:T(8,128)} %get-tuple-element.34.refs_0_.refs_2_, f32[8,4,8,512]{3,2,1,0:T(8,128)} %copy-done, f32[8,4,8,512]{3,2,1,0:T(8,128)} %collective-permute-done.11.refs_2_, f32[44,8,512]{2,1,0:T(8,128)} %copy-done.2, ...), custom_call_target="tpu_custom_call" | custom-call | tf_op jit(solution)/shard_map/second_cycle/pallas_call | solution.py:687
  120.5 12.2 %all_to_all.22 = f32[32,8,128]{2,1,0:T(8,128)S(1)} all-to-all(f32[32,8,128]{2,1,0:T(8,128)} %get-tuple-element.44), channel_id=1, replica_groups=mesh['z'=8,'core'=2,'gy'=16] {'core','gy'}, dimensions={0} | all-to-all | bytes 262144 | tf_op jit(solution)/shard_map/all_to_all | solution.py:721
  132.8 12.1 %all_to_all.23.sums_ref = f32[8,8,128]{2,1,0:T(8,128)} all-to-all(f32[8,8,128]{2,1,0:T(8,128)S(1)} %broadcast_in_dim.3), channel_id=1, replica_groups=mesh['z'=8,'core'=2,'gy'=16] {'z'}, dimensions={0} | all-to-all | bytes 65536 | tf_op jit(solution)/shard_map/all_to_all | solution.py:722
  144.9 4.5 %combine.1 = (f32[8,8,8,512]{3,2,1,0:T(8,128)}, f32[8,8,8,512]{3,2,1,0:T(8,128)}) custom-call(f32[8,8,128]{2,1,0:T(8,128)} %all_to_all.23.sums_ref, f32[8,8,8,512]{3,2,1,0:T(8,128)} %refs_0_.3, f32[8,8,8,512]{3,2,1,0:T(8,128)} %get-tuple-element.45.refs_1_, f32[8,8,8,512]{3,2,1,0:T(8,128)} %get-tuple-element.34.refs_0_.refs_2_, ...), custom_call_target="tpu_custom_call" | custom-call | tf_op jit(solution)/shard_map/combine/pallas_call | solution.py:723
  (12 shorter events, 0.1 us)
Async XLA Ops:
  0.6 11.1 %collective-permute-start.3 = (f32[8,8,512]{2,1,0:T(8,128)}, f32[8,8,512]{2,1,0:T(8,128)}, u32[]{:S(2)}, u32[]{:S(2)}) collective-permute-start(f32[8,8,512]{2,1,0:T(8,128)} %refs_7_.3), channel_id=1, source_target_pairs={{0,15},{1,0},{2,1},{3,2},{4,3},{5,4},{6,5},{7,6},{8,7},{9,8},{10,9... | collective-permute-start | bytes 393224 | tf_op jit(solution)/shard_map/ppermute | solution.py:584
  6.5 7.5 %collective-permute-start.2 = (f32[8,8,512]{2,1,0:T(8,128)}, f32[8,8,512]{2,1,0:T(8,128)}, u32[]{:S(2)}, u32[]{:S(2)}) collective-permute-start(f32[8,8,512]{2,1,0:T(8,128)} %refs_7_.3), channel_id=1, source_target_pairs={{0,1},{1,2},{2,3},{3,4},{4,5},{5,6},{6,7},{7,8},{8,9},{9,10},{10,1... | collective-permute-start | bytes 393224 | tf_op jit(solution)/shard_map/ppermute | solution.py:584
  6.5 7.5 %collective-permute-start.1 = (f32[8,8,512]{2,1,0:T(8,128)}, f32[8,8,512]{2,1,0:T(8,128)}, u32[]{:S(2)}, u32[]{:S(2)}) collective-permute-start(f32[8,8,512]{2,1,0:T(8,128)} %refs_7_.3), channel_id=1, source_target_pairs={{0,240},{16,0},{32,16},{48,32},{64,48},{80,64},{96,80},{112,96},{1... | collective-permute-start | bytes 393224 | tf_op jit(solution)/shard_map/ppermute | solution.py:584
  7.4 6.5 %collective-permute-start = (f32[8,8,512]{2,1,0:T(8,128)}, f32[8,8,512]{2,1,0:T(8,128)}, u32[]{:S(2)}, u32[]{:S(2)}) collective-permute-start(f32[8,8,512]{2,1,0:T(8,128)} %refs_7_.3), channel_id=1, source_target_pairs={{0,16},{16,32},{32,48},{48,64},{64,80},{80,96},{96,112},{112,128},... | collective-permute-start | bytes 393224 | tf_op jit(solution)/shard_map/ppermute | solution.py:584
  13.9 18.3 %collective-permute-start.4 = (f32[8,4,8,512]{3,2,1,0:T(8,128)}, f32[8,4,8,512]{3,2,1,0:T(8,128)S(1)}, u32[]{:S(2)}, u32[]{:S(2)}) collective-permute-start(f32[8,4,8,512]{3,2,1,0:T(8,128)} %get-tuple-element.27), channel_id=1, source_target_pairs={{0,1},{1,2},{2,3},{3,4},{4,5},{5,6},{6,7},{7,8},{8,9},{9,10},{10,1... | collective-permute-start | bytes 1572872 | tf_op jit(solution)/shard_map/ppermute | solution.py:584
  14.0 18.2 %collective-permute-start.5 = (f32[8,4,8,512]{3,2,1,0:T(8,128)}, f32[8,4,8,512]{3,2,1,0:T(8,128)}, u32[]{:S(2)}, u32[]{:S(2)}) collective-permute-start(f32[8,4,8,512]{3,2,1,0:T(8,128)} %get-tuple-element.28), channel_id=1, source_target_pairs={{0,15},{1,0},{2,1},{3,2},{4,3},{5,4},{6,5},{7,6},{8,7},{9,8},{10,9... | collective-permute-start | bytes 1572872 | tf_op jit(solution)/shard_map/ppermute | solution.py:584
  22.7 6.7 %collective-permute-start.7 = (f32[9,128]{1,0:T(8,128)}, f32[9,128]{1,0:T(8,128)S(1)}, u32[]{:S(2)}, u32[]{:S(2)}) collective-permute-start(f32[9,128]{1,0:T(8,128)} %first_shares.1.own_ref), channel_id=1, source_target_pairs={{0,224},{32,0},{64,32},{96,64},{128,96},{160,128},{192,160},{224,1... | collective-permute-start | bytes 13832 | tf_op jit(solution)/shard_map/ppermute | solution.py:584
  28.3 3.9 %collective-permute-start.6 = (f32[9,128]{1,0:T(8,128)}, f32[9,128]{1,0:T(8,128)S(1)}, u32[]{:S(2)}, u32[]{:S(2)}) collective-permute-start(f32[9,128]{1,0:T(8,128)} %first_shares.1.own_ref), channel_id=1, source_target_pairs={{0,32},{32,64},{64,96},{96,128},{128,160},{160,192},{192,224},{224... | collective-permute-start | bytes 13832 | tf_op jit(solution)/shard_map/ppermute | solution.py:584
  29.3 2.9 %copy-start.3 = (f32[9,128]{1,0:T(8,128)}, f32[9,128]{1,0:T(8,128)S(1)}, u32[]{:S(2)}) copy-start(f32[9,128]{1,0:T(8,128)S(1)} %collective-permute-done.7.high_ref) | copy-start | bytes 13828
  32.2 0.6 copy-start.5
  32.2 0.8 copy-start.1
  36.5 19.7 %collective-permute-start.8 = (f32[53,8,512]{2,1,0:T(8,128)}, f32[53,8,512]{2,1,0:T(8,128)}, u32[]{:S(2)}, u32[]{:S(2)}) collective-permute-start(f32[53,8,512]{2,1,0:T(8,128)} %get-tuple-element.31), channel_id=1, source_target_pairs={{0,16},{16,32},{32,48},{48,64},{64,80},{80,96},{96,112},{112,128},... | collective-permute-start | bytes 2605064 | tf_op jit(solution)/shard_map/ppermute | solution.py:584
  39.1 17.1 %collective-permute-start.9 = (f32[53,8,512]{2,1,0:T(8,128)}, f32[53,8,512]{2,1,0:T(8,128)}, u32[]{:S(2)}, u32[]{:S(2)}) collective-permute-start(f32[53,8,512]{2,1,0:T(8,128)} %get-tuple-element.32), channel_id=1, source_target_pairs={{0,240},{16,0},{32,16},{48,32},{64,48},{80,64},{96,80},{112,96},{1... | collective-permute-start | bytes 2605064 | tf_op jit(solution)/shard_map/ppermute | solution.py:584
  68.4 15.9 %collective-permute-start.10 = (f32[8,4,8,512]{3,2,1,0:T(8,128)}, f32[8,4,8,512]{3,2,1,0:T(8,128)S(1)}, u32[]{:S(2)}, u32[]{:S(2)}) collective-permute-start(f32[8,4,8,512]{3,2,1,0:T(8,128)} %get-tuple-element.35), channel_id=1, source_target_pairs={{0,1},{1,2},{2,3},{3,4},{4,5},{5,6},{6,7},{7,8},{8,9},{9,10},{10,1... | collective-permute-start | bytes 1572872 | tf_op jit(solution)/shard_map/ppermute | solution.py:584
  68.6 15.7 %collective-permute-start.11 = (f32[8,4,8,512]{3,2,1,0:T(8,128)}, f32[8,4,8,512]{3,2,1,0:T(8,128)}, u32[]{:S(2)}, u32[]{:S(2)}) collective-permute-start(f32[8,4,8,512]{3,2,1,0:T(8,128)} %get-tuple-element.36), channel_id=1, source_target_pairs={{0,15},{1,0},{2,1},{3,2},{4,3},{5,4},{6,5},{7,6},{8,7},{9,8},{10,9... | collective-permute-start | bytes 1572872 | tf_op jit(solution)/shard_map/ppermute | solution.py:584
  73.3 3.1 %collective-permute-start.13 = (f32[9,128]{1,0:T(8,128)}, f32[9,128]{1,0:T(8,128)S(1)}, u32[]{:S(2)}, u32[]{:S(2)}) collective-permute-start(f32[9,128]{1,0:T(8,128)} %get-tuple-element.37.own_ref), channel_id=1, source_target_pairs={{0,224},{32,0},{64,32},{96,64},{128,96},{160,128},{192,160},{224,1... | collective-permute-start | bytes 13832 | tf_op jit(solution)/shard_map/ppermute | solution.py:584
  74.8 4.2 %collective-permute-start.12 = (f32[9,128]{1,0:T(8,128)}, f32[9,128]{1,0:T(8,128)S(1)}, u32[]{:S(2)}, u32[]{:S(2)}) collective-permute-start(f32[9,128]{1,0:T(8,128)} %get-tuple-element.37.own_ref), channel_id=1, source_target_pairs={{0,32},{32,64},{64,96},{96,128},{128,160},{160,192},{192,224},{224... | collective-permute-start | bytes 13832 | tf_op jit(solution)/shard_map/ppermute | solution.py:584
  76.4 7.9 %copy-start.4 = (f32[9,128]{1,0:T(8,128)}, f32[9,128]{1,0:T(8,128)S(1)}, u32[]{:S(2)}) copy-start(f32[9,128]{1,0:T(8,128)S(1)} %collective-permute-done.13.high_ref) | copy-start | bytes 13828
  79.0 5.3 %copy-start.6 = (f32[9,128]{1,0:T(8,128)}, f32[9,128]{1,0:T(8,128)S(1)}, u32[]{:S(2)}) copy-start(f32[9,128]{1,0:T(8,128)S(1)} %collective-permute-done.12.low_ref) | copy-start | bytes 13828
  84.3 0.8 copy-start
  88.4 19.2 %collective-permute-start.14 = (f32[44,8,512]{2,1,0:T(8,128)}, f32[44,8,512]{2,1,0:T(8,128)S(1)}, u32[]{:S(2)}, u32[]{:S(2)}) collective-permute-start(f32[44,8,512]{2,1,0:T(8,128)} %get-tuple-element.40), channel_id=1, source_target_pairs={{0,16},{16,32},{32,48},{48,64},{64,80},{80,96},{96,112},{112,128},... | collective-permute-start | bytes 2162696 | tf_op jit(solution)/shard_map/ppermute | solution.py:584
  88.4 19.2 %collective-permute-start.15 = (f32[44,8,512]{2,1,0:T(8,128)}, f32[44,8,512]{2,1,0:T(8,128)}, u32[]{:S(2)}, u32[]{:S(2)}) collective-permute-start(f32[44,8,512]{2,1,0:T(8,128)} %get-tuple-element.41), channel_id=1, source_target_pairs={{0,240},{16,0},{32,16},{48,32},{64,48},{80,64},{96,80},{112,96},{1... | collective-permute-start | bytes 2162696 | tf_op jit(solution)/shard_map/ppermute | solution.py:584
  107.6 0.9 copy-start.2

commit v3 on v2

--- a/solution.py
+++ b/solution.py
@@ -186,13 +186,13 @@
             (kyh_hbm, KY.at[2]),
             (kxl_hbm.at[7], KX.at[0]),
             (kxh_hbm.at[0], KX.at[1]),
-            (b_hbm, b_ref),
-        ],
+        ]
+        + [(b_hbm.at[2 * i : 2 * i + 2], b_ref.at[2 * i : 2 * i + 2]) for i in range(4)],
         sems,
     )
     has_x, has_y = place(n_gx, n_gy)
     fill_border(h_ref)
-    for copy in copies:
+    for copy in copies[:5]:
         copy.wait()
 
     def one_row(i, carry):
@@ -203,7 +203,9 @@
             put(h_ref, i + 1, j + 1, mul(row(g_ref, i, j), ld(b_ref, i, j)))
         return carry
 
-    lax.fori_loop(0, 8, one_row, 0)
+    for n in range(4):
+        copies[5 + n].wait()
+        lax.fori_loop(2 * n, 2 * n + 2, one_row, 0)
     gf_ref[0] = OMEGA / (6.0 + KX[0]) * has_x[0]
     gf_ref[1] = OMEGA / (6.0 + KX[1]) * has_x[2]
     out_ref[...] = shares(
@@ -227,7 +229,7 @@
                 if not 0 <= j - dy < count:
                     continue
                 for c in range(2):
-                    term = recv_ref[c * count + j - dy, pl.ds(t * 3 + dy + 1, 1), :]
+                    term = recv_ref[c * count + j - dy, t * 3 + dy + 1]
                     value = term if value is None else value + term
             pieces.append(jnp.where(keep, jnp.broadcast_to(value, (8, L)), 0.0))
     i0 = lax.broadcasted_iota(jnp.int32, (L, L), 0)
@@ -307,7 +309,8 @@
     pass
 
 
-CELLS, LOW_AT, HIGH_AT, KAPPA_AT, INV_AT, LAST = 32, 32, 38, 44, 50, 53
+CELLS, INV_AT, LAST = 32, 32, 35
+HIGH_AT, KAPPA_AT, CORNERS = 6, 12, 18
 
 
 def corner_segments():
@@ -317,7 +320,7 @@
         at += 4 - a
 
 
-def merge_kernel(first, n_z, n_gy, own_ref, low_ref, high_ref, y_low, y_high, m_high, m_low, *refs):
+def merge_kernel(first, n_z, n_gy, own_ref, low_ref, high_ref, y_low, y_high, *refs):
     if first:
         kyl, kyh = refs[:2]
         refs = refs[2:]
@@ -327,36 +330,38 @@
         for a, at, wide in corner_segments():
             x = 8 - a if up else a - 1
             pairs.append((y_low.at[x * 4 + 4 - wide : x * 4 + 4], m.at[at : at + wide]))
-            pairs.append((y_high.at[x * 4 : x * 4 + wide], m.at[6 + at : 6 + at + wide]))
+            pairs.append((y_high.at[x * 4 : x * 4 + wide], m.at[HIGH_AT + at : HIGH_AT + at + wide]))
         if first:
             x = 5 if up else 0
-            pairs.append((kyl.at[x : x + 3], m.at[12:15]))
-            pairs.append((kyh.at[x : x + 3], m.at[15:18]))
+            pairs.append((kyl.at[x : x + 3], m.at[KAPPA_AT : KAPPA_AT + 3]))
+            pairs.append((kyh.at[x : x + 3], m.at[KAPPA_AT + 3 : KAPPA_AT + 6]))
     copies = run_copies(pairs, sems)
     z, core = lax.axis_index("z"), lax.axis_index("core")
     below = jnp.where(z > 0, 1.0, 0.0).astype(jnp.float32)
     above = jnp.where(z < n_z - 1, 1.0, 0.0).astype(jnp.float32)
-    own = [own_ref[3 * t : 3 * t + 3] for t in range(3)]
-    low = [low_ref[3 * t : 3 * t + 3] * below for t in range(3)]
-    high = [high_ref[3 * t : 3 * t + 3] * above for t in range(3)]
-    even = [own[0] + low[2], own[1], own[2] + high[0], high[1]]
-    odd = [low[1], own[0] + low[2], own[1], own[2] + high[0]]
-    slabs = [jnp.where(core == 0, e, o) for e, o in zip(even, odd)]
+    own = [own_ref[n : n + 1] for n in range(9)]
+    low = [low_ref[n : n + 1] * below for n in range(9)]
+    high = [high_ref[n : n + 1] * above for n in range(9)]
+    slabs = []
+    for dy in range(3):
+        even = [own[dy] + low[6 + dy], own[3 + dy], own[6 + dy] + high[dy], high[3 + dy]]
+        odd = [low[3 + dy], own[dy] + low[6 + dy], own[3 + dy], own[6 + dy] + high[dy]]
+        slabs.append([jnp.where(core == 0, e, o) for e, o in zip(even, odd)])
     for t in range(3):
-        for n in range(n_gy):
-            out_ref[n, 3 * t : 3 * t + 3] = slabs[t]
-            out_ref[n_gy + n, 3 * t : 3 * t + 3] = slabs[t + 1]
+        for dy in range(3):
+            for n in range(n_gy):
+                out_ref[n, 3 * t + dy] = slabs[dy][t]
+                out_ref[n_gy + n, 3 * t + dy] = slabs[dy][t + 1]
     for copy in copies:
         copy.wait()
-    end = INV_AT if first else KAPPA_AT
-    for copy in run_copies([(high_part, to_high.at[CELLS:end]), (low_part, to_low.at[CELLS:end])], sems):
+    for copy in run_copies([(high_part, to_high), (low_part, to_low)], sems):
         copy.wait()
 
 
 def cycle_kernel(first, n_gx, n_gy, *refs):
-    f_own, f_yl, f_yh, f_xl, f_xh, b_xl, b_xh = refs[:7]
-    kap_ref, kxl, kxh, kyl, kyh, recv_hbm, c_own = refs[7:14]
-    refs = refs[14:]
+    f_own, f_yl, f_yh, f_xl, f_xh, f_cl, f_ch, b_xl, b_xh, b_cl, b_ch = refs[:11]
+    kap_ref, kxl, kxh, kyl, kyh, recv_hbm, c_own = refs[11:18]
+    refs = refs[18:]
     if first:
         z_out, q_out, dots_ref, out_ref = refs[:4]
         sends = refs[4:8]
@@ -380,8 +385,8 @@
             pairs.append((ref.at[INV_AT + n // 2, :, half : half + 256], inv_ref.at[t, n * 8 : n * 8 + 8]))
     n_inv = len(pairs)
     pairs += [
-        (b_xl.at[KAPPA_AT : KAPPA_AT + 6], KC.at[0]),
-        (b_xh.at[KAPPA_AT : KAPPA_AT + 6], KC.at[1]),
+        (b_cl.at[KAPPA_AT:CORNERS], KC.at[0]),
+        (b_ch.at[KAPPA_AT:CORNERS], KC.at[1]),
         (kap_ref, KY.at[1]),
         (kyl, KY.at[0]),
         (kyh, KY.at[2]),
@@ -394,13 +399,13 @@
         (f_yl, F.at[4:12, 0:4]),
         (f_yh, F.at[4:12, 12:16]),
     ]
-    for low, ref in ((True, f_xl), (False, f_xh)):
+    for low, ref, corner in ((True, f_xl, f_cl), (False, f_xh, f_ch)):
         for i in range(4):
             pairs.append((ref.at[8 * i : 8 * i + 8], F.at[i if low else 12 + i, 4:12]))
         for a, at, wide in corner_segments():
             x = 4 - a if low else 11 + a
-            pairs.append((ref.at[LOW_AT + at : LOW_AT + at + wide], F.at[x, 4 - wide : 4]))
-            pairs.append((ref.at[HIGH_AT + at : HIGH_AT + at + wide], F.at[x, 12 : 12 + wide]))
+            pairs.append((corner.at[at : at + wide], F.at[x, 4 - wide : 4]))
+            pairs.append((corner.at[HIGH_AT + at : HIGH_AT + at + wide], F.at[x, 12 : 12 + wide]))
     n_field = len(pairs)
     if not first:
         pairs.append((extra_hbm, extra_ref))
@@ -446,22 +451,28 @@
 
     lax.fori_loop(0, 16, start_row, 0)
 
-    def sweep(src, dst, edge, coarse):
-        def one_row(x, carry):
+    def sweep(src, dst, width, coarse):
+        def one_row(x, reach):
             t = jnp.where(x >= 4, 1, 0) + jnp.where(x >= 12, 1, 0)
-            for y, here, near in beside_rows(src, x, edge, 16 - edge, lane):
+            for y, here, near in beside_rows(src, x, 4 - reach, 12 + reach, lane):
                 new = add(scale(THIRD, here), mul(add(ld(F, x, y), near), row(G, x, y + 4)))
                 if coarse:
                     jj = (1 if y >= 4 else 0) + (1 if y >= 12 else 0)
                     new = add(new, [c_ref[t * 3 + jj, :, k * L : (k + 1) * L] for k in range(CH)])
                 put(dst, x, y, new)
+
+        def inner(x, carry):
+            one_row(x, width)
             return carry
 
-        lax.fori_loop(edge, 16 - edge, one_row, 0, unroll=2)
-
-    sweep(A, B, 1, True)
+        for a in range(1, width + 1):
+            one_row(4 - a, width - a)
+            one_row(11 + a, width - a)
+        lax.fori_loop(4, 12, inner, 0, unroll=2)
+
+    sweep(A, B, 3, True)
     sweep(B, A, 2, False)
-    sweep(A, B, 3, False)
+    sweep(A, B, 1, False)
     for copy in copies[n_field:]:
         copy.wait()
     if first:
@@ -521,8 +532,10 @@
         copies = run_copies([(z_ref, z_out), (q_ref, q_out)], sems)
         total = [earlier_ref[0], earlier_ref[1], fz, zq, ez]
         packed = nil
+        sub = lax.broadcasted_iota(jnp.int32, (8, L), 0)
         for k, part in enumerate(total):
-            packed = jnp.where(lane == k, jnp.sum(part, axis=1, keepdims=True), packed)
+            packed = jnp.where(lane == 8 * k + sub, jnp.sum(part, axis=1, keepdims=True), packed)
+        packed = jnp.sum(packed, axis=0, keepdims=True)
         for n in range(2 * n_gy):
             dots_ref[n] = packed
         for copy in copies:
@@ -544,7 +557,11 @@
     sums = sums_ref[0]
     for n in range(1, sums_ref.shape[0]):
         sums = sums + sums_ref[n]
-    bz, zq, qw, wv, bw = (sums[:, k : k + 1] for k in range(5))
+    sums = jnp.broadcast_to(sums, (8, L))
+    sub = lax.broadcasted_iota(jnp.int32, (8, L), 0)
+    bz, zq, qw, wv, bw = (
+        jnp.sum(jnp.where(lanes() == 8 * k + sub, sums, 0.0), axis=1, keepdims=True) for k in range(5)
+    )
     a0 = bz / zq
     e1 = bz - a0 * (bw + zq) + a0 * a0 * qw
     beta = e1 / bz
@@ -604,24 +621,37 @@
     def along_gy(faces):
         return [shift(faces[0], ("gy",), (n_gy,), (1,)), shift(faces[1], ("gy",), (n_gy,), (-1,))]
 
+    def after(first, then):
+        return pl.pallas_call(
+            pass_kernel,
+            out_shape=[shape(*v.shape) for v in then],
+            in_specs=[HB] * (len(first) + len(then)),
+            out_specs=[HB] * len(then),
+            input_output_aliases={len(first) + n: n for n in range(len(then))},
+            compiler_params=WHOLE,
+            name="pass_on",
+        )(*first, *then)
+
+    def along_gx(to_high, to_low):
+        return [shift(to_high, GX, (n_gx,), (1,)), shift(to_low, GX, (n_gx,), (-1,))]
+
     def exchange(own, faces, messages, more):
         low = shift(own, ("z",), (n_z,), (1,))
         high = shift(own, ("z",), (n_z,), (-1,))
-        size = INV_AT if more else KAPPA_AT
-        part = pltpu.VMEM((size - CELLS, 8, CH * L), f32)
+        cells = along_gx(*after((low, high), messages))
+        size = CORNERS if more else KAPPA_AT
+        part = pltpu.VMEM((size, 8, CH * L), f32)
         out, to_high, to_low = pl.pallas_call(
             functools.partial(merge_kernel, bool(more), n_z, n_gy),
-            out_shape=[shape(2 * n_gy, 9, L)] + [shape(*m.shape) for m in messages],
-            in_specs=[VM] * 3 + [HB] * (4 + len(more)),
+            out_shape=[shape(2 * n_gy, 9, 1, L)] + [shape(size, 8, CH * L)] * 2,
+            in_specs=[VM] * 3 + [HB] * (2 + len(more)),
             out_specs=[VM, HB, HB],
-            input_output_aliases={5: 1, 6: 2},
             scratch_shapes=[part, part, pltpu.SemaphoreType.DMA((20,))],
             compiler_params=GRANT,
             name="merge_shares",
-        )(own, low, high, *(f.reshape(32, 8, CH * L) for f in faces), *messages, *more)
-        from_low = shift(to_high, GX, (n_gx,), (1,))
-        from_high = shift(to_low, GX, (n_gx,), (-1,))
-        return lax.all_to_all(out, SLAB2, 0, 0), [from_low, from_high]
+        )(own, low, high, *(f.reshape(32, 8, CH * L) for f in faces), *more)
+        corners = along_gx(to_high, to_low)
+        return lax.all_to_all(out, SLAB2, 0, 0), cells + corners
 
     def body(b, kappa, inverse):
         around = [
@@ -644,15 +674,7 @@
             compiler_params=WHOLE,
             name="pack_faces",
         )(b.reshape(64, 8, CH * L), inverse)
-        behind = pl.pallas_call(
-            pass_kernel,
-            out_shape=[y_face, y_face],
-            in_specs=[HB] * 6,
-            out_specs=[HB] * 2,
-            input_output_aliases={4: 0, 5: 1},
-            compiler_params=WHOLE,
-            name="pass_faces",
-        )(*around, packed[0], packed[1])
+        behind = after(around, packed[:2])
         b_faces = along_gy(behind)
         own = pl.pallas_call(
             functools.partial(first_shares_kernel, n_gx, n_gy),
@@ -667,7 +689,7 @@
                 pltpu.VMEM((8, 8, 8, CH * L), f32),
                 pltpu.VMEM((2, 8, CH * L), f32),
                 pltpu.VMEM((3, 8, 8, CH * L), f32),
-                pltpu.SemaphoreType.DMA((6,)),
+                pltpu.SemaphoreType.DMA((9,)),
             ],
             compiler_params=GRANT,
             name="first_shares",
@@ -678,16 +700,16 @@
             out_specs = [HB, HB, VM]
             if first:
                 outs += [shape(2, 8, L), shape(9, L), y_face, y_face]
-                outs += [shape(KAPPA_AT, 8, CH * L)] * 2
+                outs += [shape(CELLS, 8, CH * L)] * 2
                 out_specs += [VM, HB, HB, HB, HB]
             else:
-                outs += [shape(2 * n_gy, 8, L)]
+                outs += [shape(2 * n_gy, 1, L)]
             big = pltpu.VMEM((16, 16, 8, CH * L), f32)
             own_tile = pltpu.VMEM((8, 8, 8, CH * L), f32)
             return pl.pallas_call(
                 functools.partial(cycle_kernel, first, n_gx, n_gy),
                 out_shape=outs,
-                in_specs=[HB] * 14 + ([HB, VM] if more else []),
+                in_specs=[HB] * 18 + ([HB, VM] if more else []),
                 out_specs=out_specs,
                 scratch_shapes=[
                     big,
@@ -704,7 +726,7 @@
                     pltpu.VMEM((8, 8, CH * L), f32),
                     own_tile,
                     own_tile,
-                    pltpu.VMEM((2 * n_gy, 9, L), f32),
+                    pltpu.VMEM((2 * n_gy, 9, 1, L), f32),
                     own_tile,
                     pltpu.SemaphoreType.DMA((52,)),
                 ],
@@ -719,7 +741,7 @@
         w0, v0, packed = cycle(False, q0, q_faces, messages, b_messages, received, [b, dots])
 
         near_sum = jnp.sum(lax.all_to_all(packed, SLAB2, 0, 0), axis=0)
-        sums = lax.all_to_all(jnp.broadcast_to(near_sum, (n_z, 8, L)), "z", 0, 0)
+        sums = lax.all_to_all(jnp.broadcast_to(near_sum, (n_z, 1, L)), "z", 0, 0)
         return pl.pallas_call(
             combine_kernel,
             out_shape=[tile, tile],

time: 150 us -> 146 us (0.973)
  blocking collectives: 57 us -> 21.2 us
  starting transfers between devices: 31.4 us -> 52.1 us
  waiting for transfers between devices: 15.6 us -> 29.4 us
    all_to_all x3 -> x1, blocking collectives: 44.8 us -> 10.3 us  [body(): sums = lax.all_to_all(jnp.broadcast_to(near_sum, (n_z, 1, L)), 'z', 0, 0)]
    all_to_all x0 -> x2, starting transfers between devices: none -> 16 us  [exchange(): return (lax.all_to_all(out, SLAB2, 0, 0), cells + corners)]
    all_to_all x0 -> x2, waiting for transfers between devices: none -> 15.3 us  [exchange(): return (lax.all_to_all(out, SLAB2, 0, 0), cells + corners)]
    ppermute x16 -> x20, starting transfers between devices: 31.4 us -> 36.1 us  [shift(): return lax.ppermute(value, axes, pairs)]
    ppermute x16 -> x20, waiting for transfers between devices: 15.6 us -> 14.1 us  [shift(): return lax.ppermute(value, axes, pairs)]
  transfers between devices with their start and end apart: 16 -> 22, of which waited for: 6 -> 8; matrix products, arithmetic and copies ran while one was open for 0% -> 0% of each run, Pallas kernels for 4% -> 9%
where the time goes in v3:
time: 146 us
  starting transfers between devices  52.1 us (36%)
  Pallas kernels  40.7 us (28%)
  waiting for transfers between devices  29.4 us (20%)
  blocking collectives  21.2 us (15%)
    ppermute x20, starting transfers between devices, shift(): return lax.ppermute(value, axes, pairs)  36.1 us
    pallas_call x2, Pallas kernels, cycle(): pl.pallas_call(functools.partial(cycle_kernel, first, n_gx, n_gy), out_sh...  23 us
    all_to_all x2, starting transfers between devices, exchange(): return (lax.all_to_all(out, SLAB2, 0, 0), cells + corners)  16 us
    all_to_all x2, waiting for transfers between devices, exchange(): return (lax.all_to_all(out, SLAB2, 0, 0), cells + corners)  15.3 us
    ppermute x20, waiting for transfers between devices, shift(): return lax.ppermute(value, axes, pairs)  14.1 us
    all_to_all x1, blocking collectives, body(): near_sum = jnp.sum(lax.all_to_all(packed, SLAB2, 0, 0), axis=0)  10.9 us
    all_to_all x1, blocking collectives, body(): sums = lax.all_to_all(jnp.broadcast_to(near_sum, (n_z, 1, L)), 'z', 0, 0)  10.3 us
    pallas_call x2, Pallas kernels, exchange(): pl.pallas_call(functools.partial(merge_kernel, bool(more), n_z, n_gy), ou...  6.68 us
  transfers between devices with their start and end apart: 22, of which 8 were waited for; matrix products, arithmetic and copies ran while one was open for 0% of the time, Pallas kernels for 9%

profile of v3, /device:TPU:1, one launch (start us, length us, event | category | flops | bytes accessed | tf_op | source)
XLA Modules:
  0.0 145.6 jit_solution(17721550321790360940)
XLA Ops:
  0.6 5.8 %collective-permute-start.3 = (f32[8,8,512]{2,1,0:T(8,128)}, f32[8,8,512]{2,1,0:T(8,128)}, u32[]{:S(2)}, u32[]{:S(2)}) collective-permute-start(f32[8,8,512]{2,1,0:T(8,128)} %refs_11_.3), channel_id=1, source_target_pairs={{0,15},{1,0},{2,1},{3,2},{4,3},{5,4},{6,5},{7,6},{8,7},{9,8},{10,9... | collective-permute-start | bytes 393224 | tf_op jit(solution)/shard_map/ppermute | solution.py:601
  6.5 0.0 collective-permute-start.2
  6.5 1.0 collective-permute-start.1
  7.4 1.5 %collective-permute-start = (f32[8,8,512]{2,1,0:T(8,128)}, f32[8,8,512]{2,1,0:T(8,128)}, u32[]{:S(2)}, u32[]{:S(2)}) collective-permute-start(f32[8,8,512]{2,1,0:T(8,128)} %refs_11_.3), channel_id=1, source_target_pairs={{0,16},{16,32},{32,48},{48,64},{64,80},{80,96},{96,112},{112,128},... | collective-permute-start | bytes 393224 | tf_op jit(solution)/shard_map/ppermute | solution.py:601
  8.9 2.8 %pack_faces.1 = (f32[8,4,8,512]{3,2,1,0:T(8,128)}, f32[8,4,8,512]{3,2,1,0:T(8,128)}, f32[35,8,512]{2,1,0:T(8,128)}, f32[35,8,512]{2,1,0:T(8,128)}) custom-call(f32[64,8,512]{2,1,0:T(8,128)} %bitcast.5, f32[256,256]{1,0:T(8,128)} %refs_17_.3), custom_call_target="tpu_custom_call" | custom-call | tf_op jit(solution)/shard_map/pack_faces/pallas_call | solution.py:663
  11.7 0.0 collective-permute-done.3.refs_3_.kyh_hbm.refs_1_.refs_15_
  11.8 2.2 %collective-permute-done.2.refs_2_.kyl_hbm.refs_0_.refs_14_ = f32[8,8,512]{2,1,0:T(8,128)} collective-permute-done((f32[8,8,512]{2,1,0:T(8,128)}, f32[8,8,512]{2,1,0:T(8,128)}, u32[]{:S(2)}, u32[]{:S(2)}) %collective-permute-start.2) | collective-permute-done | bytes 131104 | tf_op jit(solution)/shard_map/ppermute | solution.py:601
  13.9 0.1 collective-permute-start.4
  14.0 4.8 %collective-permute-start.5 = (f32[8,4,8,512]{3,2,1,0:T(8,128)}, f32[8,4,8,512]{3,2,1,0:T(8,128)}, u32[]{:S(2)}, u32[]{:S(2)}) collective-permute-start(f32[8,4,8,512]{3,2,1,0:T(8,128)} %get-tuple-element.32), channel_id=1, source_target_pairs={{0,15},{1,0},{2,1},{3,2},{4,3},{5,4},{6,5},{7,6},{8,7},{9,8},{10,9... | collective-permute-start | bytes 1572872 | tf_op jit(solution)/shard_map/ppermute | solution.py:601
  18.8 3.7 %first_shares.1.own_ref = f32[9,128]{1,0:T(8,128)} custom-call(f32[8,8,8,512]{3,2,1,0:T(8,128)} %refs_0_.3, f32[8,8,512]{2,1,0:T(8,128)} %refs_11_.3, f32[8,8,512]{2,1,0:T(8,128)} %collective-permute-done.refs_0_.kxl_hbm.refs_12_, f32[8,8,512]{2,1,0:T(8,128)} %collective-permute-done.1.refs_1_.kxh_hbm.refs_13_, ...), custom_call_target="tpu_custom_call" | custom-call | tf_op jit(solution)/shard_map/first_shares/pallas_call | solution.py:679
  22.5 5.7 %collective-permute-start.7 = (f32[9,128]{1,0:T(8,128)}, f32[9,128]{1,0:T(8,128)}, u32[]{:S(2)}, u32[]{:S(2)}) collective-permute-start(f32[9,128]{1,0:T(8,128)} %first_shares.1.own_ref), channel_id=1, source_target_pairs={{0,224},{32,0},{64,32},{96,64},{128,96},{160,128},{192,160},{224,1... | collective-permute-start | bytes 13832 | tf_op jit(solution)/shard_map/ppermute | solution.py:601
  28.1 0.0 collective-permute-start.6
  28.1 1.0 collective-permute-done.7.refs_1_.high_ref
  29.1 3.0 %collective-permute-done.6.refs_0_.low_ref = f32[9,128]{1,0:T(8,128)} collective-permute-done((f32[9,128]{1,0:T(8,128)}, f32[9,128]{1,0:T(8,128)}, u32[]{:S(2)}, u32[]{:S(2)}) %collective-permute-start.6) | collective-permute-done | bytes 4640 | tf_op jit(solution)/shard_map/ppermute | solution.py:601
  32.2 2.5 %collective-permute-start.8 = (f32[35,8,512]{2,1,0:T(8,128)}, f32[35,8,512]{2,1,0:T(8,128)S(1)}, u32[]{:S(2)}, u32[]{:S(2)}) collective-permute-start(f32[35,8,512]{2,1,0:T(8,128)} %get-tuple-element.35), channel_id=1, source_target_pairs={{0,16},{16,32},{32,48},{48,64},{64,80},{80,96},{96,112},{112,128},... | collective-permute-start | bytes 1720328 | tf_op jit(solution)/shard_map/ppermute | solution.py:601
  34.7 1.6 %collective-permute-start.9 = (f32[35,8,512]{2,1,0:T(8,128)}, f32[35,8,512]{2,1,0:T(8,128)}, u32[]{:S(2)}, u32[]{:S(2)}) collective-permute-start(f32[35,8,512]{2,1,0:T(8,128)} %get-tuple-element.36), channel_id=1, source_target_pairs={{0,240},{16,0},{32,16},{48,32},{64,48},{80,64},{96,80},{112,96},{1... | collective-permute-start | bytes 1720328 | tf_op jit(solution)/shard_map/ppermute | solution.py:601
  36.3 3.4 %merge_shares.2 = (f32[32,9,1,128]{3,2,1,0:T(1,128)}, f32[18,8,512]{2,1,0:T(8,128)}, f32[18,8,512]{2,1,0:T(8,128)}) custom-call(f32[9,128]{1,0:T(8,128)} %first_shares.1.own_ref, f32[9,128]{1,0:T(8,128)} %collective-permute-done.6.refs_0_.low_ref, f32[9,128]{1,0:T(8,128)} %collective-permute-done.7.refs_1_.high_ref, f32[32,8,512]{2,1,0:T(8,128)} %bitcast.1.y_low, ...), custom_call_target="tpu_custom_call" | custom-call | tf_op jit(solution)/shard_map/merge_shares/pallas_call | solution.py:644
  39.7 0.2 collective-permute-start.10
  39.9 2.8 %collective-permute-start.11 = (f32[18,8,512]{2,1,0:T(8,128)}, f32[18,8,512]{2,1,0:T(8,128)}, u32[]{:S(2)}, u32[]{:S(2)}) collective-permute-start(f32[18,8,512]{2,1,0:T(8,128)} %get-tuple-element.38), channel_id=1, source_target_pairs={{0,240},{16,0},{32,16},{48,32},{64,48},{80,64},{96,80},{112,96},{1... | collective-permute-start | bytes 884744 | tf_op jit(solution)/shard_map/ppermute | solution.py:601
  42.7 6.5 %all-to-all-start = ((f32[32,9,1,128]{3,2,1,0:T(1,128)}), f32[32,9,1,128]{3,2,1,0:T(1,128)S(1)}, u32[]{:S(2)}, u32[]{:S(2)}) async-start(f32[32,9,1,128]{3,2,1,0:T(1,128)} %get-tuple-element.39), calls=%async_computation | async-start | bytes 294912 | tf_op jit(solution)/shard_map/all_to_all | solution.py:654
  49.3 0.0 collective-permute-done.8.refs_3_.refs_7_
  49.3 0.0 copy-start
  49.3 0.0 collective-permute-done.9.refs_4_.refs_8_
  49.3 7.6 %all-to-all-done.refs_16_ = f32[32,9,1,128]{3,2,1,0:T(1,128)S(1)} async-done(((f32[32,9,1,128]{3,2,1,0:T(1,128)}), f32[32,9,1,128]{3,2,1,0:T(1,128)S(1)}, u32[]{:S(2)}, u32[]{:S(2)}) %all-to-all-start) | async-done | bytes 147488 | tf_op jit(solution)/shard_map/all_to_all | solution.py:654
  56.9 0.0 collective-permute-done.11.refs_6_.refs_10_
  57.0 0.6 copy-done.1
  57.6 11.6 %first_cycle.1 = (f32[8,8,8,512]{3,2,1,0:T(8,128)}, f32[8,8,8,512]{3,2,1,0:T(8,128)}, f32[2,8,128]{2,1,0:T(8,128)}, f32[9,128]{1,0:T(8,128)}, f32[8,4,8,512]{3,2...) custom-call(f32[8,8,8,512]{3,2,1,0:T(8,128)} %refs_0_.3, ...), custom_call_target="tpu_custom_call" | custom-call | tf_op jit(solution)/shard_map/first_cycle/pallas_call | solution.py:709
  69.1 0.3 collective-permute-start.12
  69.5 4.5 %collective-permute-start.13 = (f32[8,4,8,512]{3,2,1,0:T(8,128)}, f32[8,4,8,512]{3,2,1,0:T(8,128)}, u32[]{:S(2)}, u32[]{:S(2)}) collective-permute-start(f32[8,4,8,512]{3,2,1,0:T(8,128)} %get-tuple-element.42), channel_id=1, source_target_pairs={{0,15},{1,0},{2,1},{3,2},{4,3},{5,4},{6,5},{7,6},{8,7},{9,8},{10,9... | collective-permute-start | bytes 1572872 | tf_op jit(solution)/shard_map/ppermute | solution.py:601
  74.0 0.0 collective-permute-start.15
  74.0 1.5 %collective-permute-start.14 = (f32[9,128]{1,0:T(8,128)}, f32[9,128]{1,0:T(8,128)}, u32[]{:S(2)}, u32[]{:S(2)}) collective-permute-start(f32[9,128]{1,0:T(8,128)} %get-tuple-element.43.own_ref), channel_id=1, source_target_pairs={{0,32},{32,64},{64,96},{96,128},{128,160},{160,192},{192,224},{224... | collective-permute-start | bytes 13832 | tf_op jit(solution)/shard_map/ppermute | solution.py:601
  75.5 1.6 %collective-permute-done.15.refs_1_.high_ref = f32[9,128]{1,0:T(8,128)} collective-permute-done((f32[9,128]{1,0:T(8,128)}, f32[9,128]{1,0:T(8,128)}, u32[]{:S(2)}, u32[]{:S(2)}) %collective-permute-start.15) | collective-permute-done | bytes 4640 | tf_op jit(solution)/shard_map/ppermute | solution.py:601
  77.1 1.2 collective-permute-done.14.refs_0_.low_ref
  78.3 2.4 %collective-permute-start.16 = (f32[32,8,512]{2,1,0:T(8,128)}, f32[32,8,512]{2,1,0:T(8,128)S(1)}, u32[]{:S(2)}, u32[]{:S(2)}) collective-permute-start(f32[32,8,512]{2,1,0:T(8,128)} %get-tuple-element.46), channel_id=1, source_target_pairs={{0,16},{16,32},{32,48},{48,64},{64,80},{80,96},{96,112},{112,128},... | collective-permute-start | bytes 1572872 | tf_op jit(solution)/shard_map/ppermute | solution.py:601
  80.7 5.0 %collective-permute-done.12.refs_1_ = f32[8,4,8,512]{3,2,1,0:T(8,128)} collective-permute-done((f32[8,4,8,512]{3,2,1,0:T(8,128)}, f32[8,4,8,512]{3,2,1,0:T(8,128)}, u32[]{:S(2)}, u32[]{:S(2)}) %collective-permute-start.12) | collective-permute-done | bytes 524320 | tf_op jit(solution)/shard_map/ppermute | solution.py:601
  85.8 3.2 %merge_shares.3 = (f32[32,9,1,128]{3,2,1,0:T(1,128)}, f32[12,8,512]{2,1,0:T(8,128)}, f32[12,8,512]{2,1,0:T(8,128)}) custom-call(f32[9,128]{1,0:T(8,128)} %get-tuple-element.43.own_ref, f32[9,128]{1,0:T(8,128)} %collective-permute-done.14.refs_0_.low_ref, f32[9,128]{1,0:T(8,128)} %collective-permute-done.15.refs_1_.high_ref, f32[32,8,512]{2,1,0:T(8,128)} %bitcast.3.y_low, ...), custom_call_target="tpu_custom_call" | custom-call | tf_op jit(solution)/shard_map/merge_shares/pallas_call | solution.py:644
  89.0 0.0 collective-permute-start.18
  89.1 1.4 collective-permute-start.19
  90.5 9.4 %all-to-all-start.1 = ((f32[32,9,1,128]{3,2,1,0:T(1,128)}), f32[32,9,1,128]{3,2,1,0:T(1,128)S(1)}, u32[]{:S(2)}, u32[]{:S(2)}) async-start(f32[32,9,1,128]{3,2,1,0:T(1,128)} %get-tuple-element.50), calls=%async_computation.1 | async-start | bytes 294912 | tf_op jit(solution)/shard_map/all_to_all | solution.py:654
  99.9 0.0 copy-start.3
  99.9 0.0 collective-permute-done.17.refs_4_
  100.0 7.6 %all-to-all-done.1.refs_16_ = f32[32,9,1,128]{3,2,1,0:T(1,128)S(1)} async-done(((f32[32,9,1,128]{3,2,1,0:T(1,128)}), f32[32,9,1,128]{3,2,1,0:T(1,128)S(1)}, u32[]{:S(2)}, u32[]{:S(2)}) %all-to-all-start.1) | async-done | bytes 147488 | tf_op jit(solution)/shard_map/all_to_all | solution.py:654
  107.6 0.6 copy-done.2
  108.3 11.4 %second_cycle.1 = (f32[8,8,8,512]{3,2,1,0:T(8,128)}, f32[8,8,8,512]{3,2,1,0:T(8,128)}, f32[32,1,128]{2,1,0:T(1,128)}) custom-call(f32[8,8,8,512]{3,2,1,0:T(8,128)} %get-tuple-element.40.refs_0_.refs_2_, f32[8,4,8,512]{3,2,1,0:T(8,128)} %collective-permute-done.12.refs_1_, f32[8,4,8,512]{3,2,1,0:T(8,128)} %collective-permute-done.13.refs_2_, ...), custom_call_target="tpu_custom_call" | custom-call | tf_op jit(solution)/shard_map/second_cycle/pallas_call | solution.py:709
  119.7 10.9 %all_to_all.20 = f32[32,1,128]{2,1,0:T(1,128)S(1)} all-to-all(f32[32,1,128]{2,1,0:T(1,128)} %get-tuple-element.52), channel_id=1, replica_groups=mesh['z'=8,'core'=2,'gy'=16] {'core','gy'}, dimensions={0} | all-to-all | bytes 32768 | tf_op jit(solution)/shard_map/all_to_all | solution.py:743
  130.6 0.1 reduce_sum.9
  130.7 10.3 %all_to_all.21.sums_ref = f32[8,1,128]{2,1,0:T(1,128)} all-to-all(f32[8,1,128]{2,1,0:T(1,128)S(1)} %broadcast_in_dim.3), channel_id=1, replica_groups=mesh['z'=8,'core'=2,'gy'=16] {'z'}, dimensions={0} | all-to-all | bytes 8192 | tf_op jit(solution)/shard_map/all_to_all | solution.py:744
  140.9 4.5 %combine.1 = (f32[8,8,8,512]{3,2,1,0:T(8,128)}, f32[8,8,8,512]{3,2,1,0:T(8,128)}) custom-call(f32[8,1,128]{2,1,0:T(1,128)} %all_to_all.21.sums_ref, f32[8,8,8,512]{3,2,1,0:T(8,128)} %refs_0_.3, f32[8,8,8,512]{3,2,1,0:T(8,128)} %get-tuple-element.53.refs_1_, f32[8,8,8,512]{3,2,1,0:T(8,128)} %get-tuple-element.40.refs_0_.refs_2_, ...), custom_call_target="tpu_custom_call" | custom-call | tf_op jit(solution)/shard_map/combine/pallas_call | solution.py:745
  (18 shorter events, 0.0 us)
Async XLA Ops:
  0.6 11.1 %collective-permute-start.3 = (f32[8,8,512]{2,1,0:T(8,128)}, f32[8,8,512]{2,1,0:T(8,128)}, u32[]{:S(2)}, u32[]{:S(2)}) collective-permute-start(f32[8,8,512]{2,1,0:T(8,128)} %refs_11_.3), channel_id=1, source_target_pairs={{0,15},{1,0},{2,1},{3,2},{4,3},{5,4},{6,5},{7,6},{8,7},{9,8},{10,9... | collective-permute-start | bytes 393224 | tf_op jit(solution)/shard_map/ppermute | solution.py:601
  6.5 7.5 %collective-permute-start.2 = (f32[8,8,512]{2,1,0:T(8,128)}, f32[8,8,512]{2,1,0:T(8,128)}, u32[]{:S(2)}, u32[]{:S(2)}) collective-permute-start(f32[8,8,512]{2,1,0:T(8,128)} %refs_11_.3), channel_id=1, source_target_pairs={{0,1},{1,2},{2,3},{3,4},{4,5},{5,6},{6,7},{7,8},{8,9},{9,10},{10,1... | collective-permute-start | bytes 393224 | tf_op jit(solution)/shard_map/ppermute | solution.py:601
  6.5 7.5 %collective-permute-start.1 = (f32[8,8,512]{2,1,0:T(8,128)}, f32[8,8,512]{2,1,0:T(8,128)}, u32[]{:S(2)}, u32[]{:S(2)}) collective-permute-start(f32[8,8,512]{2,1,0:T(8,128)} %refs_11_.3), channel_id=1, source_target_pairs={{0,240},{16,0},{32,16},{48,32},{64,48},{80,64},{96,80},{112,96},{1... | collective-permute-start | bytes 393224 | tf_op jit(solution)/shard_map/ppermute | solution.py:601
  7.4 6.5 %collective-permute-start = (f32[8,8,512]{2,1,0:T(8,128)}, f32[8,8,512]{2,1,0:T(8,128)}, u32[]{:S(2)}, u32[]{:S(2)}) collective-permute-start(f32[8,8,512]{2,1,0:T(8,128)} %refs_11_.3), channel_id=1, source_target_pairs={{0,16},{16,32},{32,48},{48,64},{64,80},{80,96},{96,112},{112,128},... | collective-permute-start | bytes 393224 | tf_op jit(solution)/shard_map/ppermute | solution.py:601
  13.9 22.3 %collective-permute-start.4 = (f32[8,4,8,512]{3,2,1,0:T(8,128)}, f32[8,4,8,512]{3,2,1,0:T(8,128)}, u32[]{:S(2)}, u32[]{:S(2)}) collective-permute-start(f32[8,4,8,512]{3,2,1,0:T(8,128)} %get-tuple-element.31), channel_id=1, source_target_pairs={{0,1},{1,2},{2,3},{3,4},{4,5},{5,6},{6,7},{7,8},{8,9},{9,10},{10,1... | collective-permute-start | bytes 1572872 | tf_op jit(solution)/shard_map/ppermute | solution.py:601
  14.0 22.3 %collective-permute-start.5 = (f32[8,4,8,512]{3,2,1,0:T(8,128)}, f32[8,4,8,512]{3,2,1,0:T(8,128)}, u32[]{:S(2)}, u32[]{:S(2)}) collective-permute-start(f32[8,4,8,512]{3,2,1,0:T(8,128)} %get-tuple-element.32), channel_id=1, source_target_pairs={{0,15},{1,0},{2,1},{3,2},{4,3},{5,4},{6,5},{7,6},{8,7},{9,8},{10,9... | collective-permute-start | bytes 1572872 | tf_op jit(solution)/shard_map/ppermute | solution.py:601
  22.5 6.7 %collective-permute-start.7 = (f32[9,128]{1,0:T(8,128)}, f32[9,128]{1,0:T(8,128)}, u32[]{:S(2)}, u32[]{:S(2)}) collective-permute-start(f32[9,128]{1,0:T(8,128)} %first_shares.1.own_ref), channel_id=1, source_target_pairs={{0,224},{32,0},{64,32},{96,64},{128,96},{160,128},{192,160},{224,1... | collective-permute-start | bytes 13832 | tf_op jit(solution)/shard_map/ppermute | solution.py:601
  28.1 4.0 %collective-permute-start.6 = (f32[9,128]{1,0:T(8,128)}, f32[9,128]{1,0:T(8,128)}, u32[]{:S(2)}, u32[]{:S(2)}) collective-permute-start(f32[9,128]{1,0:T(8,128)} %first_shares.1.own_ref), channel_id=1, source_target_pairs={{0,32},{32,64},{64,96},{96,128},{128,160},{160,192},{192,224},{224... | collective-permute-start | bytes 13832 | tf_op jit(solution)/shard_map/ppermute | solution.py:601
  32.2 17.1 %collective-permute-start.8 = (f32[35,8,512]{2,1,0:T(8,128)}, f32[35,8,512]{2,1,0:T(8,128)S(1)}, u32[]{:S(2)}, u32[]{:S(2)}) collective-permute-start(f32[35,8,512]{2,1,0:T(8,128)} %get-tuple-element.35), channel_id=1, source_target_pairs={{0,16},{16,32},{32,48},{48,64},{64,80},{80,96},{96,112},{112,128},... | collective-permute-start | bytes 1720328 | tf_op jit(solution)/shard_map/ppermute | solution.py:601
  34.7 14.6 %collective-permute-start.9 = (f32[35,8,512]{2,1,0:T(8,128)}, f32[35,8,512]{2,1,0:T(8,128)}, u32[]{:S(2)}, u32[]{:S(2)}) collective-permute-start(f32[35,8,512]{2,1,0:T(8,128)} %get-tuple-element.36), channel_id=1, source_target_pairs={{0,240},{16,0},{32,16},{48,32},{64,48},{80,64},{96,80},{112,96},{1... | collective-permute-start | bytes 1720328 | tf_op jit(solution)/shard_map/ppermute | solution.py:601
  39.7 17.2 %collective-permute-start.10 = (f32[18,8,512]{2,1,0:T(8,128)}, f32[18,8,512]{2,1,0:T(8,128)}, u32[]{:S(2)}, u32[]{:S(2)}) collective-permute-start(f32[18,8,512]{2,1,0:T(8,128)} %get-tuple-element.37), channel_id=1, source_target_pairs={{0,16},{16,32},{32,48},{48,64},{64,80},{80,96},{96,112},{112,128},... | collective-permute-start | bytes 884744 | tf_op jit(solution)/shard_map/ppermute | solution.py:601
  39.9 17.0 %collective-permute-start.11 = (f32[18,8,512]{2,1,0:T(8,128)}, f32[18,8,512]{2,1,0:T(8,128)}, u32[]{:S(2)}, u32[]{:S(2)}) collective-permute-start(f32[18,8,512]{2,1,0:T(8,128)} %get-tuple-element.38), channel_id=1, source_target_pairs={{0,240},{16,0},{32,16},{48,32},{64,48},{80,64},{96,80},{112,96},{1... | collective-permute-start | bytes 884744 | tf_op jit(solution)/shard_map/ppermute | solution.py:601
  42.7 14.2 %all-to-all-start = ((f32[32,9,1,128]{3,2,1,0:T(1,128)}), f32[32,9,1,128]{3,2,1,0:T(1,128)S(1)}, u32[]{:S(2)}, u32[]{:S(2)}) async-start(f32[32,9,1,128]{3,2,1,0:T(1,128)} %get-tuple-element.39), calls=%async_computation | async-start | bytes 294912 | tf_op jit(solution)/shard_map/all_to_all | solution.py:654
  49.3 7.7 %copy-start = (f32[35,8,512]{2,1,0:T(8,128)}, f32[35,8,512]{2,1,0:T(8,128)S(1)}, u32[]{:S(2)}) copy-start(f32[35,8,512]{2,1,0:T(8,128)S(1)} %collective-permute-done.8.refs_3_.refs_7_) | copy-start | bytes 1720324
  56.9 0.7 copy-start.1
  69.1 16.6 %collective-permute-start.12 = (f32[8,4,8,512]{3,2,1,0:T(8,128)}, f32[8,4,8,512]{3,2,1,0:T(8,128)}, u32[]{:S(2)}, u32[]{:S(2)}) collective-permute-start(f32[8,4,8,512]{3,2,1,0:T(8,128)} %get-tuple-element.41), channel_id=1, source_target_pairs={{0,1},{1,2},{2,3},{3,4},{4,5},{5,6},{6,7},{7,8},{8,9},{9,10},{10,1... | collective-permute-start | bytes 1572872 | tf_op jit(solution)/shard_map/ppermute | solution.py:601
  69.5 16.3 %collective-permute-start.13 = (f32[8,4,8,512]{3,2,1,0:T(8,128)}, f32[8,4,8,512]{3,2,1,0:T(8,128)}, u32[]{:S(2)}, u32[]{:S(2)}) collective-permute-start(f32[8,4,8,512]{3,2,1,0:T(8,128)} %get-tuple-element.42), channel_id=1, source_target_pairs={{0,15},{1,0},{2,1},{3,2},{4,3},{5,4},{6,5},{7,6},{8,7},{9,8},{10,9... | collective-permute-start | bytes 1572872 | tf_op jit(solution)/shard_map/ppermute | solution.py:601
  74.0 3.1 %collective-permute-start.15 = (f32[9,128]{1,0:T(8,128)}, f32[9,128]{1,0:T(8,128)}, u32[]{:S(2)}, u32[]{:S(2)}) collective-permute-start(f32[9,128]{1,0:T(8,128)} %get-tuple-element.43.own_ref), channel_id=1, source_target_pairs={{0,224},{32,0},{64,32},{96,64},{128,96},{160,128},{192,160},{224,1... | collective-permute-start | bytes 13832 | tf_op jit(solution)/shard_map/ppermute | solution.py:601
  74.0 4.3 %collective-permute-start.14 = (f32[9,128]{1,0:T(8,128)}, f32[9,128]{1,0:T(8,128)}, u32[]{:S(2)}, u32[]{:S(2)}) collective-permute-start(f32[9,128]{1,0:T(8,128)} %get-tuple-element.43.own_ref), channel_id=1, source_target_pairs={{0,32},{32,64},{64,96},{96,128},{128,160},{160,192},{192,224},{224... | collective-permute-start | bytes 13832 | tf_op jit(solution)/shard_map/ppermute | solution.py:601
  78.3 21.6 %collective-permute-start.16 = (f32[32,8,512]{2,1,0:T(8,128)}, f32[32,8,512]{2,1,0:T(8,128)S(1)}, u32[]{:S(2)}, u32[]{:S(2)}) collective-permute-start(f32[32,8,512]{2,1,0:T(8,128)} %get-tuple-element.46), channel_id=1, source_target_pairs={{0,16},{16,32},{32,48},{48,64},{64,80},{80,96},{96,112},{112,128},... | collective-permute-start | bytes 1572872 | tf_op jit(solution)/shard_map/ppermute | solution.py:601
  80.7 19.2 %collective-permute-start.17 = (f32[32,8,512]{2,1,0:T(8,128)}, f32[32,8,512]{2,1,0:T(8,128)}, u32[]{:S(2)}, u32[]{:S(2)}) collective-permute-start(f32[32,8,512]{2,1,0:T(8,128)} %get-tuple-element.47), channel_id=1, source_target_pairs={{0,240},{16,0},{32,16},{48,32},{64,48},{80,64},{96,80},{112,96},{1... | collective-permute-start | bytes 1572872 | tf_op jit(solution)/shard_map/ppermute | solution.py:601
  89.0 18.6 %collective-permute-start.18 = (f32[12,8,512]{2,1,0:T(8,128)}, f32[12,8,512]{2,1,0:T(8,128)}, u32[]{:S(2)}, u32[]{:S(2)}) collective-permute-start(f32[12,8,512]{2,1,0:T(8,128)} %get-tuple-element.48), channel_id=1, source_target_pairs={{0,16},{16,32},{32,48},{48,64},{64,80},{80,96},{96,112},{112,128},... | collective-permute-start | bytes 589832 | tf_op jit(solution)/shard_map/ppermute | solution.py:601
  89.1 18.5 %collective-permute-start.19 = (f32[12,8,512]{2,1,0:T(8,128)}, f32[12,8,512]{2,1,0:T(8,128)}, u32[]{:S(2)}, u32[]{:S(2)}) collective-permute-start(f32[12,8,512]{2,1,0:T(8,128)} %get-tuple-element.49), channel_id=1, source_target_pairs={{0,240},{16,0},{32,16},{48,32},{64,48},{80,64},{96,80},{112,96},{1... | collective-permute-start | bytes 589832 | tf_op jit(solution)/shard_map/ppermute | solution.py:601
  90.5 17.1 %all-to-all-start.1 = ((f32[32,9,1,128]{3,2,1,0:T(1,128)}), f32[32,9,1,128]{3,2,1,0:T(1,128)S(1)}, u32[]{:S(2)}, u32[]{:S(2)}) async-start(f32[32,9,1,128]{3,2,1,0:T(1,128)} %get-tuple-element.50), calls=%async_computation.1 | async-start | bytes 294912 | tf_op jit(solution)/shard_map/all_to_all | solution.py:654
  99.9 7.7 %copy-start.3 = (f32[32,8,512]{2,1,0:T(8,128)}, f32[32,8,512]{2,1,0:T(8,128)S(1)}, u32[]{:S(2)}) copy-start(f32[32,8,512]{2,1,0:T(8,128)S(1)} %collective-permute-done.16.refs_3_) | copy-start | bytes 1572868
  107.6 0.7 copy-start.2

commit v4 on v3

--- a/solution.py
+++ b/solution.py
@@ -177,13 +177,14 @@
     lax.fori_loop(0, 10, one, 0)
 
 
-def first_shares_kernel(n_gx, n_gy, b_hbm, kap_hbm, kxl_hbm, kxh_hbm, kyl_hbm, kyh_hbm, out_ref, *refs):
+def first_shares_kernel(n_gx, n_gy, b_hbm, kap_hbm, kxl_hbm, kxh_hbm, ke_hbm, ko_hbm, out_ref, *refs):
+    even, odd = parity()
     h_ref, g_ref, gf_ref, rows_ref, b_ref, KX, KY, sems = refs
     copies = run_copies(
         [
-            (kyl_hbm, KY.at[0]),
+            (ke_hbm, KY.at[2 * even]),
             (kap_hbm, KY.at[1]),
-            (kyh_hbm, KY.at[2]),
+            (ko_hbm, KY.at[2 * odd]),
             (kxl_hbm.at[7], KX.at[0]),
             (kxh_hbm.at[0], KX.at[1]),
         ]
@@ -274,6 +275,11 @@
     return (flag(gx > 0), one, flag(gx < n_gx - 1)), (flag(gy > 0), one, flag(gy < n_gy - 1))
 
 
+def parity():
+    odd = lax.rem(lax.axis_index("gy"), 2)
+    return 1 - odd, odd
+
+
 def run_copies(pairs, sems, base=0):
     copies = []
     for n, (src, dst) in enumerate(pairs):
@@ -283,8 +289,9 @@
     return copies
 
 
-def pack_kernel(n_gy, cells, inverse, to_high, to_low, m_high, m_low, b_ref, inv_ref, in_sems, sems):
+def pack_kernel(n_gy, cells, inverse, to_even, to_odd, m_high, m_low, b_ref, inv_ref, in_sems, sems):
     gy = lax.axis_index("gy")
+    even, odd = parity()
     inv = []
     for n in range(6):
         block = jnp.clip(gy - 1 + n // 2, 0, n_gy - 1) * 16 + (n % 2) * 8
@@ -296,8 +303,8 @@
         copy.wait()
     pairs = []
     for x in range(8):
-        pairs.append((b_ref.at[8 * x + 4 : 8 * x + 8], to_high.at[x]))
-        pairs.append((b_ref.at[8 * x : 8 * x + 4], to_low.at[x]))
+        pairs.append((b_ref.at[pl.ds(8 * x + 4 * even, 4)], to_even.at[x]))
+        pairs.append((b_ref.at[pl.ds(8 * x + 4 * odd, 4)], to_odd.at[x]))
     for start, m in ((32, m_high), (0, m_low)):
         pairs.append((b_ref.at[start : start + 32], m.at[0:CELLS]))
         pairs.append((inv_ref, m.at[INV_AT:LAST]))
@@ -320,21 +327,28 @@
         at += 4 - a
 
 
-def merge_kernel(first, n_z, n_gy, own_ref, low_ref, high_ref, y_low, y_high, *refs):
+def merge_kernel(first, n_z, n_gy, own_ref, low_ref, high_ref, y_even, y_odd, *refs):
     if first:
-        kyl, kyh = refs[:2]
+        k_even, k_odd = refs[:2]
         refs = refs[2:]
     out_ref, to_high, to_low, high_part, low_part, sems = refs
+    even, odd = parity()
+    sides = ((y_even, even, odd), (y_odd, odd, even))
     pairs = []
     for up, m in ((True, high_part), (False, low_part)):
         for a, at, wide in corner_segments():
             x = 8 - a if up else a - 1
-            pairs.append((y_low.at[x * 4 + 4 - wide : x * 4 + 4], m.at[at : at + wide]))
-            pairs.append((y_high.at[x * 4 : x * 4 + wide], m.at[HIGH_AT + at : HIGH_AT + at + wide]))
+            for face, above, below in sides:
+                pairs.append(
+                    (
+                        face.at[pl.ds(x * 4 + below * (4 - wide), wide)],
+                        m.at[pl.ds(at + above * HIGH_AT, wide)],
+                    )
+                )
         if first:
             x = 5 if up else 0
-            pairs.append((kyl.at[x : x + 3], m.at[KAPPA_AT : KAPPA_AT + 3]))
-            pairs.append((kyh.at[x : x + 3], m.at[KAPPA_AT + 3 : KAPPA_AT + 6]))
+            pairs.append((k_even.at[x : x + 3], m.at[pl.ds(KAPPA_AT + 3 * even, 3)]))
+            pairs.append((k_odd.at[x : x + 3], m.at[pl.ds(KAPPA_AT + 3 * odd, 3)]))
     copies = run_copies(pairs, sems)
     z, core = lax.axis_index("z"), lax.axis_index("core")
     below = jnp.where(z > 0, 1.0, 0.0).astype(jnp.float32)
@@ -344,9 +358,9 @@
     high = [high_ref[n : n + 1] * above for n in range(9)]
     slabs = []
     for dy in range(3):
-        even = [own[dy] + low[6 + dy], own[3 + dy], own[6 + dy] + high[dy], high[3 + dy]]
-        odd = [low[3 + dy], own[dy] + low[6 + dy], own[3 + dy], own[6 + dy] + high[dy]]
-        slabs.append([jnp.where(core == 0, e, o) for e, o in zip(even, odd)])
+        first_core = [own[dy] + low[6 + dy], own[3 + dy], own[6 + dy] + high[dy], high[3 + dy]]
+        second_core = [low[3 + dy], own[dy] + low[6 + dy], own[3 + dy], own[6 + dy] + high[dy]]
+        slabs.append([jnp.where(core == 0, e, o) for e, o in zip(first_core, second_core)])
     for t in range(3):
         for dy in range(3):
             for n in range(n_gy):
@@ -359,8 +373,8 @@
 
 
 def cycle_kernel(first, n_gx, n_gy, *refs):
-    f_own, f_yl, f_yh, f_xl, f_xh, f_cl, f_ch, b_xl, b_xh, b_cl, b_ch = refs[:11]
-    kap_ref, kxl, kxh, kyl, kyh, recv_hbm, c_own = refs[11:18]
+    f_own, f_even, f_odd, f_xl, f_xh, f_cl, f_ch, b_xl, b_xh, b_cl, b_ch = refs[:11]
+    kap_ref, kxl, kxh, k_even, k_odd, c_own, recv_ref = refs[11:18]
     refs = refs[18:]
     if first:
         z_out, q_out, dots_ref, out_ref = refs[:4]
@@ -369,11 +383,12 @@
     else:
         extra_hbm, earlier_ref, z_out, q_out, dots_ref = refs[:5]
         refs = refs[5:]
-    F, A, B, G, KC, KX, KY, inv_ref, c_ref, h_ref, gf_ref, rows_ref, z_ref, q_ref, recv_ref, extra_ref, sems = refs
+    F, A, B, G, KC, KX, KY, inv_ref, c_ref, h_ref, gf_ref, rows_ref, z_ref, q_ref, extra_ref, sems = refs
     has_x, has_y = place(n_gx, n_gy)
     gy = lax.axis_index("gy")
 
-    pairs = [(recv_hbm, recv_ref)]
+    even, odd = parity()
+    pairs = []
     for jj in range(3):
         block = jnp.clip(gy - 1 + jj, 0, n_gy - 1)
         pairs.append(
@@ -388,16 +403,16 @@
         (b_cl.at[KAPPA_AT:CORNERS], KC.at[0]),
         (b_ch.at[KAPPA_AT:CORNERS], KC.at[1]),
         (kap_ref, KY.at[1]),
-        (kyl, KY.at[0]),
-        (kyh, KY.at[2]),
+        (k_even, KY.at[2 * even]),
+        (k_odd, KY.at[2 * odd]),
         (kxl.at[4:8], KX.at[0]),
         (kxh.at[0:4], KX.at[1]),
     ]
     n_kappa = len(pairs)
     pairs += [
         (f_own, F.at[4:12, 4:12]),
-        (f_yl, F.at[4:12, 0:4]),
-        (f_yh, F.at[4:12, 12:16]),
+        (f_even, F.at[4:12, pl.ds(12 * even, 4)]),
+        (f_odd, F.at[4:12, pl.ds(12 * odd, 4)]),
     ]
     for low, ref, corner in ((True, f_xl, f_cl), (False, f_xh, f_ch)):
         for i in range(4):
@@ -503,8 +518,8 @@
         dots_ref[1] = zq
         copies = run_copies(
             [
-                (q_ref.at[0:8, 4:8], sends[0]),
-                (q_ref.at[0:8, 0:4], sends[1]),
+                (q_ref.at[0:8, pl.ds(4 * even, 4)], sends[0]),
+                (q_ref.at[0:8, pl.ds(4 * odd, 4)], sends[1]),
             ]
             + [(q_ref.at[4 + i], sends[2].at[8 * i : 8 * i + 8]) for i in range(4)]
             + [(q_ref.at[i], sends[3].at[8 * i : 8 * i + 8]) for i in range(4)]
@@ -618,8 +633,11 @@
     tile = shape(8, 8, 8, CH * L)
     y_face = shape(8, 4, 8, CH * L)
 
-    def along_gy(faces):
-        return [shift(faces[0], ("gy",), (n_gy,), (1,)), shift(faces[1], ("gy",), (n_gy,), (-1,))]
+    even_pairs = [(n, n ^ 1) for n in range(n_gy)]
+    odd_pairs = [(n, ((n - 1) ^ 1) + 1 if 0 < n < n_gy - 1 else n) for n in range(n_gy)]
+
+    def along_gy(to_even, to_odd):
+        return [lax.ppermute(to_even, "gy", even_pairs), lax.ppermute(to_odd, "gy", odd_pairs)]
 
     def after(first, then):
         return pl.pallas_call(
@@ -657,8 +675,7 @@
         around = [
             shift(kappa, GX, (n_gx,), (1,)),
             shift(kappa, GX, (n_gx,), (-1,)),
-            shift(kappa, ("gy",), (n_gy,), (1,)),
-            shift(kappa, ("gy",), (n_gy,), (-1,)),
+            *along_gy(kappa, kappa),
         ]
         packed = pl.pallas_call(
             functools.partial(pack_kernel, n_gy),
@@ -675,7 +692,7 @@
             name="pack_faces",
         )(b.reshape(64, 8, CH * L), inverse)
         behind = after(around, packed[:2])
-        b_faces = along_gy(behind)
+        b_faces = along_gy(*behind)
         own = pl.pallas_call(
             functools.partial(first_shares_kernel, n_gx, n_gy),
             out_shape=shape(9, L),
@@ -709,7 +726,7 @@
             return pl.pallas_call(
                 functools.partial(cycle_kernel, first, n_gx, n_gy),
                 out_shape=outs,
-                in_specs=[HB] * 18 + ([HB, VM] if more else []),
+                in_specs=[HB] * 17 + [VM] + ([HB, VM] if more else []),
                 out_specs=out_specs,
                 scratch_shapes=[
                     big,
@@ -726,17 +743,16 @@
                     pltpu.VMEM((8, 8, CH * L), f32),
                     own_tile,
                     own_tile,
-                    pltpu.VMEM((2 * n_gy, 9, 1, L), f32),
                     own_tile,
                     pltpu.SemaphoreType.DMA((52,)),
                 ],
                 compiler_params=GRANT,
                 name="first_cycle" if first else "second_cycle",
-            )(field, *faces, *messages, *b_messages, kappa, *around, received, inverse, *more)
+            )(field, *faces, *messages, *b_messages, kappa, *around, inverse, received, *more)
 
         received, b_messages = exchange(own, b_faces, packed[2:], around[2:])
         z0, q0, dots, own, *sends = cycle(True, b, b_faces, b_messages, b_messages, received, [])
-        q_faces = along_gy(sends[:2])
+        q_faces = along_gy(*sends[:2])
         received, messages = exchange(own, q_faces, sends[2:], [])
         w0, v0, packed = cycle(False, q0, q_faces, messages, b_messages, received, [b, dots])
 

time: 146 us -> 144 us (0.986)
  waiting for transfers between devices: 29.4 us -> 24.6 us
    ppermute x20 -> x14, starting transfers between devices: 36.1 us -> 17.7 us  [shift(): return lax.ppermute(value, axes, pairs)]
    ppermute x0 -> x6, starting transfers between devices: none -> 16.3 us  [the longest x3 12.9 us: along_gy(): lax.ppermute(to_odd, 'gy', odd_pairs)]
    ppermute x20 -> x14, waiting for transfers between devices: 14.1 us -> 8.18 us  [shift(): return lax.ppermute(value, axes, pairs)]
    all_to_all x2, starting transfers between devices: 16 us -> 19.3 us  [exchange(): return (lax.all_to_all(out, SLAB2, 0, 0), cells + corners)]
  transfers between devices with their start and end apart: 22 -> 22, of which waited for: 8 -> 9; matrix products, arithmetic and copies ran while one was open for 0% -> 0% of each run, Pallas kernels for 9% -> 9%
where the time goes in v4:
time: 144 us; the launch traced here: 143 us
  starting transfers between devices  53.3 us (37%)
  Pallas kernels  41.7 us (29%)
  waiting for transfers between devices  24.6 us (17%)
  blocking collectives  20.8 us (14%)
    pallas_call x2, Pallas kernels, cycle(): pl.pallas_call(functools.partial(cycle_kernel, first, n_gx, n_gy), out_sh...  24 us
    all_to_all x2, starting transfers between devices, exchange(): return (lax.all_to_all(out, SLAB2, 0, 0), cells + corners)  19.3 us
    ppermute x14, starting transfers between devices, shift(): return lax.ppermute(value, axes, pairs)  17.7 us
    all_to_all x2, waiting for transfers between devices, exchange(): return (lax.all_to_all(out, SLAB2, 0, 0), cells + corners)  15.3 us
    ppermute x3, starting transfers between devices, along_gy(): lax.ppermute(to_odd, 'gy', odd_pairs)  12.9 us
    all_to_all x1, blocking collectives, body(): near_sum = jnp.sum(lax.all_to_all(packed, SLAB2, 0, 0), axis=0)  10.9 us
    all_to_all x1, blocking collectives, body(): sums = lax.all_to_all(jnp.broadcast_to(near_sum, (n_z, 1, L)), 'z', 0, 0)  9.88 us
    ppermute x14, waiting for transfers between devices, shift(): return lax.ppermute(value, axes, pairs)  8.18 us
  transfers between devices with their start and end apart: 22, of which 9 were waited for; matrix products, arithmetic and copies ran while one was open for 0% of the time, Pallas kernels for 9%

profile of v4, /device:TPU:1, one launch (start us, length us, event | category | flops | bytes accessed | tf_op | source)
XLA Modules:
  0.0 142.8 jit_solution(11706023406897145044)
XLA Ops:
  0.6 2.2 %collective-permute-start.3 = (f32[8,8,512]{2,1,0:T(8,128)}, f32[8,8,512]{2,1,0:T(8,128)}, u32[]{:S(2)}, u32[]{:S(2)}) collective-permute-start(f32[8,8,512]{2,1,0:T(8,128)} %refs_11_.3), channel_id=1, source_target_pairs={{0,0},{1,2},{2,1},{3,4},{4,3},{5,6},{6,5},{7,8},{8,7},{9,10},{10,9... | collective-permute-start | bytes 393224 | tf_op jit(solution)/shard_map/ppermute | solution.py:640
  2.8 3.1 %collective-permute-start.2 = (f32[8,8,512]{2,1,0:T(8,128)}, f32[8,8,512]{2,1,0:T(8,128)}, u32[]{:S(2)}, u32[]{:S(2)}) collective-permute-start(f32[8,8,512]{2,1,0:T(8,128)} %refs_11_.3), channel_id=1, source_target_pairs={{0,1},{1,0},{2,3},{3,2},{4,5},{5,4},{6,7},{7,6},{8,9},{9,8},{10,11... | collective-permute-start | bytes 393224 | tf_op jit(solution)/shard_map/ppermute | solution.py:640
  5.9 1.2 collective-permute-start.1
  7.1 1.5 %collective-permute-start = (f32[8,8,512]{2,1,0:T(8,128)}, f32[8,8,512]{2,1,0:T(8,128)}, u32[]{:S(2)}, u32[]{:S(2)}) collective-permute-start(f32[8,8,512]{2,1,0:T(8,128)} %refs_11_.3), channel_id=1, source_target_pairs={{0,16},{16,32},{32,48},{48,64},{64,80},{80,96},{96,112},{112,128},... | collective-permute-start | bytes 393224 | tf_op jit(solution)/shard_map/ppermute | solution.py:616
  8.6 2.8 %pack_faces.1 = (f32[8,4,8,512]{3,2,1,0:T(8,128)}, f32[8,4,8,512]{3,2,1,0:T(8,128)}, f32[35,8,512]{2,1,0:T(8,128)}, f32[35,8,512]{2,1,0:T(8,128)}) custom-call(f32[64,8,512]{2,1,0:T(8,128)} %bitcast.5, f32[256,256]{1,0:T(8,128)} %refs_16_.3), custom_call_target="tpu_custom_call" | custom-call | tf_op jit(solution)/shard_map/pack_faces/pallas_call | solution.py:680
  11.4 0.0 collective-permute-done.3.refs_3_.ko_hbm.refs_1_.refs_15_
  11.5 0.0 collective-permute-done.2.refs_2_.ke_hbm.refs_0_.refs_14_
  11.5 0.2 collective-permute-done.1.refs_1_.kxh_hbm.refs_13_
  11.6 1.4 collective-permute-done.refs_0_.kxl_hbm.refs_12_
  13.0 0.0 collective-permute-start.4
  13.1 5.3 %collective-permute-start.5 = (f32[8,4,8,512]{3,2,1,0:T(8,128)}, f32[8,4,8,512]{3,2,1,0:T(8,128)}, u32[]{:S(2)}, u32[]{:S(2)}) collective-permute-start(f32[8,4,8,512]{3,2,1,0:T(8,128)} %get-tuple-element.32), channel_id=1, source_target_pairs={{0,0},{1,2},{2,1},{3,4},{4,3},{5,6},{6,5},{7,8},{8,7},{9,10},{10,9... | collective-permute-start | bytes 1572872 | tf_op jit(solution)/shard_map/ppermute | solution.py:640
  18.4 3.7 %first_shares.1.own_ref = f32[9,128]{1,0:T(8,128)} custom-call(f32[8,8,8,512]{3,2,1,0:T(8,128)} %refs_0_.3, f32[8,8,512]{2,1,0:T(8,128)} %refs_11_.3, f32[8,8,512]{2,1,0:T(8,128)} %collective-permute-done.refs_0_.kxl_hbm.refs_12_, f32[8,8,512]{2,1,0:T(8,128)} %collective-permute-done.1.refs_1_.kxh_hbm.refs_13_, ...), custom_call_target="tpu_custom_call" | custom-call | tf_op jit(solution)/shard_map/first_shares/pallas_call | solution.py:696
  22.1 4.4 %collective-permute-start.7 = (f32[9,128]{1,0:T(8,128)}, f32[9,128]{1,0:T(8,128)}, u32[]{:S(2)}, u32[]{:S(2)}) collective-permute-start(f32[9,128]{1,0:T(8,128)} %first_shares.1.own_ref), channel_id=1, source_target_pairs={{0,224},{32,0},{64,32},{96,64},{128,96},{160,128},{192,160},{224,1... | collective-permute-start | bytes 13832 | tf_op jit(solution)/shard_map/ppermute | solution.py:616
  26.5 0.0 collective-permute-start.6
  26.5 1.0 collective-permute-done.7.refs_1_.high_ref
  27.5 3.0 %collective-permute-done.6.refs_0_.low_ref = f32[9,128]{1,0:T(8,128)} collective-permute-done((f32[9,128]{1,0:T(8,128)}, f32[9,128]{1,0:T(8,128)}, u32[]{:S(2)}, u32[]{:S(2)}) %collective-permute-start.6) | collective-permute-done | bytes 4640 | tf_op jit(solution)/shard_map/ppermute | solution.py:616
  30.6 2.2 %collective-permute-start.8 = (f32[35,8,512]{2,1,0:T(8,128)}, f32[35,8,512]{2,1,0:T(8,128)S(1)}, u32[]{:S(2)}, u32[]{:S(2)}) collective-permute-start(f32[35,8,512]{2,1,0:T(8,128)} %get-tuple-element.35), channel_id=1, source_target_pairs={{0,16},{16,32},{32,48},{48,64},{64,80},{80,96},{96,112},{112,128},... | collective-permute-start | bytes 1720328 | tf_op jit(solution)/shard_map/ppermute | solution.py:616
  32.8 3.5 %merge_shares.2 = (f32[32,9,1,128]{3,2,1,0:T(1,128)}, f32[18,8,512]{2,1,0:T(8,128)}, f32[18,8,512]{2,1,0:T(8,128)}) custom-call(f32[9,128]{1,0:T(8,128)} %first_shares.1.own_ref, f32[9,128]{1,0:T(8,128)} %collective-permute-done.6.refs_0_.low_ref, f32[9,128]{1,0:T(8,128)} %collective-permute-done.7.refs_1_.high_ref, f32[32,8,512]{2,1,0:T(8,128)} %bitcast.1.y_even, ...), custom_call_target="tpu_custom_call" | custom-call | tf_op jit(solution)/shard_map/merge_shares/pallas_call | solution.py:662
  36.3 1.8 %collective-permute-start.10 = (f32[18,8,512]{2,1,0:T(8,128)}, f32[18,8,512]{2,1,0:T(8,128)}, u32[]{:S(2)}, u32[]{:S(2)}) collective-permute-start(f32[18,8,512]{2,1,0:T(8,128)} %get-tuple-element.37), channel_id=1, source_target_pairs={{0,16},{16,32},{32,48},{48,64},{64,80},{80,96},{96,112},{112,128},... | collective-permute-start | bytes 884744 | tf_op jit(solution)/shard_map/ppermute | solution.py:616
  38.0 1.1 collective-permute-start.11
  39.1 9.0 %all-to-all-start = ((f32[32,9,1,128]{3,2,1,0:T(1,128)}), f32[32,9,1,128]{3,2,1,0:T(1,128)S(1)}, u32[]{:S(2)}, u32[]{:S(2)}) async-start(f32[32,9,1,128]{3,2,1,0:T(1,128)} %get-tuple-element.39), calls=%async_computation | async-start | bytes 294912 | tf_op jit(solution)/shard_map/all_to_all | solution.py:672
  48.2 0.0 copy-start
  48.2 0.0 collective-permute-done.9.refs_4_.refs_8_
  48.2 7.6 %all-to-all-done.refs_17_ = f32[32,9,1,128]{3,2,1,0:T(1,128)S(1)} async-done(((f32[32,9,1,128]{3,2,1,0:T(1,128)}), f32[32,9,1,128]{3,2,1,0:T(1,128)S(1)}, u32[]{:S(2)}, u32[]{:S(2)}) %all-to-all-start) | async-done | bytes 147488 | tf_op jit(solution)/shard_map/all_to_all | solution.py:672
  55.8 0.0 collective-permute-done.11.refs_6_.refs_10_
  55.8 0.6 copy-done.1
  56.5 12.4 %first_cycle.1 = (f32[8,8,8,512]{3,2,1,0:T(8,128)}, f32[8,8,8,512]{3,2,1,0:T(8,128)}, f32[2,8,128]{2,1,0:T(8,128)}, f32[9,128]{1,0:T(8,128)}, f32[8,4,8,512]{3,2...) custom-call(f32[8,8,8,512]{3,2,1,0:T(8,128)} %refs_0_.3, ...), custom_call_target="tpu_custom_call" | custom-call | tf_op jit(solution)/shard_map/first_cycle/pallas_call | solution.py:726
  68.9 0.3 collective-permute-start.12
  69.2 5.3 %collective-permute-start.13 = (f32[8,4,8,512]{3,2,1,0:T(8,128)}, f32[8,4,8,512]{3,2,1,0:T(8,128)}, u32[]{:S(2)}, u32[]{:S(2)}) collective-permute-start(f32[8,4,8,512]{3,2,1,0:T(8,128)} %get-tuple-element.42), channel_id=1, source_target_pairs={{0,0},{1,2},{2,1},{3,4},{4,3},{5,6},{6,5},{7,8},{8,7},{9,10},{10,9... | collective-permute-start | bytes 1572872 | tf_op jit(solution)/shard_map/ppermute | solution.py:640
  74.6 1.5 %collective-permute-start.14 = (f32[9,128]{1,0:T(8,128)}, f32[9,128]{1,0:T(8,128)}, u32[]{:S(2)}, u32[]{:S(2)}) collective-permute-start(f32[9,128]{1,0:T(8,128)} %get-tuple-element.43.own_ref), channel_id=1, source_target_pairs={{0,32},{32,64},{64,96},{96,128},{128,160},{160,192},{192,224},{224... | collective-permute-start | bytes 13832 | tf_op jit(solution)/shard_map/ppermute | solution.py:616
  76.0 1.6 %collective-permute-done.15.refs_1_.high_ref = f32[9,128]{1,0:T(8,128)} collective-permute-done((f32[9,128]{1,0:T(8,128)}, f32[9,128]{1,0:T(8,128)}, u32[]{:S(2)}, u32[]{:S(2)}) %collective-permute-start.15) | collective-permute-done | bytes 4640 | tf_op jit(solution)/shard_map/ppermute | solution.py:616
  77.7 0.9 collective-permute-done.14.refs_0_.low_ref
  78.6 2.4 %collective-permute-start.16 = (f32[32,8,512]{2,1,0:T(8,128)}, f32[32,8,512]{2,1,0:T(8,128)S(1)}, u32[]{:S(2)}, u32[]{:S(2)}) collective-permute-start(f32[32,8,512]{2,1,0:T(8,128)} %get-tuple-element.46), channel_id=1, source_target_pairs={{0,16},{16,32},{32,48},{48,64},{64,80},{80,96},{96,112},{112,128},... | collective-permute-start | bytes 1572872 | tf_op jit(solution)/shard_map/ppermute | solution.py:616
  81.0 0.0 collective-permute-start.17
  81.0 1.2 collective-permute-done.12.refs_1_
  82.2 3.2 %merge_shares.3 = (f32[32,9,1,128]{3,2,1,0:T(1,128)}, f32[12,8,512]{2,1,0:T(8,128)}, f32[12,8,512]{2,1,0:T(8,128)}) custom-call(f32[9,128]{1,0:T(8,128)} %get-tuple-element.43.own_ref, f32[9,128]{1,0:T(8,128)} %collective-permute-done.14.refs_0_.low_ref, f32[9,128]{1,0:T(8,128)} %collective-permute-done.15.refs_1_.high_ref, f32[32,8,512]{2,1,0:T(8,128)} %bitcast.3.y_even, ...), custom_call_target="tpu_custom_call" | custom-call | tf_op jit(solution)/shard_map/merge_shares/pallas_call | solution.py:662
  85.5 0.6 collective-permute-start.18
  86.1 1.0 collective-permute-start.19
  87.1 10.2 %all-to-all-start.1 = ((f32[32,9,1,128]{3,2,1,0:T(1,128)}), f32[32,9,1,128]{3,2,1,0:T(1,128)S(1)}, u32[]{:S(2)}, u32[]{:S(2)}) async-start(f32[32,9,1,128]{3,2,1,0:T(1,128)} %get-tuple-element.50), calls=%async_computation.1 | async-start | bytes 294912 | tf_op jit(solution)/shard_map/all_to_all | solution.py:672
  97.3 0.0 collective-permute-done.16.refs_3_
  97.3 0.0 copy-start.3
  97.3 7.6 %all-to-all-done.1.refs_17_ = f32[32,9,1,128]{3,2,1,0:T(1,128)S(1)} async-done(((f32[32,9,1,128]{3,2,1,0:T(1,128)}), f32[32,9,1,128]{3,2,1,0:T(1,128)S(1)}, u32[]{:S(2)}, u32[]{:S(2)}) %all-to-all-start.1) | async-done | bytes 147488 | tf_op jit(solution)/shard_map/all_to_all | solution.py:672
  105.0 0.6 copy-done.2
  105.6 11.6 %second_cycle.1 = (f32[8,8,8,512]{3,2,1,0:T(8,128)}, f32[8,8,8,512]{3,2,1,0:T(8,128)}, f32[32,1,128]{2,1,0:T(1,128)}) custom-call(f32[8,8,8,512]{3,2,1,0:T(8,128)} %get-tuple-element.40.refs_0_.refs_2_, f32[8,4,8,512]{3,2,1,0:T(8,128)} %collective-permute-done.12.refs_1_, f32[8,4,8,512]{3,2,1,0:T(8,128)} %collective-permute-done.13.refs_2_, ...), custom_call_target="tpu_custom_call" | custom-call | tf_op jit(solution)/shard_map/second_cycle/pallas_call | solution.py:726
  117.2 10.9 %all_to_all.20 = f32[32,1,128]{2,1,0:T(1,128)S(1)} all-to-all(f32[32,1,128]{2,1,0:T(1,128)} %get-tuple-element.52), channel_id=1, replica_groups=mesh['z'=8,'core'=2,'gy'=16] {'core','gy'}, dimensions={0} | all-to-all | bytes 32768 | tf_op jit(solution)/shard_map/all_to_all | solution.py:759
  128.1 0.1 reduce_sum.9
  128.2 9.9 %all_to_all.21.sums_ref = f32[8,1,128]{2,1,0:T(1,128)} all-to-all(f32[8,1,128]{2,1,0:T(1,128)S(1)} %broadcast_in_dim.3), channel_id=1, replica_groups=mesh['z'=8,'core'=2,'gy'=16] {'z'}, dimensions={0} | all-to-all | bytes 8192 | tf_op jit(solution)/shard_map/all_to_all | solution.py:760
  138.1 4.5 %combine.1 = (f32[8,8,8,512]{3,2,1,0:T(8,128)}, f32[8,8,8,512]{3,2,1,0:T(8,128)}) custom-call(f32[8,1,128]{2,1,0:T(1,128)} %all_to_all.21.sums_ref, f32[8,8,8,512]{3,2,1,0:T(8,128)} %refs_0_.3, f32[8,8,8,512]{3,2,1,0:T(8,128)} %get-tuple-element.53.refs_1_, f32[8,8,8,512]{3,2,1,0:T(8,128)} %get-tuple-element.40.refs_0_.refs_2_, ...), custom_call_target="tpu_custom_call" | custom-call | tf_op jit(solution)/shard_map/combine/pallas_call | solution.py:761
  (18 shorter events, 0.0 us)
Async XLA Ops:
  0.6 10.8 %collective-permute-start.3 = (f32[8,8,512]{2,1,0:T(8,128)}, f32[8,8,512]{2,1,0:T(8,128)}, u32[]{:S(2)}, u32[]{:S(2)}) collective-permute-start(f32[8,8,512]{2,1,0:T(8,128)} %refs_11_.3), channel_id=1, source_target_pairs={{0,0},{1,2},{2,1},{3,4},{4,3},{5,6},{6,5},{7,8},{8,7},{9,10},{10,9... | collective-permute-start | bytes 393224 | tf_op jit(solution)/shard_map/ppermute | solution.py:640
  2.8 8.7 %collective-permute-start.2 = (f32[8,8,512]{2,1,0:T(8,128)}, f32[8,8,512]{2,1,0:T(8,128)}, u32[]{:S(2)}, u32[]{:S(2)}) collective-permute-start(f32[8,8,512]{2,1,0:T(8,128)} %refs_11_.3), channel_id=1, source_target_pairs={{0,1},{1,0},{2,3},{3,2},{4,5},{5,4},{6,7},{7,6},{8,9},{9,8},{10,11... | collective-permute-start | bytes 393224 | tf_op jit(solution)/shard_map/ppermute | solution.py:640
  5.9 5.8 %collective-permute-start.1 = (f32[8,8,512]{2,1,0:T(8,128)}, f32[8,8,512]{2,1,0:T(8,128)}, u32[]{:S(2)}, u32[]{:S(2)}) collective-permute-start(f32[8,8,512]{2,1,0:T(8,128)} %refs_11_.3), channel_id=1, source_target_pairs={{0,240},{16,0},{32,16},{48,32},{64,48},{80,64},{96,80},{112,96},{1... | collective-permute-start | bytes 393224 | tf_op jit(solution)/shard_map/ppermute | solution.py:616
  7.1 5.9 %collective-permute-start = (f32[8,8,512]{2,1,0:T(8,128)}, f32[8,8,512]{2,1,0:T(8,128)}, u32[]{:S(2)}, u32[]{:S(2)}) collective-permute-start(f32[8,8,512]{2,1,0:T(8,128)} %refs_11_.3), channel_id=1, source_target_pairs={{0,16},{16,32},{32,48},{48,64},{64,80},{80,96},{96,112},{112,128},... | collective-permute-start | bytes 393224 | tf_op jit(solution)/shard_map/ppermute | solution.py:616
  13.0 19.8 %collective-permute-start.4 = (f32[8,4,8,512]{3,2,1,0:T(8,128)}, f32[8,4,8,512]{3,2,1,0:T(8,128)}, u32[]{:S(2)}, u32[]{:S(2)}) collective-permute-start(f32[8,4,8,512]{3,2,1,0:T(8,128)} %get-tuple-element.31), channel_id=1, source_target_pairs={{0,1},{1,0},{2,3},{3,2},{4,5},{5,4},{6,7},{7,6},{8,9},{9,8},{10,11... | collective-permute-start | bytes 1572872 | tf_op jit(solution)/shard_map/ppermute | solution.py:640
  13.1 19.7 %collective-permute-start.5 = (f32[8,4,8,512]{3,2,1,0:T(8,128)}, f32[8,4,8,512]{3,2,1,0:T(8,128)}, u32[]{:S(2)}, u32[]{:S(2)}) collective-permute-start(f32[8,4,8,512]{3,2,1,0:T(8,128)} %get-tuple-element.32), channel_id=1, source_target_pairs={{0,0},{1,2},{2,1},{3,4},{4,3},{5,6},{6,5},{7,8},{8,7},{9,10},{10,9... | collective-permute-start | bytes 1572872 | tf_op jit(solution)/shard_map/ppermute | solution.py:640
  22.1 5.4 %collective-permute-start.7 = (f32[9,128]{1,0:T(8,128)}, f32[9,128]{1,0:T(8,128)}, u32[]{:S(2)}, u32[]{:S(2)}) collective-permute-start(f32[9,128]{1,0:T(8,128)} %first_shares.1.own_ref), channel_id=1, source_target_pairs={{0,224},{32,0},{64,32},{96,64},{128,96},{160,128},{192,160},{224,1... | collective-permute-start | bytes 13832 | tf_op jit(solution)/shard_map/ppermute | solution.py:616
  26.5 4.0 %collective-permute-start.6 = (f32[9,128]{1,0:T(8,128)}, f32[9,128]{1,0:T(8,128)}, u32[]{:S(2)}, u32[]{:S(2)}) collective-permute-start(f32[9,128]{1,0:T(8,128)} %first_shares.1.own_ref), channel_id=1, source_target_pairs={{0,32},{32,64},{64,96},{96,128},{128,160},{160,192},{192,224},{224... | collective-permute-start | bytes 13832 | tf_op jit(solution)/shard_map/ppermute | solution.py:616
  30.6 17.6 %collective-permute-start.8 = (f32[35,8,512]{2,1,0:T(8,128)}, f32[35,8,512]{2,1,0:T(8,128)S(1)}, u32[]{:S(2)}, u32[]{:S(2)}) collective-permute-start(f32[35,8,512]{2,1,0:T(8,128)} %get-tuple-element.35), channel_id=1, source_target_pairs={{0,16},{16,32},{32,48},{48,64},{64,80},{80,96},{96,112},{112,128},... | collective-permute-start | bytes 1720328 | tf_op jit(solution)/shard_map/ppermute | solution.py:616
  32.8 15.4 %collective-permute-start.9 = (f32[35,8,512]{2,1,0:T(8,128)}, f32[35,8,512]{2,1,0:T(8,128)}, u32[]{:S(2)}, u32[]{:S(2)}) collective-permute-start(f32[35,8,512]{2,1,0:T(8,128)} %get-tuple-element.36), channel_id=1, source_target_pairs={{0,240},{16,0},{32,16},{48,32},{64,48},{80,64},{96,80},{112,96},{1... | collective-permute-start | bytes 1720328 | tf_op jit(solution)/shard_map/ppermute | solution.py:616
  36.3 19.5 %collective-permute-start.10 = (f32[18,8,512]{2,1,0:T(8,128)}, f32[18,8,512]{2,1,0:T(8,128)}, u32[]{:S(2)}, u32[]{:S(2)}) collective-permute-start(f32[18,8,512]{2,1,0:T(8,128)} %get-tuple-element.37), channel_id=1, source_target_pairs={{0,16},{16,32},{32,48},{48,64},{64,80},{80,96},{96,112},{112,128},... | collective-permute-start | bytes 884744 | tf_op jit(solution)/shard_map/ppermute | solution.py:616
  38.0 17.8 %collective-permute-start.11 = (f32[18,8,512]{2,1,0:T(8,128)}, f32[18,8,512]{2,1,0:T(8,128)}, u32[]{:S(2)}, u32[]{:S(2)}) collective-permute-start(f32[18,8,512]{2,1,0:T(8,128)} %get-tuple-element.38), channel_id=1, source_target_pairs={{0,240},{16,0},{32,16},{48,32},{64,48},{80,64},{96,80},{112,96},{1... | collective-permute-start | bytes 884744 | tf_op jit(solution)/shard_map/ppermute | solution.py:616
  39.1 16.7 %all-to-all-start = ((f32[32,9,1,128]{3,2,1,0:T(1,128)}), f32[32,9,1,128]{3,2,1,0:T(1,128)S(1)}, u32[]{:S(2)}, u32[]{:S(2)}) async-start(f32[32,9,1,128]{3,2,1,0:T(1,128)} %get-tuple-element.39), calls=%async_computation | async-start | bytes 294912 | tf_op jit(solution)/shard_map/all_to_all | solution.py:672
  48.2 7.7 %copy-start = (f32[35,8,512]{2,1,0:T(8,128)}, f32[35,8,512]{2,1,0:T(8,128)S(1)}, u32[]{:S(2)}) copy-start(f32[35,8,512]{2,1,0:T(8,128)S(1)} %collective-permute-done.8.refs_3_.refs_7_) | copy-start | bytes 1720324
  55.8 0.7 copy-start.1
  68.9 13.3 %collective-permute-start.12 = (f32[8,4,8,512]{3,2,1,0:T(8,128)}, f32[8,4,8,512]{3,2,1,0:T(8,128)}, u32[]{:S(2)}, u32[]{:S(2)}) collective-permute-start(f32[8,4,8,512]{3,2,1,0:T(8,128)} %get-tuple-element.41), channel_id=1, source_target_pairs={{0,1},{1,0},{2,3},{3,2},{4,5},{5,4},{6,7},{7,6},{8,9},{9,8},{10,11... | collective-permute-start | bytes 1572872 | tf_op jit(solution)/shard_map/ppermute | solution.py:640
  69.2 13.0 %collective-permute-start.13 = (f32[8,4,8,512]{3,2,1,0:T(8,128)}, f32[8,4,8,512]{3,2,1,0:T(8,128)}, u32[]{:S(2)}, u32[]{:S(2)}) collective-permute-start(f32[8,4,8,512]{3,2,1,0:T(8,128)} %get-tuple-element.42), channel_id=1, source_target_pairs={{0,0},{1,2},{2,1},{3,4},{4,3},{5,6},{6,5},{7,8},{8,7},{9,10},{10,9... | collective-permute-start | bytes 1572872 | tf_op jit(solution)/shard_map/ppermute | solution.py:640
  74.6 3.1 %collective-permute-start.15 = (f32[9,128]{1,0:T(8,128)}, f32[9,128]{1,0:T(8,128)}, u32[]{:S(2)}, u32[]{:S(2)}) collective-permute-start(f32[9,128]{1,0:T(8,128)} %get-tuple-element.43.own_ref), channel_id=1, source_target_pairs={{0,224},{32,0},{64,32},{96,64},{128,96},{160,128},{192,160},{224,1... | collective-permute-start | bytes 13832 | tf_op jit(solution)/shard_map/ppermute | solution.py:616
  74.6 4.0 %collective-permute-start.14 = (f32[9,128]{1,0:T(8,128)}, f32[9,128]{1,0:T(8,128)}, u32[]{:S(2)}, u32[]{:S(2)}) collective-permute-start(f32[9,128]{1,0:T(8,128)} %get-tuple-element.43.own_ref), channel_id=1, source_target_pairs={{0,32},{32,64},{64,96},{96,128},{128,160},{160,192},{192,224},{224... | collective-permute-start | bytes 13832 | tf_op jit(solution)/shard_map/ppermute | solution.py:616
  78.6 18.7 %collective-permute-start.16 = (f32[32,8,512]{2,1,0:T(8,128)}, f32[32,8,512]{2,1,0:T(8,128)S(1)}, u32[]{:S(2)}, u32[]{:S(2)}) collective-permute-start(f32[32,8,512]{2,1,0:T(8,128)} %get-tuple-element.46), channel_id=1, source_target_pairs={{0,16},{16,32},{32,48},{48,64},{64,80},{80,96},{96,112},{112,128},... | collective-permute-start | bytes 1572872 | tf_op jit(solution)/shard_map/ppermute | solution.py:616
  81.0 16.3 %collective-permute-start.17 = (f32[32,8,512]{2,1,0:T(8,128)}, f32[32,8,512]{2,1,0:T(8,128)}, u32[]{:S(2)}, u32[]{:S(2)}) collective-permute-start(f32[32,8,512]{2,1,0:T(8,128)} %get-tuple-element.47), channel_id=1, source_target_pairs={{0,240},{16,0},{32,16},{48,32},{64,48},{80,64},{96,80},{112,96},{1... | collective-permute-start | bytes 1572872 | tf_op jit(solution)/shard_map/ppermute | solution.py:616
  85.5 19.5 %collective-permute-start.18 = (f32[12,8,512]{2,1,0:T(8,128)}, f32[12,8,512]{2,1,0:T(8,128)}, u32[]{:S(2)}, u32[]{:S(2)}) collective-permute-start(f32[12,8,512]{2,1,0:T(8,128)} %get-tuple-element.48), channel_id=1, source_target_pairs={{0,16},{16,32},{32,48},{48,64},{64,80},{80,96},{96,112},{112,128},... | collective-permute-start | bytes 589832 | tf_op jit(solution)/shard_map/ppermute | solution.py:616
  86.1 18.9 %collective-permute-start.19 = (f32[12,8,512]{2,1,0:T(8,128)}, f32[12,8,512]{2,1,0:T(8,128)}, u32[]{:S(2)}, u32[]{:S(2)}) collective-permute-start(f32[12,8,512]{2,1,0:T(8,128)} %get-tuple-element.49), channel_id=1, source_target_pairs={{0,240},{16,0},{32,16},{48,32},{64,48},{80,64},{96,80},{112,96},{1... | collective-permute-start | bytes 589832 | tf_op jit(solution)/shard_map/ppermute | solution.py:616
  87.1 17.9 %all-to-all-start.1 = ((f32[32,9,1,128]{3,2,1,0:T(1,128)}), f32[32,9,1,128]{3,2,1,0:T(1,128)S(1)}, u32[]{:S(2)}, u32[]{:S(2)}) async-start(f32[32,9,1,128]{3,2,1,0:T(1,128)} %get-tuple-element.50), calls=%async_computation.1 | async-start | bytes 294912 | tf_op jit(solution)/shard_map/all_to_all | solution.py:672
  97.3 7.7 %copy-start.3 = (f32[32,8,512]{2,1,0:T(8,128)}, f32[32,8,512]{2,1,0:T(8,128)S(1)}, u32[]{:S(2)}) copy-start(f32[32,8,512]{2,1,0:T(8,128)S(1)} %collective-permute-done.16.refs_3_) | copy-start | bytes 1572868
  104.9 0.7 copy-start.2

commit v5 on v4

--- a/solution.py
+++ b/solution.py
@@ -95,7 +95,7 @@
             rows_ref[i, :, k * L : (k + 1) * L] = total[k]
         return a1, ylo, yhi
 
-    a1, ylo, yhi = lax.fori_loop(0, 8, one_row, (zero, zero, zero))
+    a1, ylo, yhi = lax.fori_loop(0, 8, one_row, (zero, zero, zero), unroll=2)
     rows = [[rows_ref[i, :, k * L : (k + 1) * L] for k in range(CH)] for i in range(8)]
     s_all = add(*rows)
     edges = (rows[0], rows[7], ylo, yhi)
@@ -374,7 +374,7 @@
 
 def cycle_kernel(first, n_gx, n_gy, *refs):
     f_own, f_even, f_odd, f_xl, f_xh, f_cl, f_ch, b_xl, b_xh, b_cl, b_ch = refs[:11]
-    kap_ref, kxl, kxh, k_even, k_odd, c_own, recv_ref = refs[11:18]
+    kap_ref, kxl, kxh, k_even, k_odd, c_own, recv_hbm = refs[11:18]
     refs = refs[18:]
     if first:
         z_out, q_out, dots_ref, out_ref = refs[:4]
@@ -383,12 +383,12 @@
     else:
         extra_hbm, earlier_ref, z_out, q_out, dots_ref = refs[:5]
         refs = refs[5:]
-    F, A, B, G, KC, KX, KY, inv_ref, c_ref, h_ref, gf_ref, rows_ref, z_ref, q_ref, extra_ref, sems = refs
+    F, A, B, G, KC, KX, KY, inv_ref, c_ref, h_ref, gf_ref, rows_ref, z_ref, q_ref, extra_ref, recv_ref, sems = refs
     has_x, has_y = place(n_gx, n_gy)
     gy = lax.axis_index("gy")
 
     even, odd = parity()
-    pairs = []
+    pairs = [(recv_hbm, recv_ref)]
     for jj in range(3):
         block = jnp.clip(gy - 1 + jj, 0, n_gy - 1)
         pairs.append(
@@ -464,7 +464,7 @@
             put(A, x, y, mul(row(G, x, y + 4), ld(F, x, y)))
         return carry
 
-    lax.fori_loop(0, 16, start_row, 0)
+    lax.fori_loop(0, 16, start_row, 0, unroll=2)
 
     def sweep(src, dst, width, coarse):
         def one_row(x, reach):
@@ -512,7 +512,7 @@
                 ez = functools.reduce(lambda a, b: a + b, mul(ld(extra_ref, i, j), here), ez)
         return fz, zq, ez
 
-    fz, zq, ez = lax.fori_loop(0, 8, image_row, (nil, nil, nil))
+    fz, zq, ez = lax.fori_loop(0, 8, image_row, (nil, nil, nil), unroll=2)
     if first:
         dots_ref[0] = fz
         dots_ref[1] = zq
@@ -726,7 +726,7 @@
             return pl.pallas_call(
                 functools.partial(cycle_kernel, first, n_gx, n_gy),
                 out_shape=outs,
-                in_specs=[HB] * 17 + [VM] + ([HB, VM] if more else []),
+                in_specs=[HB] * 18 + ([HB, VM] if more else []),
                 out_specs=out_specs,
                 scratch_shapes=[
                     big,
@@ -744,6 +744,7 @@
                     own_tile,
                     own_tile,
                     own_tile,
+                    pltpu.VMEM((2 * n_gy, 9, 1, L), f32),
                     pltpu.SemaphoreType.DMA((52,)),
                 ],
                 compiler_params=GRANT,

time: 144 us -> 142 us (0.986)
  Pallas kernels: 41.7 us -> 39.7 us
    pallas_call x2, Pallas kernels: 24 us -> 22.3 us  [cycle(): pl.pallas_call(functools.partial(cycle_kernel, first, n_gx, n_gy), out_sh...]
where the time goes in v5:
time: 142 us; the launch traced here: 141 us
  starting transfers between devices  53.2 us (37%)
  Pallas kernels  39.7 us (28%)
  waiting for transfers between devices  24.8 us (17%)
  blocking collectives  20.8 us (15%)
    pallas_call x2, Pallas kernels, cycle(): pl.pallas_call(functools.partial(cycle_kernel, first, n_gx, n_gy), out_sh...  22.3 us
    all_to_all x2, starting transfers between devices, exchange(): return (lax.all_to_all(out, SLAB2, 0, 0), cells + corners)  19 us
    ppermute x14, starting transfers between devices, shift(): return lax.ppermute(value, axes, pairs)  17.9 us
    all_to_all x2, waiting for transfers between devices, exchange(): return (lax.all_to_all(out, SLAB2, 0, 0), cells + corners)  15.3 us
    ppermute x3, starting transfers between devices, along_gy(): lax.ppermute(to_odd, 'gy', odd_pairs)  12.9 us
    all_to_all x1, blocking collectives, body(): near_sum = jnp.sum(lax.all_to_all(packed, SLAB2, 0, 0), axis=0)  10.9 us
    all_to_all x1, blocking collectives, body(): sums = lax.all_to_all(jnp.broadcast_to(near_sum, (n_z, 1, L)), 'z', 0, 0)  9.88 us
    ppermute x14, waiting for transfers between devices, shift(): return lax.ppermute(value, axes, pairs)  8.37 us
  transfers between devices with their start and end apart: 22, of which 9 were waited for; matrix products, arithmetic and copies ran while one was open for 0% of the time, Pallas kernels for 9%

profile of v5, /device:TPU:1, one launch (start us, length us, event | category | flops | bytes accessed | tf_op | source)
XLA Modules:
  0.0 140.8 jit_solution(9830013553147638239)
XLA Ops:
  0.6 2.2 %collective-permute-start.3 = (f32[8,8,512]{2,1,0:T(8,128)}, f32[8,8,512]{2,1,0:T(8,128)}, u32[]{:S(2)}, u32[]{:S(2)}) collective-permute-start(f32[8,8,512]{2,1,0:T(8,128)} %refs_11_.3), channel_id=1, source_target_pairs={{0,0},{1,2},{2,1},{3,4},{4,3},{5,6},{6,5},{7,8},{8,7},{9,10},{10,9... | collective-permute-start | bytes 393224 | tf_op jit(solution)/shard_map/ppermute | solution.py:640
  2.8 3.1 %collective-permute-start.2 = (f32[8,8,512]{2,1,0:T(8,128)}, f32[8,8,512]{2,1,0:T(8,128)}, u32[]{:S(2)}, u32[]{:S(2)}) collective-permute-start(f32[8,8,512]{2,1,0:T(8,128)} %refs_11_.3), channel_id=1, source_target_pairs={{0,1},{1,0},{2,3},{3,2},{4,5},{5,4},{6,7},{7,6},{8,9},{9,8},{10,11... | collective-permute-start | bytes 393224 | tf_op jit(solution)/shard_map/ppermute | solution.py:640
  5.9 1.2 collective-permute-start.1
  7.1 1.5 %collective-permute-start = (f32[8,8,512]{2,1,0:T(8,128)}, f32[8,8,512]{2,1,0:T(8,128)}, u32[]{:S(2)}, u32[]{:S(2)}) collective-permute-start(f32[8,8,512]{2,1,0:T(8,128)} %refs_11_.3), channel_id=1, source_target_pairs={{0,16},{16,32},{32,48},{48,64},{64,80},{80,96},{96,112},{112,128},... | collective-permute-start | bytes 393224 | tf_op jit(solution)/shard_map/ppermute | solution.py:616
  8.6 2.8 %pack_faces.1 = (f32[8,4,8,512]{3,2,1,0:T(8,128)}, f32[8,4,8,512]{3,2,1,0:T(8,128)}, f32[35,8,512]{2,1,0:T(8,128)}, f32[35,8,512]{2,1,0:T(8,128)}) custom-call(f32[64,8,512]{2,1,0:T(8,128)} %bitcast.5, f32[256,256]{1,0:T(8,128)} %refs_16_.3), custom_call_target="tpu_custom_call" | custom-call | tf_op jit(solution)/shard_map/pack_faces/pallas_call | solution.py:680
  11.4 0.0 collective-permute-done.3.refs_3_.ko_hbm.refs_1_.refs_15_
  11.5 0.0 collective-permute-done.2.refs_2_.ke_hbm.refs_0_.refs_14_
  11.5 0.2 collective-permute-done.1.refs_1_.kxh_hbm.refs_13_
  11.6 1.4 collective-permute-done.refs_0_.kxl_hbm.refs_12_
  13.0 0.0 collective-permute-start.4
  13.1 5.3 %collective-permute-start.5 = (f32[8,4,8,512]{3,2,1,0:T(8,128)}, f32[8,4,8,512]{3,2,1,0:T(8,128)}, u32[]{:S(2)}, u32[]{:S(2)}) collective-permute-start(f32[8,4,8,512]{3,2,1,0:T(8,128)} %get-tuple-element.32), channel_id=1, source_target_pairs={{0,0},{1,2},{2,1},{3,4},{4,3},{5,6},{6,5},{7,8},{8,7},{9,10},{10,9... | collective-permute-start | bytes 1572872 | tf_op jit(solution)/shard_map/ppermute | solution.py:640
  18.4 3.4 %first_shares.1.own_ref = f32[9,128]{1,0:T(8,128)} custom-call(f32[8,8,8,512]{3,2,1,0:T(8,128)} %refs_0_.3, f32[8,8,512]{2,1,0:T(8,128)} %refs_11_.3, f32[8,8,512]{2,1,0:T(8,128)} %collective-permute-done.refs_0_.kxl_hbm.refs_12_, f32[8,8,512]{2,1,0:T(8,128)} %collective-permute-done.1.refs_1_.kxh_hbm.refs_13_, ...), custom_call_target="tpu_custom_call" | custom-call | tf_op jit(solution)/shard_map/first_shares/pallas_call | solution.py:696
  21.8 4.4 %collective-permute-start.7 = (f32[9,128]{1,0:T(8,128)}, f32[9,128]{1,0:T(8,128)}, u32[]{:S(2)}, u32[]{:S(2)}) collective-permute-start(f32[9,128]{1,0:T(8,128)} %first_shares.1.own_ref), channel_id=1, source_target_pairs={{0,224},{32,0},{64,32},{96,64},{128,96},{160,128},{192,160},{224,1... | collective-permute-start | bytes 13832 | tf_op jit(solution)/shard_map/ppermute | solution.py:616
  26.2 1.0 collective-permute-done.7.refs_1_.high_ref
  27.2 3.0 %collective-permute-done.6.refs_0_.low_ref = f32[9,128]{1,0:T(8,128)} collective-permute-done((f32[9,128]{1,0:T(8,128)}, f32[9,128]{1,0:T(8,128)}, u32[]{:S(2)}, u32[]{:S(2)}) %collective-permute-start.6) | collective-permute-done | bytes 4640 | tf_op jit(solution)/shard_map/ppermute | solution.py:616
  30.3 2.2 %collective-permute-start.8 = (f32[35,8,512]{2,1,0:T(8,128)}, f32[35,8,512]{2,1,0:T(8,128)S(1)}, u32[]{:S(2)}, u32[]{:S(2)}) collective-permute-start(f32[35,8,512]{2,1,0:T(8,128)} %get-tuple-element.35), channel_id=1, source_target_pairs={{0,16},{16,32},{32,48},{48,64},{64,80},{80,96},{96,112},{112,128},... | collective-permute-start | bytes 1720328 | tf_op jit(solution)/shard_map/ppermute | solution.py:616
  32.5 0.0 collective-permute-start.9
  32.5 0.0 collective-permute-done.4.refs_1_
  32.5 3.5 %merge_shares.2 = (f32[32,9,1,128]{3,2,1,0:T(1,128)}, f32[18,8,512]{2,1,0:T(8,128)}, f32[18,8,512]{2,1,0:T(8,128)}) custom-call(f32[9,128]{1,0:T(8,128)} %first_shares.1.own_ref, f32[9,128]{1,0:T(8,128)} %collective-permute-done.6.refs_0_.low_ref, f32[9,128]{1,0:T(8,128)} %collective-permute-done.7.refs_1_.high_ref, f32[32,8,512]{2,1,0:T(8,128)} %bitcast.1.y_even, ...), custom_call_target="tpu_custom_call" | custom-call | tf_op jit(solution)/shard_map/merge_shares/pallas_call | solution.py:662
  36.0 1.8 %collective-permute-start.10 = (f32[18,8,512]{2,1,0:T(8,128)}, f32[18,8,512]{2,1,0:T(8,128)}, u32[]{:S(2)}, u32[]{:S(2)}) collective-permute-start(f32[18,8,512]{2,1,0:T(8,128)} %get-tuple-element.37), channel_id=1, source_target_pairs={{0,16},{16,32},{32,48},{48,64},{64,80},{80,96},{96,112},{112,128},... | collective-permute-start | bytes 884744 | tf_op jit(solution)/shard_map/ppermute | solution.py:616
  37.7 1.1 collective-permute-start.11
  38.8 9.0 %all-to-all-start = ((f32[32,9,1,128]{3,2,1,0:T(1,128)}), f32[32,9,1,128]{3,2,1,0:T(1,128)S(1)}, u32[]{:S(2)}, u32[]{:S(2)}) async-start(f32[32,9,1,128]{3,2,1,0:T(1,128)} %get-tuple-element.39), calls=%async_computation | async-start | bytes 294912 | tf_op jit(solution)/shard_map/all_to_all | solution.py:672
  47.9 0.0 collective-permute-done.8.refs_3_.refs_7_
  47.9 0.0 copy-start
  47.9 7.6 %all-to-all-done.refs_17_ = f32[32,9,1,128]{3,2,1,0:T(1,128)S(1)} async-done(((f32[32,9,1,128]{3,2,1,0:T(1,128)}), f32[32,9,1,128]{3,2,1,0:T(1,128)S(1)}, u32[]{:S(2)}, u32[]{:S(2)}) %all-to-all-start) | async-done | bytes 147488 | tf_op jit(solution)/shard_map/all_to_all | solution.py:672
  55.6 0.6 copy-done.1
  56.2 11.2 %first_cycle.1 = (f32[8,8,8,512]{3,2,1,0:T(8,128)}, f32[8,8,8,512]{3,2,1,0:T(8,128)}, f32[2,8,128]{2,1,0:T(8,128)}, f32[9,128]{1,0:T(8,128)}, f32[8,4,8,512]{3,2...) custom-call(f32[8,8,8,512]{3,2,1,0:T(8,128)} %refs_0_.3, ...), custom_call_target="tpu_custom_call" | custom-call | tf_op jit(solution)/shard_map/first_cycle/pallas_call | solution.py:726
  67.4 0.3 collective-permute-start.12
  67.7 5.3 %collective-permute-start.13 = (f32[8,4,8,512]{3,2,1,0:T(8,128)}, f32[8,4,8,512]{3,2,1,0:T(8,128)}, u32[]{:S(2)}, u32[]{:S(2)}) collective-permute-start(f32[8,4,8,512]{3,2,1,0:T(8,128)} %get-tuple-element.42), channel_id=1, source_target_pairs={{0,0},{1,2},{2,1},{3,4},{4,3},{5,6},{6,5},{7,8},{8,7},{9,10},{10,9... | collective-permute-start | bytes 1572872 | tf_op jit(solution)/shard_map/ppermute | solution.py:640
  73.1 0.2 collective-permute-start.15
  73.3 1.3 collective-permute-start.14
  74.6 1.6 %collective-permute-done.15.refs_1_.high_ref = f32[9,128]{1,0:T(8,128)} collective-permute-done((f32[9,128]{1,0:T(8,128)}, f32[9,128]{1,0:T(8,128)}, u32[]{:S(2)}, u32[]{:S(2)}) %collective-permute-start.15) | collective-permute-done | bytes 4640 | tf_op jit(solution)/shard_map/ppermute | solution.py:616
  76.2 1.1 collective-permute-done.14.refs_0_.low_ref
  77.3 2.2 %collective-permute-start.16 = (f32[32,8,512]{2,1,0:T(8,128)}, f32[32,8,512]{2,1,0:T(8,128)S(1)}, u32[]{:S(2)}, u32[]{:S(2)}) collective-permute-start(f32[32,8,512]{2,1,0:T(8,128)} %get-tuple-element.46), channel_id=1, source_target_pairs={{0,16},{16,32},{32,48},{48,64},{64,80},{80,96},{96,112},{112,128},... | collective-permute-start | bytes 1572872 | tf_op jit(solution)/shard_map/ppermute | solution.py:616
  79.6 0.1 collective-permute-start.17
  79.6 1.1 collective-permute-done.12.refs_1_
  80.8 3.2 %merge_shares.3 = (f32[32,9,1,128]{3,2,1,0:T(1,128)}, f32[12,8,512]{2,1,0:T(8,128)}, f32[12,8,512]{2,1,0:T(8,128)}) custom-call(f32[9,128]{1,0:T(8,128)} %get-tuple-element.43.own_ref, f32[9,128]{1,0:T(8,128)} %collective-permute-done.14.refs_0_.low_ref, f32[9,128]{1,0:T(8,128)} %collective-permute-done.15.refs_1_.high_ref, f32[32,8,512]{2,1,0:T(8,128)} %bitcast.3.y_even, ...), custom_call_target="tpu_custom_call" | custom-call | tf_op jit(solution)/shard_map/merge_shares/pallas_call | solution.py:662
  84.0 0.6 collective-permute-start.18
  84.6 1.3 collective-permute-start.19
  85.9 9.9 %all-to-all-start.1 = ((f32[32,9,1,128]{3,2,1,0:T(1,128)}), f32[32,9,1,128]{3,2,1,0:T(1,128)S(1)}, u32[]{:S(2)}, u32[]{:S(2)}) async-start(f32[32,9,1,128]{3,2,1,0:T(1,128)} %get-tuple-element.50), calls=%async_computation.1 | async-start | bytes 294912 | tf_op jit(solution)/shard_map/all_to_all | solution.py:672
  95.8 0.0 copy-start.3
  95.8 7.6 %all-to-all-done.1.refs_17_ = f32[32,9,1,128]{3,2,1,0:T(1,128)S(1)} async-done(((f32[32,9,1,128]{3,2,1,0:T(1,128)}), f32[32,9,1,128]{3,2,1,0:T(1,128)S(1)}, u32[]{:S(2)}, u32[]{:S(2)}) %all-to-all-start.1) | async-done | bytes 147488 | tf_op jit(solution)/shard_map/all_to_all | solution.py:672
  103.5 0.6 copy-done.2
  104.1 11.1 %second_cycle.1 = (f32[8,8,8,512]{3,2,1,0:T(8,128)}, f32[8,8,8,512]{3,2,1,0:T(8,128)}, f32[32,1,128]{2,1,0:T(1,128)}) custom-call(f32[8,8,8,512]{3,2,1,0:T(8,128)} %get-tuple-element.40.refs_0_.refs_2_, f32[8,4,8,512]{3,2,1,0:T(8,128)} %collective-permute-done.12.refs_1_, f32[8,4,8,512]{3,2,1,0:T(8,128)} %collective-permute-done.13.refs_2_, ...), custom_call_target="tpu_custom_call" | custom-call | tf_op jit(solution)/shard_map/second_cycle/pallas_call | solution.py:726
  115.2 10.9 %all_to_all.20 = f32[32,1,128]{2,1,0:T(1,128)S(1)} all-to-all(f32[32,1,128]{2,1,0:T(1,128)} %get-tuple-element.52), channel_id=1, replica_groups=mesh['z'=8,'core'=2,'gy'=16] {'core','gy'}, dimensions={0} | all-to-all | bytes 32768 | tf_op jit(solution)/shard_map/all_to_all | solution.py:760
  126.1 0.1 reduce_sum.9
  126.2 9.9 %all_to_all.21.sums_ref = f32[8,1,128]{2,1,0:T(1,128)} all-to-all(f32[8,1,128]{2,1,0:T(1,128)S(1)} %broadcast_in_dim.3), channel_id=1, replica_groups=mesh['z'=8,'core'=2,'gy'=16] {'z'}, dimensions={0} | all-to-all | bytes 8192 | tf_op jit(solution)/shard_map/all_to_all | solution.py:761
  136.1 4.5 %combine.1 = (f32[8,8,8,512]{3,2,1,0:T(8,128)}, f32[8,8,8,512]{3,2,1,0:T(8,128)}) custom-call(f32[8,1,128]{2,1,0:T(1,128)} %all_to_all.21.sums_ref, f32[8,8,8,512]{3,2,1,0:T(8,128)} %refs_0_.3, f32[8,8,8,512]{3,2,1,0:T(8,128)} %get-tuple-element.53.refs_1_, f32[8,8,8,512]{3,2,1,0:T(8,128)} %get-tuple-element.40.refs_0_.refs_2_, ...), custom_call_target="tpu_custom_call" | custom-call | tf_op jit(solution)/shard_map/combine/pallas_call | solution.py:762
  (18 shorter events, 0.0 us)
Async XLA Ops:
  0.6 10.8 %collective-permute-start.3 = (f32[8,8,512]{2,1,0:T(8,128)}, f32[8,8,512]{2,1,0:T(8,128)}, u32[]{:S(2)}, u32[]{:S(2)}) collective-permute-start(f32[8,8,512]{2,1,0:T(8,128)} %refs_11_.3), channel_id=1, source_target_pairs={{0,0},{1,2},{2,1},{3,4},{4,3},{5,6},{6,5},{7,8},{8,7},{9,10},{10,9... | collective-permute-start | bytes 393224 | tf_op jit(solution)/shard_map/ppermute | solution.py:640
  2.8 8.7 %collective-permute-start.2 = (f32[8,8,512]{2,1,0:T(8,128)}, f32[8,8,512]{2,1,0:T(8,128)}, u32[]{:S(2)}, u32[]{:S(2)}) collective-permute-start(f32[8,8,512]{2,1,0:T(8,128)} %refs_11_.3), channel_id=1, source_target_pairs={{0,1},{1,0},{2,3},{3,2},{4,5},{5,4},{6,7},{7,6},{8,9},{9,8},{10,11... | collective-permute-start | bytes 393224 | tf_op jit(solution)/shard_map/ppermute | solution.py:640
  5.9 5.8 %collective-permute-start.1 = (f32[8,8,512]{2,1,0:T(8,128)}, f32[8,8,512]{2,1,0:T(8,128)}, u32[]{:S(2)}, u32[]{:S(2)}) collective-permute-start(f32[8,8,512]{2,1,0:T(8,128)} %refs_11_.3), channel_id=1, source_target_pairs={{0,240},{16,0},{32,16},{48,32},{64,48},{80,64},{96,80},{112,96},{1... | collective-permute-start | bytes 393224 | tf_op jit(solution)/shard_map/ppermute | solution.py:616
  7.1 5.9 %collective-permute-start = (f32[8,8,512]{2,1,0:T(8,128)}, f32[8,8,512]{2,1,0:T(8,128)}, u32[]{:S(2)}, u32[]{:S(2)}) collective-permute-start(f32[8,8,512]{2,1,0:T(8,128)} %refs_11_.3), channel_id=1, source_target_pairs={{0,16},{16,32},{32,48},{48,64},{64,80},{80,96},{96,112},{112,128},... | collective-permute-start | bytes 393224 | tf_op jit(solution)/shard_map/ppermute | solution.py:616
  13.0 19.5 %collective-permute-start.4 = (f32[8,4,8,512]{3,2,1,0:T(8,128)}, f32[8,4,8,512]{3,2,1,0:T(8,128)}, u32[]{:S(2)}, u32[]{:S(2)}) collective-permute-start(f32[8,4,8,512]{3,2,1,0:T(8,128)} %get-tuple-element.31), channel_id=1, source_target_pairs={{0,1},{1,0},{2,3},{3,2},{4,5},{5,4},{6,7},{7,6},{8,9},{9,8},{10,11... | collective-permute-start | bytes 1572872 | tf_op jit(solution)/shard_map/ppermute | solution.py:640
  13.1 19.5 %collective-permute-start.5 = (f32[8,4,8,512]{3,2,1,0:T(8,128)}, f32[8,4,8,512]{3,2,1,0:T(8,128)}, u32[]{:S(2)}, u32[]{:S(2)}) collective-permute-start(f32[8,4,8,512]{3,2,1,0:T(8,128)} %get-tuple-element.32), channel_id=1, source_target_pairs={{0,0},{1,2},{2,1},{3,4},{4,3},{5,6},{6,5},{7,8},{8,7},{9,10},{10,9... | collective-permute-start | bytes 1572872 | tf_op jit(solution)/shard_map/ppermute | solution.py:640
  21.8 5.4 %collective-permute-start.7 = (f32[9,128]{1,0:T(8,128)}, f32[9,128]{1,0:T(8,128)}, u32[]{:S(2)}, u32[]{:S(2)}) collective-permute-start(f32[9,128]{1,0:T(8,128)} %first_shares.1.own_ref), channel_id=1, source_target_pairs={{0,224},{32,0},{64,32},{96,64},{128,96},{160,128},{192,160},{224,1... | collective-permute-start | bytes 13832 | tf_op jit(solution)/shard_map/ppermute | solution.py:616
  26.2 4.0 %collective-permute-start.6 = (f32[9,128]{1,0:T(8,128)}, f32[9,128]{1,0:T(8,128)}, u32[]{:S(2)}, u32[]{:S(2)}) collective-permute-start(f32[9,128]{1,0:T(8,128)} %first_shares.1.own_ref), channel_id=1, source_target_pairs={{0,32},{32,64},{64,96},{96,128},{128,160},{160,192},{192,224},{224... | collective-permute-start | bytes 13832 | tf_op jit(solution)/shard_map/ppermute | solution.py:616
  30.3 17.6 %collective-permute-start.8 = (f32[35,8,512]{2,1,0:T(8,128)}, f32[35,8,512]{2,1,0:T(8,128)S(1)}, u32[]{:S(2)}, u32[]{:S(2)}) collective-permute-start(f32[35,8,512]{2,1,0:T(8,128)} %get-tuple-element.35), channel_id=1, source_target_pairs={{0,16},{16,32},{32,48},{48,64},{64,80},{80,96},{96,112},{112,128},... | collective-permute-start | bytes 1720328 | tf_op jit(solution)/shard_map/ppermute | solution.py:616
  32.5 15.4 %collective-permute-start.9 = (f32[35,8,512]{2,1,0:T(8,128)}, f32[35,8,512]{2,1,0:T(8,128)}, u32[]{:S(2)}, u32[]{:S(2)}) collective-permute-start(f32[35,8,512]{2,1,0:T(8,128)} %get-tuple-element.36), channel_id=1, source_target_pairs={{0,240},{16,0},{32,16},{48,32},{64,48},{80,64},{96,80},{112,96},{1... | collective-permute-start | bytes 1720328 | tf_op jit(solution)/shard_map/ppermute | solution.py:616
  36.0 19.5 %collective-permute-start.10 = (f32[18,8,512]{2,1,0:T(8,128)}, f32[18,8,512]{2,1,0:T(8,128)}, u32[]{:S(2)}, u32[]{:S(2)}) collective-permute-start(f32[18,8,512]{2,1,0:T(8,128)} %get-tuple-element.37), channel_id=1, source_target_pairs={{0,16},{16,32},{32,48},{48,64},{64,80},{80,96},{96,112},{112,128},... | collective-permute-start | bytes 884744 | tf_op jit(solution)/shard_map/ppermute | solution.py:616
  37.7 17.8 %collective-permute-start.11 = (f32[18,8,512]{2,1,0:T(8,128)}, f32[18,8,512]{2,1,0:T(8,128)}, u32[]{:S(2)}, u32[]{:S(2)}) collective-permute-start(f32[18,8,512]{2,1,0:T(8,128)} %get-tuple-element.38), channel_id=1, source_target_pairs={{0,240},{16,0},{32,16},{48,32},{64,48},{80,64},{96,80},{112,96},{1... | collective-permute-start | bytes 884744 | tf_op jit(solution)/shard_map/ppermute | solution.py:616
  38.8 16.7 %all-to-all-start = ((f32[32,9,1,128]{3,2,1,0:T(1,128)}), f32[32,9,1,128]{3,2,1,0:T(1,128)S(1)}, u32[]{:S(2)}, u32[]{:S(2)}) async-start(f32[32,9,1,128]{3,2,1,0:T(1,128)} %get-tuple-element.39), calls=%async_computation | async-start | bytes 294912 | tf_op jit(solution)/shard_map/all_to_all | solution.py:672
  47.9 7.7 %copy-start = (f32[35,8,512]{2,1,0:T(8,128)}, f32[35,8,512]{2,1,0:T(8,128)S(1)}, u32[]{:S(2)}) copy-start(f32[35,8,512]{2,1,0:T(8,128)S(1)} %collective-permute-done.8.refs_3_.refs_7_) | copy-start | bytes 1720324
  55.5 0.7 copy-start.1
  67.4 13.3 %collective-permute-start.12 = (f32[8,4,8,512]{3,2,1,0:T(8,128)}, f32[8,4,8,512]{3,2,1,0:T(8,128)}, u32[]{:S(2)}, u32[]{:S(2)}) collective-permute-start(f32[8,4,8,512]{3,2,1,0:T(8,128)} %get-tuple-element.41), channel_id=1, source_target_pairs={{0,1},{1,0},{2,3},{3,2},{4,5},{5,4},{6,7},{7,6},{8,9},{9,8},{10,11... | collective-permute-start | bytes 1572872 | tf_op jit(solution)/shard_map/ppermute | solution.py:640
  67.7 13.0 %collective-permute-start.13 = (f32[8,4,8,512]{3,2,1,0:T(8,128)}, f32[8,4,8,512]{3,2,1,0:T(8,128)}, u32[]{:S(2)}, u32[]{:S(2)}) collective-permute-start(f32[8,4,8,512]{3,2,1,0:T(8,128)} %get-tuple-element.42), channel_id=1, source_target_pairs={{0,0},{1,2},{2,1},{3,4},{4,3},{5,6},{6,5},{7,8},{8,7},{9,10},{10,9... | collective-permute-start | bytes 1572872 | tf_op jit(solution)/shard_map/ppermute | solution.py:640
  73.1 3.1 %collective-permute-start.15 = (f32[9,128]{1,0:T(8,128)}, f32[9,128]{1,0:T(8,128)}, u32[]{:S(2)}, u32[]{:S(2)}) collective-permute-start(f32[9,128]{1,0:T(8,128)} %get-tuple-element.43.own_ref), channel_id=1, source_target_pairs={{0,224},{32,0},{64,32},{96,64},{128,96},{160,128},{192,160},{224,1... | collective-permute-start | bytes 13832 | tf_op jit(solution)/shard_map/ppermute | solution.py:616
  73.3 4.0 %collective-permute-start.14 = (f32[9,128]{1,0:T(8,128)}, f32[9,128]{1,0:T(8,128)}, u32[]{:S(2)}, u32[]{:S(2)}) collective-permute-start(f32[9,128]{1,0:T(8,128)} %get-tuple-element.43.own_ref), channel_id=1, source_target_pairs={{0,32},{32,64},{64,96},{96,128},{128,160},{160,192},{192,224},{224... | collective-permute-start | bytes 13832 | tf_op jit(solution)/shard_map/ppermute | solution.py:616
  77.3 18.5 %collective-permute-start.16 = (f32[32,8,512]{2,1,0:T(8,128)}, f32[32,8,512]{2,1,0:T(8,128)S(1)}, u32[]{:S(2)}, u32[]{:S(2)}) collective-permute-start(f32[32,8,512]{2,1,0:T(8,128)} %get-tuple-element.46), channel_id=1, source_target_pairs={{0,16},{16,32},{32,48},{48,64},{64,80},{80,96},{96,112},{112,128},... | collective-permute-start | bytes 1572872 | tf_op jit(solution)/shard_map/ppermute | solution.py:616
  79.6 16.3 %collective-permute-start.17 = (f32[32,8,512]{2,1,0:T(8,128)}, f32[32,8,512]{2,1,0:T(8,128)}, u32[]{:S(2)}, u32[]{:S(2)}) collective-permute-start(f32[32,8,512]{2,1,0:T(8,128)} %get-tuple-element.47), channel_id=1, source_target_pairs={{0,240},{16,0},{32,16},{48,32},{64,48},{80,64},{96,80},{112,96},{1... | collective-permute-start | bytes 1572872 | tf_op jit(solution)/shard_map/ppermute | solution.py:616
  84.0 19.5 %collective-permute-start.18 = (f32[12,8,512]{2,1,0:T(8,128)}, f32[12,8,512]{2,1,0:T(8,128)}, u32[]{:S(2)}, u32[]{:S(2)}) collective-permute-start(f32[12,8,512]{2,1,0:T(8,128)} %get-tuple-element.48), channel_id=1, source_target_pairs={{0,16},{16,32},{32,48},{48,64},{64,80},{80,96},{96,112},{112,128},... | collective-permute-start | bytes 589832 | tf_op jit(solution)/shard_map/ppermute | solution.py:616
  84.6 18.9 %collective-permute-start.19 = (f32[12,8,512]{2,1,0:T(8,128)}, f32[12,8,512]{2,1,0:T(8,128)}, u32[]{:S(2)}, u32[]{:S(2)}) collective-permute-start(f32[12,8,512]{2,1,0:T(8,128)} %get-tuple-element.49), channel_id=1, source_target_pairs={{0,240},{16,0},{32,16},{48,32},{64,48},{80,64},{96,80},{112,96},{1... | collective-permute-start | bytes 589832 | tf_op jit(solution)/shard_map/ppermute | solution.py:616
  85.9 17.6 %all-to-all-start.1 = ((f32[32,9,1,128]{3,2,1,0:T(1,128)}), f32[32,9,1,128]{3,2,1,0:T(1,128)S(1)}, u32[]{:S(2)}, u32[]{:S(2)}) async-start(f32[32,9,1,128]{3,2,1,0:T(1,128)} %get-tuple-element.50), calls=%async_computation.1 | async-start | bytes 294912 | tf_op jit(solution)/shard_map/all_to_all | solution.py:672
  95.8 7.7 %copy-start.3 = (f32[32,8,512]{2,1,0:T(8,128)}, f32[32,8,512]{2,1,0:T(8,128)S(1)}, u32[]{:S(2)}) copy-start(f32[32,8,512]{2,1,0:T(8,128)S(1)} %collective-permute-done.16.refs_3_) | copy-start | bytes 1572868
  103.5 0.7 copy-start.2
